TPU v7x, 128 devices: a whole 4x4x4 slice. The times are simulated.
128 devices in a mesh: visit: 8 (over x, core), tile: 16 (over y, z).
Axes of the slice: x: 4, y: 4, z: 4, core: 2. Of those that a mesh axis runs over, the one named last changes fastest.
Arguments:
- image: bfloat16 [1536, 512, 512], P(('visit', 'tile')), may hold values from -6 to 6
- inv_var: bfloat16 [1536, 512], P(('visit', 'tile')), may hold values from 0.099609375 to 3
- kernel_index: int32 [1536], P(('visit', 'tile')), may hold values from 0 to 7
- dest: int32 [1536, 1], P(('visit', 'tile')), may hold values from 0 to 15; in each aligned block of 12 rows (0 to 11, 12 to 23, ...) at most 2 rows name the same one
- position: int32 [1536], P(('visit', 'tile')), may hold values from 0 to 3
- row_taps: float32 [8, 41], replicated, may hold values from 0.005 to 0.06
- col_taps: float32 [8, 41], replicated, may hold values from 0.005 to 0.06
Outputs:
- coadd: float32 [16, 4, 512, 512], P('tile', None, 'visit')
Inputs may be any that keep to these rules, and one draw needn't show every extreme that they name: `dest`: among the rows of one device no sky tile is named more than 2 times.
All inputs are finite; a program needn't handle non-finite values.
Results may differ from a plain program's by a relative error of at most 0.0055.
Values may be sent and summed in bfloat16 or wider, within the bound.
No kernel may reach another device: no remote copies, remote signals or barrier semaphores. Data moves between devices by JAX's collectives and lax.ppermute only.
A program may use at most 192 MiB of HBM per device.

v0:
```python
import jax
import jax.numpy as jnp
from jax import lax
from jax.sharding import PartitionSpec as P

NB = 8
POS = 4
CAP = 2


def band_tables(tap_table, side_len):
    kernel_count, tap_count = tap_table.shape
    half_taps = (tap_count - 1) // 2
    margin = side_len - 1 - half_taps
    padded = jnp.pad(tap_table.astype(jnp.bfloat16), ((0, 0), (margin, margin)))
    flipped = jnp.flip(padded, axis=1)
    span = 2 * side_len - 1
    repeated = jnp.tile(flipped, (1, side_len))
    window = repeated[:, side_len - 1 : side_len - 1 + side_len * (span - 1)]
    return window.reshape(kernel_count, side_len, span - 1)[:, :, :side_len]


def match_blocks(pixels, kernel_table, row_bands, col_bands):
    row_pick = jnp.einsum(
        "sk,kij->sij", kernel_table, row_bands, preferred_element_type=jnp.float32
    ).astype(jnp.bfloat16)
    col_pick = jnp.einsum(
        "sk,kij->sij", kernel_table, col_bands, preferred_element_type=jnp.float32
    ).astype(jnp.bfloat16)
    half_pass = jnp.einsum(
        "sij,sjl->sil", row_pick, pixels, preferred_element_type=jnp.float32
    ).astype(jnp.bfloat16)
    return jnp.einsum(
        "sil,sml->sim", half_pass, col_pick, preferred_element_type=jnp.float32
    ).astype(jnp.bfloat16)


def weigh_sum(matched, weight, pos_table):
    weight_f = weight.astype(jnp.float32)
    weighted = weight_f[..., None] * matched
    table_f = pos_table.astype(jnp.float32)
    numerator = jnp.einsum("snp,snrc->nprc", table_f, weighted, precision=lax.Precision.HIGHEST)
    denominator = jnp.einsum("snp,snr->npr", table_f, weight_f, precision=lax.Precision.HIGHEST)
    return (numerator, denominator)


def pack_slots(values, placement):
    flattened = values.reshape(values.shape[0], -1)
    packed = jnp.dot(placement, flattened, preferred_element_type=jnp.float32).astype(jnp.bfloat16)
    return packed.reshape((placement.shape[0],) + values.shape[1:])


def per_device(image, inv_var, kernel_index, dest, position, row_taps, col_taps):
    tile_count = lax.axis_size("tile")
    block_count, side_len, _ = image.shape
    slot_count = tile_count * CAP
    row_bands = band_tables(row_taps, side_len)
    col_bands = band_tables(col_taps, side_len)
    target = dest[:, 0]
    earlier = lax.broadcasted_iota(jnp.int32, (block_count, block_count), 1) < lax.broadcasted_iota(
        jnp.int32, (block_count, block_count), 0
    )
    before = jnp.sum(((target[:, None] == target[None, :]) & earlier).astype(jnp.int32), axis=1)
    slot_of = target * CAP + before
    placement = (
        lax.broadcasted_iota(jnp.int32, (slot_count, block_count), 0) == slot_of[None, :]
    ).astype(jnp.bfloat16)
    pos_table = (
        position[:, None] == lax.broadcasted_iota(jnp.int32, (block_count, POS), 1)
    ).astype(jnp.bfloat16)
    kernel_table = (
        kernel_index[:, None] == lax.broadcasted_iota(jnp.int32, (block_count, NB), 1)
    ).astype(jnp.bfloat16)
    slot_pos = pack_slots(pos_table, placement).reshape(tile_count, CAP, POS)
    slot_weight = pack_slots(inv_var, placement).reshape(tile_count, CAP, side_len)
    slot_pixels = pack_slots(image, placement).reshape(tile_count, CAP, side_len, side_len)
    slot_kernel = pack_slots(kernel_table, placement).reshape(tile_count, CAP, NB)
    pixels = lax.all_to_all(slot_pixels, "tile", split_axis=0, concat_axis=0, tiled=True)
    weight = lax.all_to_all(slot_weight, "tile", split_axis=0, concat_axis=0, tiled=True)
    arrived_pos = lax.all_to_all(slot_pos, "tile", split_axis=0, concat_axis=0, tiled=True)
    kernels = lax.all_to_all(slot_kernel, "tile", split_axis=0, concat_axis=0, tiled=True)
    sources = pixels.shape[0]
    item_count = pixels.shape[1]
    matched = match_blocks(
        pixels.reshape(sources * item_count, side_len, side_len),
        kernels.reshape(sources * item_count, NB),
        row_bands,
        col_bands,
    )
    numerator, denominator = weigh_sum(
        matched.reshape(sources, item_count, side_len, side_len), weight, arrived_pos
    )
    numerator, denominator = (
        lax.psum_scatter(jnp.sum(numerator, 0), "visit", scatter_dimension=1, tiled=True),
        lax.psum_scatter(jnp.sum(denominator, 0), "visit", scatter_dimension=1, tiled=True),
    )
    coadd_tile = numerator / jnp.maximum(denominator, 1.0)[..., None]
    return coadd_tile[None]


def solution(mesh):
    in_specs = (
        P(("visit", "tile"), None, None),
        P(("visit", "tile"), None),
        P(("visit", "tile")),
        P(("visit", "tile"), None),
        P(("visit", "tile")),
        P(),
        P(),
    )
    out_specs = P("tile", None, "visit", None)
    return jax.shard_map(
        per_device, mesh=mesh, in_specs=in_specs, out_specs=out_specs, check_vma=False
    )
```

profile of v0, /device:TPU:0, one launch (start us, length us, event | category | flops | bytes accessed | tf_op | source)
XLA Modules:
  0.0 586.8 jit_solution(18268810657750778838)
XLA Ops:
  6.5 0.0 copy-start
  6.5 0.9 convert_reduce_fusion
  7.4 0.7 multiply_add_fusion
  8.1 0.9 convolution_convert_fusion.5
  9.0 0.7 copy.53
  9.7 8.1 %all-to-all-start = ((bf16[16,2,4]{2,1,0:T(2,128)(2,1)}), bf16[16,2,4]{2,1,0:T(2,128)(2,1)S(1)}, u32[]{:S(2)}, u32[]{:S(2)}) async-start(bf16[16,2,4]{2,1,0:T(2,128)(2,1)} %bitcast.1), calls=%async_computation | async-start | bytes 16384 | tf_op jit(solution)/shard_map/all_to_all | solution.py:80
  17.9 0.9 convolution_convert_fusion.4
  18.8 0.7 copy.56
  19.4 5.9 %all-to-all-done = bf16[16,2,4]{2,1,0:T(2,128)(2,1)S(1)} async-done(((bf16[16,2,4]{2,1,0:T(2,128)(2,1)}), bf16[16,2,4]{2,1,0:T(2,128)(2,1)S(1)}, u32[]{:S(2)}, u32[]{:S(2)}) %all-to-all-start) | async-done | bytes 288 | tf_op jit(solution)/shard_map/all_to_all | solution.py:80
  25.3 3.5 all-to-all-start.2
  28.8 0.0 copy-done
  28.8 0.1 convolution_convert_fusion.3
  29.0 6.7 %pad.9 = bf16[16,512,512]{2,1,0:T(8,128)(2,1)} pad(bf16[12,512,512]{2,1,0:T(8,128)(2,1)} %param.7, bf16[]{:T(256)} %constant.3.clone.1), padding=0_4x0_0x0_0 | pad | bytes 14680066
  35.7 11.4 %copy.78 = bf16[2,8,512,512]{3,1,2,0:T(8,128)(2,1)} copy(bf16[2,8,512,512]{3,2,1,0:T(8,128)(2,1)} %bitcast.47) | data formatting | bytes 16777216
  47.0 0.6 reshape.49
  47.7 0.0 all-to-all-done.2
  47.7 7.2 %all-to-all-start.1 = ((bf16[16,2,512]{2,1,0:T(2,128)(2,1)}), bf16[16,2,512]{2,1,0:T(2,128)(2,1)S(1)}, u32[]{:S(2)}, u32[]{:S(2)}) async-start(bf16[16,2,512]{2,1,0:T(2,128)(2,1)} %reshape.49), calls=%async_computation.1 | async-start | bytes 65536 | tf_op jit(solution)/shard_map/all_to_all | solution.py:79
  54.8 11.4 %convolution_convert_fusion = bf16[32,262144]{1,0:T(8,128)(2,1)} fusion(bf16[12,262144]{1,0:T(8,128)(2,1)} %bitcast.46, s32[12]{0:T(128)S(1)} %multiply_add_fusion), kind=kOutput, calls=%fused_computation | convolution fusion | flops 209715584 | bytes 23068720 | tf_op jit(solution)/shard_map/dot_general | solution.py:49
  66.3 16.7 %copy.79 = bf16[4,8,512,512]{3,2,1,0:T(8,128)(2,1)} copy(bf16[4,8,512,512]{3,1,2,0:T(8,128)(2,1)} %bitcast.44) | data formatting | bytes 33554432
  82.9 0.0 all-to-all-done.1
  82.9 7.4 %all-to-all-start.3 = ((bf16[16,2,512,512]{3,2,1,0:T(8,128)(2,1)}), bf16[16,2,512,512]{3,2,1,0:T(8,128)(2,1)}, u32[]{:S(2)}, u32[]{:S(2)}) async-start(bf16[16,2,512,512]{3,2,1,0:T(8,128)(2,1)} %bitcast.45), calls=%async_computation.3 | async-start | bytes 33554432 | tf_op jit(solution)/shard_map/all_to_all | solution.py:78
  90.3 9.7 %reduce-scatter.4.cloned.1.call-start = ((), (), s32[]{:S(2)}) async-start(), calls=%async_computation.5 | async-start | bytes 294912
  100.1 0.1 pad.7
  100.2 0.6 reverse.1
  100.8 0.1 slice.21
  100.9 4.3 tile.8
  105.2 14.0 %reshape.69 = bf16[4190208]{0:T(1024)(128)(2,1)} reshape(bf16[8,512,1023]{2,1,0:T(8,128)(2,1)} %tile.8) | data formatting | bytes 16760832
  119.2 15.5 %tile.9 = bf16[8,523776]{1,0:T(8,128)(2,1)} reshape(bf16[4190208]{0:T(1024)(128)(2,1)} %reshape.69) | data formatting | bytes 16760832 | tf_op jit(solution)/shard_map/tile | solution.py:18
  134.7 8.1 %slice.16 = bf16[8,523264]{1,0:T(8,128)(2,1)} slice(bf16[8,523776]{1,0:T(8,128)(2,1)} %tile.9), slice={[0:8], [511:523775]} | slice | bytes 16744448 | tf_op jit(solution)/shard_map/slice | solution.py:19
  142.8 0.0 copy-start.3
  142.8 10.5 %reshape.71 = bf16[4186112]{0:T(1024)(128)(2,1)} reshape(bf16[8,523264]{1,0:T(8,128)(2,1)} %slice.16) | data formatting | bytes 16744448
  153.3 16.5 %reshape.52 = bf16[8,512,1022]{2,1,0:T(8,128)(2,1)} reshape(bf16[4186112]{0:T(1024)(128)(2,1)} %reshape.71) | data formatting | bytes 16744448 | tf_op jit(solution)/shard_map/reshape | solution.py:20
  169.8 4.5 slice.17
  174.3 0.1 pad.8
  174.4 0.6 reverse
  175.0 0.1 slice.20
  175.1 4.4 tile.20
  179.5 14.4 %reshape.65 = bf16[4190208]{0:T(1024)(128)(2,1)} reshape(bf16[8,512,1023]{2,1,0:T(8,128)(2,1)} %tile.20) | data formatting | bytes 16760832
  193.9 15.6 %tile.21 = bf16[8,523776]{1,0:T(8,128)(2,1)} reshape(bf16[4190208]{0:T(1024)(128)(2,1)} %reshape.65) | data formatting | bytes 16760832 | tf_op jit(solution)/shard_map/tile | solution.py:18
  209.5 8.0 %slice.18 = bf16[8,523264]{1,0:T(8,128)(2,1)} slice(bf16[8,523776]{1,0:T(8,128)(2,1)} %tile.21), slice={[0:8], [511:523775]} | slice | bytes 16744448 | tf_op jit(solution)/shard_map/slice | solution.py:19
  217.5 10.5 %reshape.67 = bf16[4186112]{0:T(1024)(128)(2,1)} reshape(bf16[8,523264]{1,0:T(8,128)(2,1)} %slice.18) | data formatting | bytes 16744448
  228.0 16.5 %reshape.55 = bf16[8,512,1022]{2,1,0:T(8,128)(2,1)} reshape(bf16[4186112]{0:T(1024)(128)(2,1)} %reshape.67) | data formatting | bytes 16744448 | tf_op jit(solution)/shard_map/reshape | solution.py:20
  244.5 4.5 slice.19
  248.9 0.1 copy.64
  249.0 11.3 %convolution_convert_fusion.2 = bf16[32,512,512]{2,0,1:T(8,128)(2,1)} fusion(bf16[32,8,1]{1,0,2:T(8,128)(2,1)S(1)} %bitcast.49, bf16[8,512,512]{2,1,0:T(8,128)(2,1)} %slice.17), kind=kOutput, calls=%fused_computation.10 | convolution fusion | flops 142606336 | bytes 20972032 | tf_op jit(solution)/shard_map/sk,kij->sij/dot_general | solution.py:24
  260.3 11.7 %convolution_convert_fusion.1 = bf16[32,512,512]{2,0,1:T(8,128)(2,1)} fusion(bf16[32,8,1]{1,0,2:T(8,128)(2,1)S(1)} %bitcast.50, bf16[8,512,512]{2,1,0:T(8,128)(2,1)} %slice.19), kind=kOutput, calls=%fused_computation.9 | convolution fusion | flops 142606336 | bytes 20972032 | tf_op jit(solution)/shard_map/sk,kij->sij/dot_general | solution.py:27
  272.0 0.2 copy.55
  272.2 1.0 convolution_bitcast_fusion
  273.2 0.0 reduce-scatter.4.cloned.1.call-update
  273.2 0.0 all-reduce.5.cloned.1.call-start
  273.3 106.5 %all-to-all-done.3 = bf16[16,2,512,512]{3,2,1,0:T(8,128)(2,1)} async-done(((bf16[16,2,512,512]{3,2,1,0:T(8,128)(2,1)}), bf16[16,2,512,512]{3,2,1,0:T(8,128)(2,1)}, u32[]{:S(2)}, u32[]{:S(2)}) %all-to-all-start.3) | async-done | bytes 16777248 | tf_op jit(solution)/shard_map/all_to_all | solution.py:78
  379.8 35.6 %fusion.46 = bf16[32,512,512]{2,1,0:T(8,128)(2,1)} fusion(bf16[32,512,512]{2,1,0:T(8,128)(2,1)} %bitcast.6, bf16[32,512,512]{2,0,1:T(8,128)(2,1)} %convolution_convert_fusion.2), kind=kOutput, calls=%fused_computation.7.clone.clone.clone.1 | convolution fusion | flops 8598323200 | bytes 50331648 | tf_op jit(solution)/shard_map/sij,sjl->sil/dot_general | solution.py:30
  415.4 26.3 %fusion.11 = bf16[32,512,512]{2,1,0:T(8,128)(2,1)} fusion(bf16[32,512,512]{2,0,1:T(8,128)(2,1)} %convolution_convert_fusion.1, bf16[32,512,512]{2,1,0:T(8,128)(2,1)} %fusion.46), kind=kOutput, calls=%fused_computation.11 | convolution fusion | flops 8598323200 | bytes 50331648 | tf_op jit(solution)/shard_map/sil,sml->sim/dot_general | solution.py:33
  441.7 18.8 %convert.1 = f32[16,2,512,512]{3,2,1,0:T(8,128)} convert(bf16[16,2,512,512]{3,2,1,0:T(8,128)(2,1)} %bitcast.48) | non-fusion elementwise | flops 8388608 | bytes 50331648 | tf_op jit(solution)/shard_map/convert_element_type | solution.py:40
  460.5 39.3 %fusion.20 = f32[4,512,512]{2,0,1:T(4,128)} fusion(f32[16,2,512,512]{3,2,1,0:T(8,128)} %convert.1, f32[16,2,512]{0,1,2:T(2,128)S(1)} %copy.55, bf16[16,2,4]{0,2,1:T(4,128)(2,1)S(1)} %copy.64), kind=kOutput, calls=%fused_computation.14 | convolution fusion | flops 411041792 | bytes 37814528 | tf_op jit(solution)/shard_map/snp,snrc->nprc/dot_general | solution.py:42
  499.8 0.0 all-reduce.5.cloned.1.call-update
  499.8 0.6 dynamic-slice
  501.1 0.0 reduce-scatter.4.cloned.1.call-done
  501.1 0.8 copy.75
  502.0 0.1 copy.67
  502.1 75.5 %all-reduce.5.cloned.1.call-done = f32[4,512,512]{2,0,1:T(4,128)} async-done(((f32[4,512,512]{2,0,1:T(4,128)}), f32[4,512,512]{2,0,1:T(4,128)}) %all-reduce.5.cloned.1.call-update) | async-done | bytes 4194320
  577.6 1.2 fusion.21
  578.8 1.0 copy.68
  579.8 0.0 copy-done.1
  (10 shorter events, 0.0 us)
Async XLA Ops:
  6.5 22.3 %copy-start = (bf16[12,512]{1,0:T(8,128)(2,1)S(1)}, bf16[12,512]{1,0:T(8,128)(2,1)}, u32[]{:S(2)}) copy-start(bf16[12,512]{1,0:T(8,128)(2,1)} %param.8) | copy-start | bytes 36868
  9.7 15.6 %all-to-all-start = ((bf16[16,2,4]{2,1,0:T(2,128)(2,1)}), bf16[16,2,4]{2,1,0:T(2,128)(2,1)S(1)}, u32[]{:S(2)}, u32[]{:S(2)}) async-start(bf16[16,2,4]{2,1,0:T(2,128)(2,1)} %bitcast.1), calls=%async_computation | async-start | bytes 16384 | tf_op jit(solution)/shard_map/all_to_all | solution.py:80
  25.3 22.3 %all-to-all-start.2 = ((bf16[16,2,8]{2,1,0:T(2,128)(2,1)}), bf16[16,2,8]{2,1,0:T(2,128)(2,1)S(1)}, u32[]{:S(2)}, u32[]{:S(2)}) async-start(bf16[16,2,8]{2,1,0:T(2,128)(2,1)} %bitcast.3), calls=%async_computation.2 | async-start | bytes 16384 | tf_op jit(solution)/shard_map/all_to_all | solution.py:81
  47.7 35.3 %all-to-all-start.1 = ((bf16[16,2,512]{2,1,0:T(2,128)(2,1)}), bf16[16,2,512]{2,1,0:T(2,128)(2,1)S(1)}, u32[]{:S(2)}, u32[]{:S(2)}) async-start(bf16[16,2,512]{2,1,0:T(2,128)(2,1)} %reshape.49), calls=%async_computation.1 | async-start | bytes 65536 | tf_op jit(solution)/shard_map/all_to_all | solution.py:79
  82.9 17.2 %copy-start.2 = (f32[8,41]{1,0:T(8,128)S(1)}, f32[8,41]{1,0:T(8,128)}, u32[]{:S(2)}) copy-start(f32[8,41]{1,0:T(8,128)} %param.12) | copy-start | bytes 3940
  82.9 296.9 %all-to-all-start.3 = ((bf16[16,2,512,512]{3,2,1,0:T(8,128)(2,1)}), bf16[16,2,512,512]{3,2,1,0:T(8,128)(2,1)}, u32[]{:S(2)}, u32[]{:S(2)}) async-start(bf16[16,2,512,512]{3,2,1,0:T(8,128)(2,1)} %bitcast.45), calls=%async_computation.3 | async-start | bytes 33554432 | tf_op jit(solution)/shard_map/all_to_all | solution.py:78
  90.3 410.8 %reduce-scatter.4.cloned.1.call-start = ((), (), s32[]{:S(2)}) async-start(), calls=%async_computation.5 | async-start | bytes 294912
  142.8 31.5 %copy-start.3 = (f32[8,41]{1,0:T(8,128)S(1)}, f32[8,41]{1,0:T(8,128)}, u32[]{:S(2)}) copy-start(f32[8,41]{1,0:T(8,128)} %param.13) | copy-start | bytes 3940
  273.2 304.4 %all-reduce.5.cloned.1.call-start = ((), (), s32[]{:S(2)}) async-start(), calls=%async_computation.6 | async-start | bytes 8388608
  441.7 138.1 %copy-start.1 = (bf16[12,512]{1,0:T(8,128)(2,1)S(1)}, bf16[12,512]{1,0:T(8,128)(2,1)}, u32[]{:S(2)}) copy-start(bf16[12,512]{1,0:T(8,128)(2,1)} %param.8) | copy-start | bytes 36868
  460.5 39.3 %copy-start.4 = (u32[128]{0:T(128)S(1)}, u32[128]{0:T(128)}, u32[]{:S(2)}) copy-start(u32[128]{0:T(128)} %constant.20) | copy-start | bytes 1540
Sparse Core Ops, SparseCore 0:
  273.4 31.9 reduce-scatter.3
  499.9 77.6 all-reduce.4
where the time goes:
time: 596 us; the launch traced here: 587 us
  local copies, waits for them, and re-layouts  188 us (32%)
  waiting for transfers between devices  188 us (32%)
  matrix products  138 us (23%)
  starting transfers between devices  35.9 us (6%)
  other arithmetic  21.6 us (4%)
  between operations  14.4 us (2%)
    all_to_all x1, waiting for transfers between devices, per_device(): lax.all_to_all(slot_pixels, 'tile', split_axis=0, concat_axis=0, tiled=True)  107 us
    unnamed x23, local copies, waits for them, and re-layouts  87 us
    unnamed x4, waiting for transfers between devices  75.6 us
    another operation x4, local copies, waits for them, and re-layouts, band_tables(): repeated = jnp.tile(flipped, (1, side_len))  39.8 us
    dot_general x1, matrix products, weigh_sum(): jnp.einsum('snp,snrc->nprc', table_f, weighted, precision=lax.Precision.H...  39.3 us
    dot_general x1, matrix products, match_blocks(): jnp.einsum('sij,sjl->sil', row_pick, pixels, preferred_element_type=jnp.f...  35.6 us
    reshape x2, local copies, waits for them, and re-layouts, band_tables(): return window.reshape(kernel_count, side_len, span - 1)[:, :, :side_len]  33 us
    dot_general x1, matrix products, match_blocks(): jnp.einsum('sil,sml->sim', half_pass, col_pick, preferred_element_type=jn...  26.3 us
  transfers between devices with their start and end apart: 6, of which 3 were waited for; matrix products, arithmetic and copies ran while one was open for 58% of the time, Pallas kernels for 0%

commit v1 on v0

v1 whole, which is shorter than its diff:
```python
import functools

import jax
import jax.numpy as jnp
from jax import lax
from jax.experimental import pallas as pl
from jax.experimental.pallas import tpu as pltpu
from jax.sharding import PartitionSpec as P

NB = 8
POS = 4
LANE = 128
BF = jnp.bfloat16
F32 = jnp.float32
CHUNKS = ((0, 128), (128, 128), (256, 128), (384, 128))


def toeplitz(row, length):
    wide = jnp.broadcast_to(row, (LANE, length))
    return pltpu.roll(wide, 0, 1, stride=1, stride_axis=0)


def match_kernel(col0, width, kidx_ref, rtap_ref, ctap_ref, img_ref, iv_ref, *rest):
    outs, (rband, cband, whole) = rest[:-3], rest[-3:]
    parts = len(outs)
    b = pl.program_id(0)
    side = img_ref.shape[2]
    blocks = iv_ref.shape[0]
    taps = rtap_ref.shape[1]
    half = (taps - 1) // 2
    length = 3 * LANE
    rows = side // parts

    @pl.when(b == 0)
    def _():
        q = lax.broadcasted_iota(jnp.int32, (taps, length), 0)
        n = lax.broadcasted_iota(jnp.int32, (taps, length), 1)
        pick = (n + q == LANE + half).astype(F32).astype(BF)
        rbase = jnp.dot(rtap_ref[...].astype(BF), pick, preferred_element_type=F32)
        cbase = jnp.dot(ctap_ref[...].astype(BF), pick, preferred_element_type=F32)
        rband[...] = jnp.zeros_like(rband)
        tiles = side // LANE
        for k in range(NB):
            t = toeplitz(rbase[k : k + 1], length).astype(BF)
            for a in range(tiles):
                lo, hi = max(a - 1, 0), min(a + 2, tiles)
                off = (lo - (a - 1)) * LANE
                rband[k, a * LANE : (a + 1) * LANE, lo * LANE : hi * LANE] = t[
                    :, off : off + (hi - lo) * LANE
                ]
            cband[k] = toeplitz(cbase[k : k + 1], length).astype(BF)

    k = kidx_ref[b]
    tiles = side // LANE
    pieces = []
    for g in range(col0 // LANE, (col0 + width) // LANE):
        lo, hi = max(g - 1, 0), min(g + 2, tiles)
        off = (lo - (g - 1)) * LANE
        window = img_ref[0, :, lo * LANE : hi * LANE]
        ct = cband[k, :, off : off + (hi - lo) * LANE]
        pieces.append(
            lax.dot_general(window, ct, (((1,), (1,)), ((), ())), preferred_element_type=F32).astype(BF)
        )
    mid = pieces[0] if len(pieces) == 1 else jnp.concatenate(pieces, axis=1)
    matched = jnp.dot(rband[k], mid, preferred_element_type=F32)
    onehot = (lax.broadcasted_iota(jnp.int32, (blocks, width), 0) == b).astype(F32).astype(BF)
    weight = lax.dot_general(iv_ref[...], onehot, (((0,), (0,)), ((), ())), preferred_element_type=F32)
    whole[...] = (matched * weight).astype(BF)
    me = lax.axis_index("visit")
    for i in range(parts):
        to = lax.rem(me + i, parts)
        outs[i][0] = whole[pl.ds(pl.multiple_of(to * rows, rows), rows), :]


def match_chunk(col0, width, parts, kidx, row_taps, col_taps, image, inv_var):
    blocks, side, _ = image.shape
    rows = side // parts
    length = 3 * LANE
    full = lambda shape: pl.BlockSpec(shape, lambda b, *_: (0,) * len(shape))
    grid_spec = pltpu.PrefetchScalarGridSpec(
        num_scalar_prefetch=1,
        grid=(blocks,),
        in_specs=[
            full(row_taps.shape),
            full(col_taps.shape),
            pl.BlockSpec((1, side, side), lambda b, *_: (b, 0, 0)),
            full(inv_var.shape),
        ],
        out_specs=[pl.BlockSpec((1, rows, width), lambda b, *_: (b, 0, 0))] * parts,
        scratch_shapes=[
            pltpu.VMEM((NB, side, side), BF),
            pltpu.VMEM((NB, LANE, length), BF),
            pltpu.VMEM((side, width), BF),
        ],
    )
    return pl.pallas_call(
        functools.partial(match_kernel, col0, width),
        grid_spec=grid_spec,
        out_shape=[jax.ShapeDtypeStruct((blocks, rows, width), BF)] * parts,
        compiler_params=pltpu.CompilerParams(vmem_limit_bytes=32 << 20),
        cost_estimate=pl.CostEstimate(
            flops=2 * blocks * side * side * 256 * 2,
            bytes_accessed=image.size * 2 + blocks * side * width * 2,
            transcendentals=0,
        ),
        name="match",
    )(kidx, row_taps, col_taps, image, inv_var)


def gather_kernel(combo_ref, *rest):
    parts = len(rest) - 2
    pieces, out_ref, acc = rest[:parts], rest[parts], rest[parts + 1]
    blocks = pieces[0].shape[0]
    me = lax.axis_index("visit")
    acc[...] = jnp.zeros_like(acc)
    for i in range(parts):
        base = lax.rem(me - i + parts, parts) * blocks
        for b in range(blocks):
            c = combo_ref[base + b]
            acc[c] += pieces[i][b].astype(F32)
    out_ref[...] = acc[...].astype(BF)


def gather_chunk(combos, pieces, count):
    blocks, rows, width = pieces[0].shape
    vm = pl.BlockSpec(memory_space=pltpu.VMEM)
    return pl.pallas_call(
        gather_kernel,
        in_specs=[pl.BlockSpec(memory_space=pltpu.SMEM)] + [vm] * len(pieces),
        out_specs=vm,
        out_shape=jax.ShapeDtypeStruct((count, rows, width), BF),
        scratch_shapes=[pltpu.VMEM((count, rows, width), F32)],
        compiler_params=pltpu.CompilerParams(vmem_limit_bytes=32 << 20),
        cost_estimate=pl.CostEstimate(
            flops=blocks * len(pieces) * rows * width * 2,
            bytes_accessed=blocks * len(pieces) * rows * width * 2 * 4,
            transcendentals=0,
        ),
        name="gather",
    )(combos, *pieces)


def per_device(image, inv_var, kernel_index, dest, position, row_taps, col_taps):
    tiles = lax.axis_size("tile")
    visits = lax.axis_size("visit")
    blocks, side, _ = image.shape
    rows = side // visits
    count = tiles * POS

    combo = dest[:, 0] * POS + position
    packed = jnp.concatenate(
        [inv_var, jnp.broadcast_to(combo.astype(BF)[:, None], (blocks, LANE))], axis=1
    )
    gathered = lax.all_gather(packed, "visit", axis=0, tiled=True)
    combos = gathered[:, side].astype(jnp.int32)
    me = lax.axis_index("visit")
    iv_rows = lax.dynamic_slice_in_dim(gathered, me * rows, rows, axis=1)
    table = (lax.broadcasted_iota(jnp.int32, (count, visits * blocks), 0) == combos[None, :]).astype(BF)
    den_part = jnp.dot(table, iv_rows, preferred_element_type=F32)
    den_all = lax.all_to_all(den_part.reshape(tiles, POS, rows), "tile", 0, 0, tiled=True)
    den = jnp.maximum(jnp.sum(den_all, axis=0), 1.0)

    results = []
    for col0, width in CHUNKS:
        pieces = match_chunk(col0, width, visits, kernel_index, row_taps, col_taps, image, inv_var)
        arrived = [pieces[0]]
        for i in range(1, visits):
            perm = [(s, (s + i) % visits) for s in range(visits)]
            arrived.append(lax.ppermute(pieces[i], "visit", perm))
        partial = gather_chunk(combos, arrived, count)
        swapped = lax.all_to_all(partial.reshape(tiles, POS * rows, width), "tile", 0, 0, tiled=True)
        total = jnp.sum(swapped.reshape(tiles, POS, rows, width).astype(F32), axis=0)
        results.append(total / den[:, :, None])
    return jnp.concatenate(results, axis=2)[None]


def solution(mesh):
    in_specs = (
        P(("visit", "tile"), None, None),
        P(("visit", "tile"), None),
        P(("visit", "tile")),
        P(("visit", "tile"), None),
        P(("visit", "tile")),
        P(),
        P(),
    )
    out_specs = P("tile", None, "visit", None)
    return jax.shard_map(
        per_device, mesh=mesh, in_specs=in_specs, out_specs=out_specs, check_vma=False
    )
```

time: 596 us -> 221 us (0.37); the launches traced: 587 us -> 220 us
  local copies, waits for them, and re-layouts: 188 us -> 15.3 us
  matrix products: 138 us -> 0.2 us
  waiting for transfers between devices: 188 us -> 60 us
  Pallas kernels: 0 us -> 47 us
  starting transfers between devices: 35.9 us -> 72.3 us
  blocking collectives: 0 us -> 19.8 us
  other arithmetic: 21.6 us -> 4.83 us
  between operations: 14.4 us -> 0.3 us
    dot_general x10 -> x1, matrix products: 138 us -> 0.2 us  [per_device(): den_part = jnp.dot(table, iv_rows, preferred_element_type=F32)]
    all_to_all x4 -> x5, waiting for transfers between devices: 112 us -> 21.6 us  [the longest x4 16.4 us: per_device(): lax.all_to_all(partial.reshape(tiles, POS * rows, width), 'tile', 0, 0, t...]
    unnamed x4 -> x0, waiting for transfers between devices: 75.6 us -> none
    unnamed x23 -> x31, local copies, waits for them, and re-layouts: 87 us -> 14.7 us
    pallas_call x0 -> x8, Pallas kernels: none -> 47 us  [the longest x4 38 us: match_chunk(): pl.pallas_call(functools.partial(match_kernel, col0, width), grid_spec=gr...]
    another operation x4 -> x0, local copies, waits for them, and re-layouts: 39.8 us -> none  [band_tables(): repeated = jnp.tile(flipped, (1, side_len))]
    ppermute x0 -> x28, starting transfers between devices: none -> 39.3 us  [per_device(): arrived.append(lax.ppermute(pieces[i], 'visit', perm))]
    ppermute x0 -> x28, waiting for transfers between devices: none -> 38.4 us  [per_device(): arrived.append(lax.ppermute(pieces[i], 'visit', perm))]
  transfers between devices with their start and end apart: 6 -> 33, of which waited for: 3 -> 18; matrix products, arithmetic and copies ran while one was open for 58% -> 2% of each run, Pallas kernels for 0% -> 17%
where the time goes in v1:
time: 221 us; the launch traced here: 220 us
  starting transfers between devices  72.3 us (33%)
  waiting for transfers between devices  60 us (27%)
  Pallas kernels  47 us (21%)
  blocking collectives  19.8 us (9%)
  local copies, waits for them, and re-layouts  15.3 us (7%)
  other arithmetic  4.83 us (2%)
    ppermute x28, starting transfers between devices, per_device(): arrived.append(lax.ppermute(pieces[i], 'visit', perm))  39.3 us
    ppermute x28, waiting for transfers between devices, per_device(): arrived.append(lax.ppermute(pieces[i], 'visit', perm))  38.4 us
    pallas_call x4, Pallas kernels, match_chunk(): pl.pallas_call(functools.partial(match_kernel, col0, width), grid_spec=gr...  38 us
    all_to_all x4, starting transfers between devices, per_device(): lax.all_to_all(partial.reshape(tiles, POS * rows, width), 'tile', 0, 0, t...  24.9 us
    all_gather x1, blocking collectives, per_device(): gathered = lax.all_gather(packed, 'visit', axis=0, tiled=True)  19.8 us
    all_to_all x4, waiting for transfers between devices, per_device(): lax.all_to_all(partial.reshape(tiles, POS * rows, width), 'tile', 0, 0, t...  16.4 us
    unnamed x31, local copies, waits for them, and re-layouts  14.7 us
    pallas_call x4, Pallas kernels, gather_chunk(): pl.pallas_call(gather_kernel, in_specs=[pl.BlockSpec(memory_space=pltpu.S...  9.09 us
  transfers between devices with their start and end apart: 33, of which 18 were waited for; matrix products, arithmetic and copies ran while one was open for 2% of the time, Pallas kernels for 17%

profile of v1, /device:TPU:0, one launch (start us, length us, event | category | flops | bytes accessed | tf_op | source)
XLA Modules:
  0.0 219.8 jit_solution(2998534656989647573)
XLA Ops:
  0.0 0.7 copy-done
  0.7 2.8 %copy-done.2 = bf16[12,512,512]{2,1,0:T(8,128)(2,1)S(1)} copy-done((bf16[12,512,512]{2,1,0:T(8,128)(2,1)S(1)}, bf16[12,512,512]{2,1,0:T(8,128)(2,1)}, u32[]{:S(2)}) %copy-start.2) | copy-done | bytes 6291480
  3.5 0.7 copy-done.6
  4.2 0.7 copy-done.8
  4.9 0.7 copy-done.10
  5.5 10.2 %match.5 = (bf16[12,64,128]{2,1,0:T(8,128)(2,1)S(1)}, bf16[12,64,128]{2,1,0:T(8,128)(2,1)S(1)}, bf16[12,64,128]{2,1,0:T(8,128)(2,1)S(1)}, bf16[12,64,128]{2,1,0:...) custom-call(s32[12]{0:T(128)S(1)} %copy-done.10, ...), custom_call_target="tpu_custom_call" | custom-call | flops 3221225472 | bytes 7864320 | tf_op jit(solution)/shard_map/match/pallas_call | solution.py:96
  15.8 1.6 collective-permute-start.8
  17.4 2.0 collective-permute-start.9
  19.5 2.0 collective-permute-start.10
  21.5 1.6 collective-permute-start.11
  23.2 19.8 %all-gather = bf16[8,12,640]{2,1,0:T(8,128)(2,1)S(1)} all-gather(bf16[1,12,640]{2,1,0:T(8,128)(2,1)S(1)} %maximum_bitcast_fusion.1), channel_id=1, replica_groups=mesh['visit'=8,'tile'=16] {'visit'}, dimensions={0}, use_global_device_ids=true | all-gather | bytes 138240 | tf_op jit(solution)/shard_map/all_gather | solution.py:154
  43.2 3.1 %collective-permute-start.12 = (bf16[12,64,128]{2,1,0:T(8,128)(2,1)S(1)}, bf16[12,64,128]{2,1,0:T(8,128)(2,1)S(1)}, u32[]{:S(2)}, u32[]{:S(2)}) collective-permute-start(bf16[12,64,128]{2,1,0:T(8,128)(2,1)S(1)} %get-tuple-element.51), channel_id=1, source_target_pairs={{0,96},{16,112},{32,0},{48,16},{64,32},{80,48},{96,64},{112,80},{1... | collective-permute-start | bytes 589832 | tf_op jit(solution)/shard_map/ppermute | solution.py:169
  46.3 0.2 fusion
  46.5 0.7 reshape.45
  47.2 8.0 %all-to-all-start.1 = ((f32[16,1,256]{2,1,0:T(1,128)}), f32[16,1,256]{2,1,0:T(1,128)S(1)}, u32[]{:S(2)}, u32[]{:S(2)}) async-start(f32[16,1,256]{2,1,0:T(1,128)} %reshape.45), calls=%async_computation.1 | async-start | bytes 32768 | tf_op jit(solution)/shard_map/all_to_all | solution.py:160
  55.3 2.3 %gather.5 = bf16[64,64,128]{2,1,0:T(8,128)(2,1)} custom-call(s32[96]{0:T(128)S(1)} %convert_reduce_fusion.4.combo_ref, bf16[12,64,128]{2,1,0:T(8,128)(2,1)S(1)} %get-tuple-element.45.rest_0_, bf16[12,64,128]{2,1,0:T(8,128)(2,1)S(1)} %collective-permute-done.7.rest_1_, bf16[12,64,128]{2,1,0:T(8,128)(2,1)S(1)} %collective-permute-done.8.rest_2_, ...), custom_call_target="tpu_custom_call" | custom-call | flops 1572864 | bytes 6291456 | tf_op jit(solution)/shard_map/gather/pallas_call | solution.py:127
  57.6 5.2 %all-to-all-done.1 = f32[16,1,256]{2,1,0:T(1,128)S(1)} async-done(((f32[16,1,256]{2,1,0:T(1,128)}), f32[16,1,256]{2,1,0:T(1,128)S(1)}, u32[]{:S(2)}, u32[]{:S(2)}) %all-to-all-start.1) | async-done | bytes 16416 | tf_op jit(solution)/shard_map/all_to_all | solution.py:160
  62.8 3.7 %all-to-all-start.2 = ((bf16[16,256,128]{2,1,0:T(8,128)(2,1)}), bf16[16,256,128]{2,1,0:T(8,128)(2,1)S(1)}, u32[]{:S(2)}, u32[]{:S(2)}) async-start(bf16[16,256,128]{2,1,0:T(8,128)(2,1)} %bitcast.5), calls=%async_computation.2 | async-start | bytes 2097152 | tf_op jit(solution)/shard_map/all_to_all | solution.py:171
  66.6 2.8 %copy-done.3 = bf16[12,512,512]{2,1,0:T(8,128)(2,1)S(1)} copy-done((bf16[12,512,512]{2,1,0:T(8,128)(2,1)S(1)}, bf16[12,512,512]{2,1,0:T(8,128)(2,1)}, u32[]{:S(2)}) %copy-start.3) | copy-done | bytes 6291480
  69.3 8.8 %match.4 = (bf16[12,64,128]{2,1,0:T(8,128)(2,1)S(1)}, bf16[12,64,128]{2,1,0:T(8,128)(2,1)S(1)}, bf16[12,64,128]{2,1,0:T(8,128)(2,1)S(1)}, bf16[12,64,128]{2,1,0:...) custom-call(s32[12]{0:T(128)S(1)} %copy-done.11, ...), custom_call_target="tpu_custom_call" | custom-call | flops 3221225472 | bytes 7864320 | tf_op jit(solution)/shard_map/match/pallas_call | solution.py:96
  78.1 1.7 collective-permute-start.1
  79.9 0.2 collective-permute-start.2
  80.0 3.9 %collective-permute-start.3 = (bf16[12,64,128]{2,1,0:T(8,128)(2,1)S(1)}, bf16[12,64,128]{2,1,0:T(8,128)(2,1)S(1)}, u32[]{:S(2)}, u32[]{:S(2)}) collective-permute-start(bf16[12,64,128]{2,1,0:T(8,128)(2,1)S(1)} %get-tuple-element.41), channel_id=1, source_target_pairs={{0,64},{16,80},{32,96},{48,112},{64,0},{80,16},{96,32},{112,48},{1... | collective-permute-start | bytes 589832 | tf_op jit(solution)/shard_map/ppermute | solution.py:169
  83.9 2.0 collective-permute-done.rest_1_
  85.9 1.2 collective-permute-done.1.rest_2_
  87.1 2.6 %collective-permute-start.6 = (bf16[12,64,128]{2,1,0:T(8,128)(2,1)S(1)}, bf16[12,64,128]{2,1,0:T(8,128)(2,1)S(1)}, u32[]{:S(2)}, u32[]{:S(2)}) collective-permute-start(bf16[12,64,128]{2,1,0:T(8,128)(2,1)S(1)} %get-tuple-element.44), channel_id=1, source_target_pairs={{0,112},{16,0},{32,16},{48,32},{64,48},{80,64},{96,80},{112,96},{1... | collective-permute-start | bytes 589832 | tf_op jit(solution)/shard_map/ppermute | solution.py:169
  89.7 4.0 %collective-permute-done.2.rest_3_ = bf16[12,64,128]{2,1,0:T(8,128)(2,1)S(1)} collective-permute-done((bf16[12,64,128]{2,1,0:T(8,128)(2,1)S(1)}, bf16[12,64,128]{2,1,0:T(8,128)(2,1)S(1)}, u32[]{:S(2)}, u32[]{:S(2)}) %collective-permute-start.2) | collective-permute-done | bytes 196640 | tf_op jit(solution)/shard_map/ppermute | solution.py:169
  93.7 1.2 collective-permute-done.3.rest_4_
  94.9 2.2 %collective-permute-done.4.rest_5_ = bf16[12,64,128]{2,1,0:T(8,128)(2,1)S(1)} collective-permute-done((bf16[12,64,128]{2,1,0:T(8,128)(2,1)S(1)}, bf16[12,64,128]{2,1,0:T(8,128)(2,1)S(1)}, u32[]{:S(2)}, u32[]{:S(2)}) %collective-permute-start.4) | collective-permute-done | bytes 196640 | tf_op jit(solution)/shard_map/ppermute | solution.py:169
  97.1 0.8 collective-permute-done.5.rest_6_
  97.9 1.4 collective-permute-done.6.rest_7_
  99.3 2.3 %gather.4 = bf16[64,64,128]{2,1,0:T(8,128)(2,1)} custom-call(s32[96]{0:T(128)S(1)} %convert_reduce_fusion.4.combo_ref, bf16[12,64,128]{2,1,0:T(8,128)(2,1)S(1)} %get-tuple-element.37.rest_0_, bf16[12,64,128]{2,1,0:T(8,128)(2,1)S(1)} %collective-permute-done.rest_1_, bf16[12,64,128]{2,1,0:T(8,128)(2,1)S(1)} %collective-permute-done.1.rest_2_, ...), custom_call_target="tpu_custom_call" | custom-call | flops 1572864 | bytes 6291456 | tf_op jit(solution)/shard_map/gather/pallas_call | solution.py:127
  101.6 7.1 %all-to-all-start = ((bf16[16,256,128]{2,1,0:T(8,128)(2,1)}), bf16[16,256,128]{2,1,0:T(8,128)(2,1)S(1)}, u32[]{:S(2)}, u32[]{:S(2)}) async-start(bf16[16,256,128]{2,1,0:T(8,128)(2,1)} %bitcast.2), calls=%async_computation | async-start | bytes 2097152 | tf_op jit(solution)/shard_map/all_to_all | solution.py:171
  108.8 2.8 %copy-done.4 = bf16[12,512,512]{2,1,0:T(8,128)(2,1)S(1)} copy-done((bf16[12,512,512]{2,1,0:T(8,128)(2,1)S(1)}, bf16[12,512,512]{2,1,0:T(8,128)(2,1)}, u32[]{:S(2)}) %copy-start.4) | copy-done | bytes 6291480
  111.5 8.8 %match.7 = (bf16[12,64,128]{2,1,0:T(8,128)(2,1)S(1)}, bf16[12,64,128]{2,1,0:T(8,128)(2,1)S(1)}, bf16[12,64,128]{2,1,0:T(8,128)(2,1)S(1)}, bf16[12,64,128]{2,1,0:...) custom-call(s32[12]{0:T(128)S(1)} %copy-done.11, ...), custom_call_target="tpu_custom_call" | custom-call | flops 3221225472 | bytes 7864320 | tf_op jit(solution)/shard_map/match/pallas_call | solution.py:96
  120.3 3.9 %collective-permute-start.21 = (bf16[12,64,128]{2,1,0:T(8,128)(2,1)S(1)}, bf16[12,64,128]{2,1,0:T(8,128)(2,1)S(1)}, u32[]{:S(2)}, u32[]{:S(2)}) collective-permute-start(bf16[12,64,128]{2,1,0:T(8,128)(2,1)S(1)} %get-tuple-element.62), channel_id=1, source_target_pairs={{0,16},{16,32},{32,48},{48,64},{64,80},{80,96},{96,112},{112,0},{1... | collective-permute-start | bytes 589832 | tf_op jit(solution)/shard_map/ppermute | solution.py:169
  124.3 4.1 %collective-permute-start.24 = (bf16[12,64,128]{2,1,0:T(8,128)(2,1)S(1)}, bf16[12,64,128]{2,1,0:T(8,128)(2,1)S(1)}, u32[]{:S(2)}, u32[]{:S(2)}) collective-permute-start(bf16[12,64,128]{2,1,0:T(8,128)(2,1)S(1)} %get-tuple-element.65), channel_id=1, source_target_pairs={{0,64},{16,80},{32,96},{48,112},{64,0},{80,16},{96,32},{112,48},{1... | collective-permute-start | bytes 589832 | tf_op jit(solution)/shard_map/ppermute | solution.py:169
  128.3 2.4 %collective-permute-start.26 = (bf16[12,64,128]{2,1,0:T(8,128)(2,1)S(1)}, bf16[12,64,128]{2,1,0:T(8,128)(2,1)S(1)}, u32[]{:S(2)}, u32[]{:S(2)}) collective-permute-start(bf16[12,64,128]{2,1,0:T(8,128)(2,1)S(1)} %get-tuple-element.67), channel_id=1, source_target_pairs={{0,96},{16,112},{32,0},{48,16},{64,32},{80,48},{96,64},{112,80},{1... | collective-permute-start | bytes 589832 | tf_op jit(solution)/shard_map/ppermute | solution.py:169
  130.7 10.0 %collective-permute-done.22.rest_2_ = bf16[12,64,128]{2,1,0:T(8,128)(2,1)S(1)} collective-permute-done((bf16[12,64,128]{2,1,0:T(8,128)(2,1)S(1)}, bf16[12,64,128]{2,1,0:T(8,128)(2,1)S(1)}, u32[]{:S(2)}, u32[]{:S(2)}) %collective-permute-start.22) | collective-permute-done | bytes 196640 | tf_op jit(solution)/shard_map/ppermute | solution.py:169
  140.8 0.8 collective-permute-done.25.rest_5_
  141.6 0.9 collective-permute-done.26.rest_6_
  142.5 2.4 %collective-permute-done.27.rest_7_ = bf16[12,64,128]{2,1,0:T(8,128)(2,1)S(1)} collective-permute-done((bf16[12,64,128]{2,1,0:T(8,128)(2,1)S(1)}, bf16[12,64,128]{2,1,0:T(8,128)(2,1)S(1)}, u32[]{:S(2)}, u32[]{:S(2)}) %collective-permute-start.27) | collective-permute-done | bytes 196640 | tf_op jit(solution)/shard_map/ppermute | solution.py:169
  144.9 2.3 %gather.7 = bf16[64,64,128]{2,1,0:T(8,128)(2,1)} custom-call(s32[96]{0:T(128)S(1)} %convert_reduce_fusion.4.combo_ref, bf16[12,64,128]{2,1,0:T(8,128)(2,1)S(1)} %get-tuple-element.61.rest_0_, bf16[12,64,128]{2,1,0:T(8,128)(2,1)S(1)} %collective-permute-done.21.rest_1_, bf16[12,64,128]{2,1,0:T(8,128)(2,1)S(1)} %collective-permute-done.22.rest_2_, ...), custom_call_target="tpu_custom_call" | custom-call | flops 1572864 | bytes 6291456 | tf_op jit(solution)/shard_map/gather/pallas_call | solution.py:127
  147.2 7.2 %all-to-all-start.4 = ((bf16[16,256,128]{2,1,0:T(8,128)(2,1)}), bf16[16,256,128]{2,1,0:T(8,128)(2,1)}, u32[]{:S(2)}, u32[]{:S(2)}) async-start(bf16[16,256,128]{2,1,0:T(8,128)(2,1)} %bitcast.9), calls=%async_computation.4 | async-start | bytes 2097152 | tf_op jit(solution)/shard_map/all_to_all | solution.py:171
  154.4 2.8 %copy-done.5 = bf16[12,512,512]{2,1,0:T(8,128)(2,1)S(1)} copy-done((bf16[12,512,512]{2,1,0:T(8,128)(2,1)S(1)}, bf16[12,512,512]{2,1,0:T(8,128)(2,1)}, u32[]{:S(2)}) %copy-start.5) | copy-done | bytes 6291480
  157.2 10.2 %match.6 = (bf16[12,64,128]{2,1,0:T(8,128)(2,1)S(1)}, bf16[12,64,128]{2,1,0:T(8,128)(2,1)S(1)}, bf16[12,64,128]{2,1,0:T(8,128)(2,1)S(1)}, bf16[12,64,128]{2,1,0:...) custom-call(s32[12]{0:T(128)S(1)} %copy-done.11, ...), custom_call_target="tpu_custom_call" | custom-call | flops 3221225472 | bytes 7864320 | tf_op jit(solution)/shard_map/match/pallas_call | solution.py:96
  167.4 0.6 collective-permute-start.14
  168.1 4.1 %collective-permute-start.17 = (bf16[12,64,128]{2,1,0:T(8,128)(2,1)S(1)}, bf16[12,64,128]{2,1,0:T(8,128)(2,1)S(1)}, u32[]{:S(2)}, u32[]{:S(2)}) collective-permute-start(bf16[12,64,128]{2,1,0:T(8,128)(2,1)S(1)} %get-tuple-element.57), channel_id=1, source_target_pairs={{0,64},{16,80},{32,96},{48,112},{64,0},{80,16},{96,32},{112,48},{1... | collective-permute-start | bytes 589832 | tf_op jit(solution)/shard_map/ppermute | solution.py:169
  172.1 2.9 %collective-permute-start.18 = (bf16[12,64,128]{2,1,0:T(8,128)(2,1)S(1)}, bf16[12,64,128]{2,1,0:T(8,128)(2,1)S(1)}, u32[]{:S(2)}, u32[]{:S(2)}) collective-permute-start(bf16[12,64,128]{2,1,0:T(8,128)(2,1)S(1)} %get-tuple-element.58), channel_id=1, source_target_pairs={{0,80},{16,96},{32,112},{48,0},{64,16},{80,32},{96,48},{112,64},{1... | collective-permute-start | bytes 589832 | tf_op jit(solution)/shard_map/ppermute | solution.py:169
  175.1 2.8 %collective-permute-done.15.rest_2_ = bf16[12,64,128]{2,1,0:T(8,128)(2,1)S(1)} collective-permute-done((bf16[12,64,128]{2,1,0:T(8,128)(2,1)S(1)}, bf16[12,64,128]{2,1,0:T(8,128)(2,1)S(1)}, u32[]{:S(2)}, u32[]{:S(2)}) %collective-permute-start.15) | collective-permute-done | bytes 196640 | tf_op jit(solution)/shard_map/ppermute | solution.py:169
  177.8 2.4 %collective-permute-start.20 = (bf16[12,64,128]{2,1,0:T(8,128)(2,1)S(1)}, bf16[12,64,128]{2,1,0:T(8,128)(2,1)S(1)}, u32[]{:S(2)}, u32[]{:S(2)}) collective-permute-start(bf16[12,64,128]{2,1,0:T(8,128)(2,1)S(1)} %get-tuple-element.60), channel_id=1, source_target_pairs={{0,112},{16,0},{32,16},{48,32},{64,48},{80,64},{96,80},{112,96},{1... | collective-permute-start | bytes 589832 | tf_op jit(solution)/shard_map/ppermute | solution.py:169
  180.4 5.1 %collective-permute-done.17.rest_4_ = bf16[12,64,128]{2,1,0:T(8,128)(2,1)S(1)} collective-permute-done((bf16[12,64,128]{2,1,0:T(8,128)(2,1)S(1)}, bf16[12,64,128]{2,1,0:T(8,128)(2,1)S(1)}, u32[]{:S(2)}, u32[]{:S(2)}) %collective-permute-start.17) | collective-permute-done | bytes 196640 | tf_op jit(solution)/shard_map/ppermute | solution.py:169
  185.5 0.8 collective-permute-done.19.rest_6_
  186.3 2.6 %collective-permute-done.20.rest_7_ = bf16[12,64,128]{2,1,0:T(8,128)(2,1)S(1)} collective-permute-done((bf16[12,64,128]{2,1,0:T(8,128)(2,1)S(1)}, bf16[12,64,128]{2,1,0:T(8,128)(2,1)S(1)}, u32[]{:S(2)}, u32[]{:S(2)}) %collective-permute-start.20) | collective-permute-done | bytes 196640 | tf_op jit(solution)/shard_map/ppermute | solution.py:169
  188.9 2.3 %gather.6 = bf16[64,64,128]{2,1,0:T(8,128)(2,1)} custom-call(s32[96]{0:T(128)S(1)} %convert_reduce_fusion.4.combo_ref, bf16[12,64,128]{2,1,0:T(8,128)(2,1)S(1)} %get-tuple-element.53.rest_0_, bf16[12,64,128]{2,1,0:T(8,128)(2,1)S(1)} %collective-permute-done.14.rest_1_, bf16[12,64,128]{2,1,0:T(8,128)(2,1)S(1)} %collective-permute-done.15.rest_2_, ...), custom_call_target="tpu_custom_call" | custom-call | flops 1572864 | bytes 6291456 | tf_op jit(solution)/shard_map/gather/pallas_call | solution.py:127
  191.1 6.9 %all-to-all-start.3 = ((bf16[16,256,128]{2,1,0:T(8,128)(2,1)}), bf16[16,256,128]{2,1,0:T(8,128)(2,1)}, u32[]{:S(2)}, u32[]{:S(2)}) async-start(bf16[16,256,128]{2,1,0:T(8,128)(2,1)} %bitcast.7), calls=%async_computation.3 | async-start | bytes 2097152 | tf_op jit(solution)/shard_map/all_to_all | solution.py:171
  198.1 0.5 broadcast.13
  198.6 0.7 reduce.6
  199.4 0.1 convert_reduce_fusion.2
  199.6 0.1 convert_reduce_fusion.3
  199.7 1.4 convert_reduce_fusion
  201.1 16.4 %all-to-all-done.3 = bf16[16,256,128]{2,1,0:T(8,128)(2,1)} async-done(((bf16[16,256,128]{2,1,0:T(8,128)(2,1)}), bf16[16,256,128]{2,1,0:T(8,128)(2,1)}, u32[]{:S(2)}, u32[]{:S(2)}) %all-to-all-start.3) | async-done | bytes 1048608 | tf_op jit(solution)/shard_map/all_to_all | solution.py:171
  217.5 1.4 convert_reduce_fusion.1
  219.0 0.8 maximum_bitcast_fusion
  (57 shorter events, 0.9 us)
Async XLA Ops:
  0.0 0.7 copy-start
  0.7 2.8 %copy-start.2 = (bf16[12,512,512]{2,1,0:T(8,128)(2,1)S(1)}, bf16[12,512,512]{2,1,0:T(8,128)(2,1)}, u32[]{:S(2)}) copy-start(bf16[12,512,512]{2,1,0:T(8,128)(2,1)} %img_ref.7) | copy-start | bytes 18874372
  3.5 0.7 copy-start.6
  4.2 0.7 copy-start.8
  4.9 0.7 copy-start.10
  5.5 17.6 %copy-start.12 = (s32[12]{0:T(128)S(1)}, s32[12]{0:T(128)}, u32[]{:S(2)}) copy-start(s32[12]{0:T(128)} %param.11) | copy-start | bytes 148
  5.5 17.6 %copy-start.13 = (s32[12,1]{0,1:T(1,128)S(1)}, s32[12,1]{0,1:T(1,128)}, u32[]{:S(2)}) copy-start(s32[12,1]{0,1:T(1,128)} %param.10) | copy-start | bytes 148
  15.8 27.4 %collective-permute-start.7 = (bf16[12,64,128]{2,1,0:T(8,128)(2,1)S(1)}, bf16[12,64,128]{2,1,0:T(8,128)(2,1)S(1)}, u32[]{:S(2)}, u32[]{:S(2)}) collective-permute-start(bf16[12,64,128]{2,1,0:T(8,128)(2,1)S(1)} %get-tuple-element.46), channel_id=1, source_target_pairs={{0,16},{16,32},{32,48},{48,64},{64,80},{80,96},{96,112},{112,0},{1... | collective-permute-start | bytes 589832 | tf_op jit(solution)/shard_map/ppermute | solution.py:169
  15.8 30.5 %collective-permute-start.8 = (bf16[12,64,128]{2,1,0:T(8,128)(2,1)S(1)}, bf16[12,64,128]{2,1,0:T(8,128)(2,1)S(1)}, u32[]{:S(2)}, u32[]{:S(2)}) collective-permute-start(bf16[12,64,128]{2,1,0:T(8,128)(2,1)S(1)} %get-tuple-element.47), channel_id=1, source_target_pairs={{0,32},{16,48},{32,64},{48,80},{64,96},{80,112},{96,0},{112,16},{1... | collective-permute-start | bytes 589832 | tf_op jit(solution)/shard_map/ppermute | solution.py:169
  17.4 37.8 %collective-permute-start.9 = (bf16[12,64,128]{2,1,0:T(8,128)(2,1)S(1)}, bf16[12,64,128]{2,1,0:T(8,128)(2,1)S(1)}, u32[]{:S(2)}, u32[]{:S(2)}) collective-permute-start(bf16[12,64,128]{2,1,0:T(8,128)(2,1)S(1)} %get-tuple-element.48), channel_id=1, source_target_pairs={{0,48},{16,64},{32,80},{48,96},{64,112},{80,0},{96,16},{112,32},{1... | collective-permute-start | bytes 589832 | tf_op jit(solution)/shard_map/ppermute | solution.py:169
  19.5 35.8 %collective-permute-start.10 = (bf16[12,64,128]{2,1,0:T(8,128)(2,1)S(1)}, bf16[12,64,128]{2,1,0:T(8,128)(2,1)S(1)}, u32[]{:S(2)}, u32[]{:S(2)}) collective-permute-start(bf16[12,64,128]{2,1,0:T(8,128)(2,1)S(1)} %get-tuple-element.49), channel_id=1, source_target_pairs={{0,64},{16,80},{32,96},{48,112},{64,0},{80,16},{96,32},{112,48},{1... | collective-permute-start | bytes 589832 | tf_op jit(solution)/shard_map/ppermute | solution.py:169
  21.5 33.8 %collective-permute-start.11 = (bf16[12,64,128]{2,1,0:T(8,128)(2,1)S(1)}, bf16[12,64,128]{2,1,0:T(8,128)(2,1)S(1)}, u32[]{:S(2)}, u32[]{:S(2)}) collective-permute-start(bf16[12,64,128]{2,1,0:T(8,128)(2,1)S(1)} %get-tuple-element.50), channel_id=1, source_target_pairs={{0,80},{16,96},{32,112},{48,0},{64,16},{80,32},{96,48},{112,64},{1... | collective-permute-start | bytes 589832 | tf_op jit(solution)/shard_map/ppermute | solution.py:169
  43.2 12.1 %collective-permute-start.12 = (bf16[12,64,128]{2,1,0:T(8,128)(2,1)S(1)}, bf16[12,64,128]{2,1,0:T(8,128)(2,1)S(1)}, u32[]{:S(2)}, u32[]{:S(2)}) collective-permute-start(bf16[12,64,128]{2,1,0:T(8,128)(2,1)S(1)} %get-tuple-element.51), channel_id=1, source_target_pairs={{0,96},{16,112},{32,0},{48,16},{64,32},{80,48},{96,64},{112,80},{1... | collective-permute-start | bytes 589832 | tf_op jit(solution)/shard_map/ppermute | solution.py:169
  46.3 9.0 %collective-permute-start.13 = (bf16[12,64,128]{2,1,0:T(8,128)(2,1)S(1)}, bf16[12,64,128]{2,1,0:T(8,128)(2,1)S(1)}, u32[]{:S(2)}, u32[]{:S(2)}) collective-permute-start(bf16[12,64,128]{2,1,0:T(8,128)(2,1)S(1)} %get-tuple-element.52), channel_id=1, source_target_pairs={{0,112},{16,0},{32,16},{48,32},{64,48},{80,64},{96,80},{112,96},{1... | collective-permute-start | bytes 589832 | tf_op jit(solution)/shard_map/ppermute | solution.py:169
  47.2 15.7 %all-to-all-start.1 = ((f32[16,1,256]{2,1,0:T(1,128)}), f32[16,1,256]{2,1,0:T(1,128)S(1)}, u32[]{:S(2)}, u32[]{:S(2)}) async-start(f32[16,1,256]{2,1,0:T(1,128)} %reshape.45), calls=%async_computation.1 | async-start | bytes 32768 | tf_op jit(solution)/shard_map/all_to_all | solution.py:160
  55.3 11.2 %copy-start.1 = (bf16[12,512]{1,0:T(8,128)(2,1)S(1)}, bf16[12,512]{1,0:T(8,128)(2,1)}, u32[]{:S(2)}) copy-start(bf16[12,512]{1,0:T(8,128)(2,1)} %iv_ref.7) | copy-start | bytes 36868
  55.3 11.2 %copy-start.7 = (f32[8,41]{1,0:T(8,128)S(1)}, f32[8,41]{1,0:T(8,128)}, u32[]{:S(2)}) copy-start(f32[8,41]{1,0:T(8,128)} %rtap_ref.7) | copy-start | bytes 3940
  55.3 11.2 %copy-start.9 = (f32[8,41]{1,0:T(8,128)S(1)}, f32[8,41]{1,0:T(8,128)}, u32[]{:S(2)}) copy-start(f32[8,41]{1,0:T(8,128)} %ctap_ref.7) | copy-start | bytes 3940
  55.3 11.2 %copy-start.11 = (s32[12]{0:T(128)S(1)}, s32[12]{0:T(128)}, u32[]{:S(2)}) copy-start(s32[12]{0:T(128)} %kidx_ref.7) | copy-start | bytes 148
  62.8 38.7 %all-to-all-start.2 = ((bf16[16,256,128]{2,1,0:T(8,128)(2,1)}), bf16[16,256,128]{2,1,0:T(8,128)(2,1)S(1)}, u32[]{:S(2)}, u32[]{:S(2)}) async-start(bf16[16,256,128]{2,1,0:T(8,128)(2,1)} %bitcast.5), calls=%async_computation.2 | async-start | bytes 2097152 | tf_op jit(solution)/shard_map/all_to_all | solution.py:171
  66.5 2.8 %copy-start.3 = (bf16[12,512,512]{2,1,0:T(8,128)(2,1)S(1)}, bf16[12,512,512]{2,1,0:T(8,128)(2,1)}, u32[]{:S(2)}) copy-start(bf16[12,512,512]{2,1,0:T(8,128)(2,1)} %img_ref.7) | copy-start | bytes 18874372
  78.1 7.8 %collective-permute-start = (bf16[12,64,128]{2,1,0:T(8,128)(2,1)S(1)}, bf16[12,64,128]{2,1,0:T(8,128)(2,1)S(1)}, u32[]{:S(2)}, u32[]{:S(2)}) collective-permute-start(bf16[12,64,128]{2,1,0:T(8,128)(2,1)S(1)} %get-tuple-element.38), channel_id=1, source_target_pairs={{0,16},{16,32},{32,48},{48,64},{64,80},{80,96},{96,112},{112,0},{1... | collective-permute-start | bytes 589832 | tf_op jit(solution)/shard_map/ppermute | solution.py:169
  78.1 9.0 %collective-permute-start.1 = (bf16[12,64,128]{2,1,0:T(8,128)(2,1)S(1)}, bf16[12,64,128]{2,1,0:T(8,128)(2,1)S(1)}, u32[]{:S(2)}, u32[]{:S(2)}) collective-permute-start(bf16[12,64,128]{2,1,0:T(8,128)(2,1)S(1)} %get-tuple-element.39), channel_id=1, source_target_pairs={{0,32},{16,48},{32,64},{48,80},{64,96},{80,112},{96,0},{112,16},{1... | collective-permute-start | bytes 589832 | tf_op jit(solution)/shard_map/ppermute | solution.py:169
  79.9 13.9 %collective-permute-start.2 = (bf16[12,64,128]{2,1,0:T(8,128)(2,1)S(1)}, bf16[12,64,128]{2,1,0:T(8,128)(2,1)S(1)}, u32[]{:S(2)}, u32[]{:S(2)}) collective-permute-start(bf16[12,64,128]{2,1,0:T(8,128)(2,1)S(1)} %get-tuple-element.40), channel_id=1, source_target_pairs={{0,48},{16,64},{32,80},{48,96},{64,112},{80,0},{96,16},{112,32},{1... | collective-permute-start | bytes 589832 | tf_op jit(solution)/shard_map/ppermute | solution.py:169
  80.0 14.9 %collective-permute-start.3 = (bf16[12,64,128]{2,1,0:T(8,128)(2,1)S(1)}, bf16[12,64,128]{2,1,0:T(8,128)(2,1)S(1)}, u32[]{:S(2)}, u32[]{:S(2)}) collective-permute-start(bf16[12,64,128]{2,1,0:T(8,128)(2,1)S(1)} %get-tuple-element.41), channel_id=1, source_target_pairs={{0,64},{16,80},{32,96},{48,112},{64,0},{80,16},{96,32},{112,48},{1... | collective-permute-start | bytes 589832 | tf_op jit(solution)/shard_map/ppermute | solution.py:169
  83.9 13.2 %collective-permute-start.4 = (bf16[12,64,128]{2,1,0:T(8,128)(2,1)S(1)}, bf16[12,64,128]{2,1,0:T(8,128)(2,1)S(1)}, u32[]{:S(2)}, u32[]{:S(2)}) collective-permute-start(bf16[12,64,128]{2,1,0:T(8,128)(2,1)S(1)} %get-tuple-element.42), channel_id=1, source_target_pairs={{0,80},{16,96},{32,112},{48,0},{64,16},{80,32},{96,48},{112,64},{1... | collective-permute-start | bytes 589832 | tf_op jit(solution)/shard_map/ppermute | solution.py:169
  85.9 12.0 %collective-permute-start.5 = (bf16[12,64,128]{2,1,0:T(8,128)(2,1)S(1)}, bf16[12,64,128]{2,1,0:T(8,128)(2,1)S(1)}, u32[]{:S(2)}, u32[]{:S(2)}) collective-permute-start(bf16[12,64,128]{2,1,0:T(8,128)(2,1)S(1)} %get-tuple-element.43), channel_id=1, source_target_pairs={{0,96},{16,112},{32,0},{48,16},{64,32},{80,48},{96,64},{112,80},{1... | collective-permute-start | bytes 589832 | tf_op jit(solution)/shard_map/ppermute | solution.py:169
  87.1 12.2 %collective-permute-start.6 = (bf16[12,64,128]{2,1,0:T(8,128)(2,1)S(1)}, bf16[12,64,128]{2,1,0:T(8,128)(2,1)S(1)}, u32[]{:S(2)}, u32[]{:S(2)}) collective-permute-start(bf16[12,64,128]{2,1,0:T(8,128)(2,1)S(1)} %get-tuple-element.44), channel_id=1, source_target_pairs={{0,112},{16,0},{32,16},{48,32},{64,48},{80,64},{96,80},{112,96},{1... | collective-permute-start | bytes 589832 | tf_op jit(solution)/shard_map/ppermute | solution.py:169
  101.6 45.6 %all-to-all-start = ((bf16[16,256,128]{2,1,0:T(8,128)(2,1)}), bf16[16,256,128]{2,1,0:T(8,128)(2,1)S(1)}, u32[]{:S(2)}, u32[]{:S(2)}) async-start(bf16[16,256,128]{2,1,0:T(8,128)(2,1)} %bitcast.2), calls=%async_computation | async-start | bytes 2097152 | tf_op jit(solution)/shard_map/all_to_all | solution.py:171
  108.7 2.8 %copy-start.4 = (bf16[12,512,512]{2,1,0:T(8,128)(2,1)S(1)}, bf16[12,512,512]{2,1,0:T(8,128)(2,1)}, u32[]{:S(2)}) copy-start(bf16[12,512,512]{2,1,0:T(8,128)(2,1)} %img_ref.7) | copy-start | bytes 18874372
  120.3 8.0 %collective-permute-start.21 = (bf16[12,64,128]{2,1,0:T(8,128)(2,1)S(1)}, bf16[12,64,128]{2,1,0:T(8,128)(2,1)S(1)}, u32[]{:S(2)}, u32[]{:S(2)}) collective-permute-start(bf16[12,64,128]{2,1,0:T(8,128)(2,1)S(1)} %get-tuple-element.62), channel_id=1, source_target_pairs={{0,16},{16,32},{32,48},{48,64},{64,80},{80,96},{96,112},{112,0},{1... | collective-permute-start | bytes 589832 | tf_op jit(solution)/shard_map/ppermute | solution.py:169
  124.2 16.6 %collective-permute-start.22 = (bf16[12,64,128]{2,1,0:T(8,128)(2,1)S(1)}, bf16[12,64,128]{2,1,0:T(8,128)(2,1)S(1)}, u32[]{:S(2)}, u32[]{:S(2)}) collective-permute-start(bf16[12,64,128]{2,1,0:T(8,128)(2,1)S(1)} %get-tuple-element.63), channel_id=1, source_target_pairs={{0,32},{16,48},{32,64},{48,80},{64,96},{80,112},{96,0},{112,16},{1... | collective-permute-start | bytes 589832 | tf_op jit(solution)/shard_map/ppermute | solution.py:169
  124.3 16.5 %collective-permute-start.23 = (bf16[12,64,128]{2,1,0:T(8,128)(2,1)S(1)}, bf16[12,64,128]{2,1,0:T(8,128)(2,1)S(1)}, u32[]{:S(2)}, u32[]{:S(2)}) collective-permute-start(bf16[12,64,128]{2,1,0:T(8,128)(2,1)S(1)} %get-tuple-element.64), channel_id=1, source_target_pairs={{0,48},{16,64},{32,80},{48,96},{64,112},{80,0},{96,16},{112,32},{1... | collective-permute-start | bytes 589832 | tf_op jit(solution)/shard_map/ppermute | solution.py:169
  124.3 16.5 %collective-permute-start.24 = (bf16[12,64,128]{2,1,0:T(8,128)(2,1)S(1)}, bf16[12,64,128]{2,1,0:T(8,128)(2,1)S(1)}, u32[]{:S(2)}, u32[]{:S(2)}) collective-permute-start(bf16[12,64,128]{2,1,0:T(8,128)(2,1)S(1)} %get-tuple-element.65), channel_id=1, source_target_pairs={{0,64},{16,80},{32,96},{48,112},{64,0},{80,16},{96,32},{112,48},{1... | collective-permute-start | bytes 589832 | tf_op jit(solution)/shard_map/ppermute | solution.py:169
  128.3 13.2 %collective-permute-start.25 = (bf16[12,64,128]{2,1,0:T(8,128)(2,1)S(1)}, bf16[12,64,128]{2,1,0:T(8,128)(2,1)S(1)}, u32[]{:S(2)}, u32[]{:S(2)}) collective-permute-start(bf16[12,64,128]{2,1,0:T(8,128)(2,1)S(1)} %get-tuple-element.66), channel_id=1, source_target_pairs={{0,80},{16,96},{32,112},{48,0},{64,16},{80,32},{96,48},{112,64},{1... | collective-permute-start | bytes 589832 | tf_op jit(solution)/shard_map/ppermute | solution.py:169
  128.3 14.1 %collective-permute-start.26 = (bf16[12,64,128]{2,1,0:T(8,128)(2,1)S(1)}, bf16[12,64,128]{2,1,0:T(8,128)(2,1)S(1)}, u32[]{:S(2)}, u32[]{:S(2)}) collective-permute-start(bf16[12,64,128]{2,1,0:T(8,128)(2,1)S(1)} %get-tuple-element.67), channel_id=1, source_target_pairs={{0,96},{16,112},{32,0},{48,16},{64,32},{80,48},{96,64},{112,80},{1... | collective-permute-start | bytes 589832 | tf_op jit(solution)/shard_map/ppermute | solution.py:169
  140.8 4.1 %collective-permute-start.27 = (bf16[12,64,128]{2,1,0:T(8,128)(2,1)S(1)}, bf16[12,64,128]{2,1,0:T(8,128)(2,1)S(1)}, u32[]{:S(2)}, u32[]{:S(2)}) collective-permute-start(bf16[12,64,128]{2,1,0:T(8,128)(2,1)S(1)} %get-tuple-element.68), channel_id=1, source_target_pairs={{0,112},{16,0},{32,16},{48,32},{64,48},{80,64},{96,80},{112,96},{1... | collective-permute-start | bytes 589832 | tf_op jit(solution)/shard_map/ppermute | solution.py:169
  147.2 44.0 %all-to-all-start.4 = ((bf16[16,256,128]{2,1,0:T(8,128)(2,1)}), bf16[16,256,128]{2,1,0:T(8,128)(2,1)}, u32[]{:S(2)}, u32[]{:S(2)}) async-start(bf16[16,256,128]{2,1,0:T(8,128)(2,1)} %bitcast.9), calls=%async_computation.4 | async-start | bytes 2097152 | tf_op jit(solution)/shard_map/all_to_all | solution.py:171
  154.4 2.8 %copy-start.5 = (bf16[12,512,512]{2,1,0:T(8,128)(2,1)S(1)}, bf16[12,512,512]{2,1,0:T(8,128)(2,1)}, u32[]{:S(2)}) copy-start(bf16[12,512,512]{2,1,0:T(8,128)(2,1)} %img_ref.7) | copy-start | bytes 18874372
  167.4 7.7 %collective-permute-start.14 = (bf16[12,64,128]{2,1,0:T(8,128)(2,1)S(1)}, bf16[12,64,128]{2,1,0:T(8,128)(2,1)S(1)}, u32[]{:S(2)}, u32[]{:S(2)}) collective-permute-start(bf16[12,64,128]{2,1,0:T(8,128)(2,1)S(1)} %get-tuple-element.54), channel_id=1, source_target_pairs={{0,16},{16,32},{32,48},{48,64},{64,80},{80,96},{96,112},{112,0},{1... | collective-permute-start | bytes 589832 | tf_op jit(solution)/shard_map/ppermute | solution.py:169
  168.0 9.8 %collective-permute-start.15 = (bf16[12,64,128]{2,1,0:T(8,128)(2,1)S(1)}, bf16[12,64,128]{2,1,0:T(8,128)(2,1)S(1)}, u32[]{:S(2)}, u32[]{:S(2)}) collective-permute-start(bf16[12,64,128]{2,1,0:T(8,128)(2,1)S(1)} %get-tuple-element.55), channel_id=1, source_target_pairs={{0,32},{16,48},{32,64},{48,80},{64,96},{80,112},{96,0},{112,16},{1... | collective-permute-start | bytes 589832 | tf_op jit(solution)/shard_map/ppermute | solution.py:169
  168.1 12.3 %collective-permute-start.16 = (bf16[12,64,128]{2,1,0:T(8,128)(2,1)S(1)}, bf16[12,64,128]{2,1,0:T(8,128)(2,1)S(1)}, u32[]{:S(2)}, u32[]{:S(2)}) collective-permute-start(bf16[12,64,128]{2,1,0:T(8,128)(2,1)S(1)} %get-tuple-element.56), channel_id=1, source_target_pairs={{0,48},{16,64},{32,80},{48,96},{64,112},{80,0},{96,16},{112,32},{1... | collective-permute-start | bytes 589832 | tf_op jit(solution)/shard_map/ppermute | solution.py:169
  168.1 17.4 %collective-permute-start.17 = (bf16[12,64,128]{2,1,0:T(8,128)(2,1)S(1)}, bf16[12,64,128]{2,1,0:T(8,128)(2,1)S(1)}, u32[]{:S(2)}, u32[]{:S(2)}) collective-permute-start(bf16[12,64,128]{2,1,0:T(8,128)(2,1)S(1)} %get-tuple-element.57), channel_id=1, source_target_pairs={{0,64},{16,80},{32,96},{48,112},{64,0},{80,16},{96,32},{112,48},{1... | collective-permute-start | bytes 589832 | tf_op jit(solution)/shard_map/ppermute | solution.py:169
  172.1 13.4 %collective-permute-start.18 = (bf16[12,64,128]{2,1,0:T(8,128)(2,1)S(1)}, bf16[12,64,128]{2,1,0:T(8,128)(2,1)S(1)}, u32[]{:S(2)}, u32[]{:S(2)}) collective-permute-start(bf16[12,64,128]{2,1,0:T(8,128)(2,1)S(1)} %get-tuple-element.58), channel_id=1, source_target_pairs={{0,80},{16,96},{32,112},{48,0},{64,16},{80,32},{96,48},{112,64},{1... | collective-permute-start | bytes 589832 | tf_op jit(solution)/shard_map/ppermute | solution.py:169
  175.1 11.2 %collective-permute-start.19 = (bf16[12,64,128]{2,1,0:T(8,128)(2,1)S(1)}, bf16[12,64,128]{2,1,0:T(8,128)(2,1)S(1)}, u32[]{:S(2)}, u32[]{:S(2)}) collective-permute-start(bf16[12,64,128]{2,1,0:T(8,128)(2,1)S(1)} %get-tuple-element.59), channel_id=1, source_target_pairs={{0,96},{16,112},{32,0},{48,16},{64,32},{80,48},{96,64},{112,80},{1... | collective-permute-start | bytes 589832 | tf_op jit(solution)/shard_map/ppermute | solution.py:169
  177.8 11.0 %collective-permute-start.20 = (bf16[12,64,128]{2,1,0:T(8,128)(2,1)S(1)}, bf16[12,64,128]{2,1,0:T(8,128)(2,1)S(1)}, u32[]{:S(2)}, u32[]{:S(2)}) collective-permute-start(bf16[12,64,128]{2,1,0:T(8,128)(2,1)S(1)} %get-tuple-element.60), channel_id=1, source_target_pairs={{0,112},{16,0},{32,16},{48,32},{64,48},{80,64},{96,80},{112,96},{1... | collective-permute-start | bytes 589832 | tf_op jit(solution)/shard_map/ppermute | solution.py:169
  191.1 26.3 %all-to-all-start.3 = ((bf16[16,256,128]{2,1,0:T(8,128)(2,1)}), bf16[16,256,128]{2,1,0:T(8,128)(2,1)}, u32[]{:S(2)}, u32[]{:S(2)}) async-start(bf16[16,256,128]{2,1,0:T(8,128)(2,1)} %bitcast.7), calls=%async_computation.3 | async-start | bytes 2097152 | tf_op jit(solution)/shard_map/all_to_all | solution.py:171

commit v2 on v0

v2 whole, which is shorter than its diff:
```python
import functools

import jax
import jax.numpy as jnp
import numpy as np
from jax import lax
from jax.experimental import pallas as pl
from jax.experimental.pallas import tpu as pltpu
from jax.sharding import Mesh, PartitionSpec as P

NB = 8
POS = 4
LANE = 128
BF = jnp.bfloat16
F32 = jnp.float32
NX, NC, NY, NZ = 4, 2, 4, 4
VISITS, TILES = NX * NC, NY * NZ
COUNT = TILES * POS
SUB = 16
VMEM_BIG = 60 << 20
Y_OFFSETS = tuple((dc, dy) for dc in range(NC) for dy in range(NY))


def toeplitz(row, length):
    wide = jnp.broadcast_to(row, (LANE, length))
    return pltpu.roll(wide, 0, 1, stride=1, stride_axis=0)


def band_blocks(table, taps_ref):
    count = taps_ref.shape[1]
    half = (count - 1) // 2
    length = 3 * LANE
    q = lax.broadcasted_iota(jnp.int32, (count, length), 0)
    n = lax.broadcasted_iota(jnp.int32, (count, length), 1)
    pick = (n + q == LANE + half).astype(F32).astype(BF)
    base = jnp.dot(taps_ref[...].astype(BF), pick, preferred_element_type=F32)
    for k in range(NB):
        table[k] = toeplitz(base[k : k + 1], length).astype(BF)


def put_band(band, block, first, tiles):
    for a in range(band.shape[0] // LANE):
        at = first + a
        lo, hi = max(at - 1, 0), min(at + 2, tiles)
        off = (lo - (at - 1)) * LANE
        band[a * LANE : (a + 1) * LANE, lo * LANE : hi * LANE] = block[:, off : off + (hi - lo) * LANE]


def column_pass(b, h, mid, cband, iv_ref):
    blocks, side = iv_ref.shape
    width = side // 2
    onehot = (lax.broadcasted_iota(jnp.int32, (blocks, LANE), 0) == b).astype(F32).astype(BF)
    weight = lax.dot_general(iv_ref[...], onehot, (((0,), (0,)), ((), ())), preferred_element_type=F32)
    weight = jnp.concatenate([weight] * (width // LANE), axis=1)
    lo, hi = (0, 3 * LANE) if h == 0 else (side - 3 * LANE, side)
    matched = lax.dot_general(
        mid[:, lo:hi], cband[:, lo:hi], (((1,), (1,)), ((), ())), preferred_element_type=F32
    )
    return (matched * weight).astype(BF)


def combo_rows(dest_ref, pos_ref, blocks):
    row = lax.broadcasted_iota(jnp.int32, (SUB, LANE), 0)
    places = jnp.full((SUB, LANE), COUNT, jnp.int32)
    for b in range(blocks):
        places = jnp.where(row == b, dest_ref[b] * POS + pos_ref[b], places)
    return places.astype(F32).astype(BF)


def first_kernel(kidx_ref, dest_ref, pos_ref, rtap_ref, ctap_ref, img_ref, iv_ref, mid_ref, *rest):
    y_refs, (rtab, ctab, rband, cband, whole) = rest[:-5], rest[-5:]
    b = pl.program_id(0)
    blocks, side = iv_ref.shape
    tiles, rows = side // LANE, side // VISITS

    @pl.when(b == 0)
    def _():
        band_blocks(rtab, rtap_ref)
        band_blocks(ctab, ctap_ref)
        rband[...] = jnp.zeros_like(rband)
        cband[...] = jnp.zeros_like(cband)
        places = combo_rows(dest_ref, pos_ref, blocks)
        for ref in y_refs:
            ref[blocks * rows :, LANE:] = places
            ref[blocks * rows :, :LANE] = places

    k = kidx_ref[b]
    put_band(rband, rtab.at[k], 0, tiles)
    put_band(cband, ctab.at[k], tiles // 2, tiles)
    mid = jnp.dot(rband[...], img_ref[0], preferred_element_type=F32).astype(BF)
    mid_ref[0] = mid
    whole[...] = column_pass(b, 1, mid, cband, iv_ref)
    mc, my = lax.axis_index("core"), lax.axis_index("y")
    for i, (dc, dy) in enumerate(Y_OFFSETS):
        core, sub = lax.rem(mc + dc, NC), lax.rem(my + dy, NY)
        for x in range(NX):
            start = pl.multiple_of((x * NC + core) * rows + sub * SUB, SUB)
            to = pl.multiple_of(b * rows + x * SUB, SUB)
            y_refs[i][pl.ds(to, SUB), :] = whole[pl.ds(start, SUB), :]


def second_kernel(kidx_ref, dest_ref, pos_ref, ctap_ref, mid_ref, iv_ref, x_ref, ctab, cband):
    b = pl.program_id(0)
    blocks, side = iv_ref.shape
    tiles, rows = side // LANE, side // VISITS

    @pl.when(b == 0)
    def _():
        band_blocks(ctab, ctap_ref)
        cband[...] = jnp.zeros_like(cband)
        places = combo_rows(dest_ref, pos_ref, blocks)
        weights = jnp.concatenate([iv_ref[...].astype(F32), jnp.zeros((SUB - blocks, side), F32)], axis=0)
        for v in range(VISITS):
            part = weights[:, (v // 2) * LANE : (v // 2 + 1) * LANE]
            if v % 2:
                part = pltpu.roll(part, rows, 1)
            x_ref[v, blocks * rows :, :LANE] = part.astype(BF)
            x_ref[v, blocks * rows :, LANE:] = places

    put_band(cband, ctab.at[kidx_ref[b]], 0, tiles)
    weighted = column_pass(b, 0, mid_ref[0], cband, iv_ref)
    at = pl.ds(pl.multiple_of(b * rows, rows), rows)
    for v in range(VISITS):
        x_ref[v, at, :] = weighted[v * rows : (v + 1) * rows]


def match(kidx, dest, position, row_taps, col_taps, image, inv_var):
    blocks, side, _ = image.shape
    rows, width = side // VISITS, side // 2
    tall = blocks * rows + SUB
    full = lambda shape: pl.BlockSpec(shape, lambda b, *_: (0,) * len(shape))
    block = pl.BlockSpec((1, side, side), lambda b, *_: (b, 0, 0))
    table, half_band = pltpu.VMEM((NB, LANE, 3 * LANE), BF), pltpu.VMEM((width, side), BF)
    shape = jax.ShapeDtypeStruct
    params = pltpu.CompilerParams(vmem_limit_bytes=VMEM_BIG)
    mid, *y_parts = pl.pallas_call(
        first_kernel,
        grid_spec=pltpu.PrefetchScalarGridSpec(
            num_scalar_prefetch=3,
            grid=(blocks,),
            in_specs=[full(row_taps.shape), full(col_taps.shape), block, full(inv_var.shape)],
            out_specs=[block] + [full((tall, width))] * len(Y_OFFSETS),
            scratch_shapes=[table, table, pltpu.VMEM((side, side), BF), half_band, pltpu.VMEM((side, width), BF)],
        ),
        out_shape=[shape(image.shape, BF)] + [shape((tall, width), BF)] * len(Y_OFFSETS),
        compiler_params=params,
        cost_estimate=pl.CostEstimate(
            flops=3 * blocks * side**3, bytes_accessed=image.size * 5, transcendentals=0
        ),
        name="match_first",
    )(kidx, dest, position, row_taps, col_taps, image, inv_var)
    x_part = pl.pallas_call(
        second_kernel,
        grid_spec=pltpu.PrefetchScalarGridSpec(
            num_scalar_prefetch=3,
            grid=(blocks,),
            in_specs=[full(col_taps.shape), block, full(inv_var.shape)],
            out_specs=full((VISITS, tall, width)),
            scratch_shapes=[table, half_band],
        ),
        out_shape=shape((VISITS, tall, width), BF),
        compiler_params=params,
        cost_estimate=pl.CostEstimate(
            flops=blocks * side**3, bytes_accessed=image.size * 3, transcendentals=0
        ),
        name="match_second",
    )(kidx, dest, position, col_taps, mid, inv_var)
    return x_part, y_parts


def read_places(notes, flat, smem, sem):
    places = jnp.concatenate([n.astype(F32) for n in notes], axis=0)
    size = VISITS * SUB
    row = lax.broadcasted_iota(jnp.int32, (size, LANE), 0)
    lane = lax.broadcasted_iota(jnp.int32, (size, LANE), 1)
    line = jnp.sum(jnp.where(row == lane, places, 0.0), axis=0, keepdims=True)
    flat[...] = line.astype(jnp.int32)
    copy = pltpu.make_async_copy(flat, smem, sem)
    copy.start()
    copy.wait()
    return line


def gather_x_kernel(in_ref, after_ref, out_ref, acc, flat, smem, sem):
    rows, width = acc.shape[1:]
    blocks = (in_ref.shape[1] - SUB) // rows
    top = blocks * rows
    line = read_places([in_ref[v, top:, LANE:] for v in range(VISITS)], flat, smem, sem)
    acc[...] = jnp.zeros_like(acc)
    for v in range(VISITS):
        for b in range(blocks):
            acc[smem[0, v * SUB + b]] += in_ref[v, b * rows : (b + 1) * rows].astype(F32)
    place = lax.broadcasted_iota(jnp.int32, (COUNT, LANE), 0)
    hit = (place == line.astype(jnp.int32)).astype(F32).astype(BF)
    weights = jnp.concatenate([in_ref[v, top:, :LANE].astype(F32) for v in range(VISITS)], axis=0).astype(BF)
    den = jnp.dot(hit, weights, preferred_element_type=F32)
    high = den.astype(BF).astype(F32)
    both = jnp.concatenate([high, den - high], axis=1)
    for t in range(TILES):
        for p in range(POS):
            out_ref[t, p * rows : (p + 1) * rows] = acc[t * POS + p].astype(BF)
        pad = jnp.zeros((SUB - POS, width), F32)
        out_ref[t, POS * rows :] = jnp.concatenate([both[t * POS : (t + 1) * POS], pad], axis=0).astype(BF)


def gather_y_kernel(*rest):
    n = len(Y_OFFSETS)
    pieces, outs, (acc, flat, smem, sem) = rest[:n], rest[n:-4], rest[-4:]
    rows = acc.shape[1]
    blocks = (pieces[0].shape[0] - SUB) // rows
    mx = lax.axis_index("x")
    read_places([r[blocks * rows :, LANE:] for r in pieces], flat, smem, sem)
    acc[...] = jnp.zeros_like(acc)
    for i in range(n):
        for b in range(blocks):
            acc[smem[0, i * SUB + b]] += pieces[i][b * rows : (b + 1) * rows].astype(F32)
    for i in range(NX):
        to = pl.multiple_of(lax.rem(mx + i, NX) * SUB, SUB)
        outs[i][...] = acc[:, pl.ds(to, SUB), :].astype(BF)


def vmem_call(kernel, name, out_shape, args, scratch=(), after=0):
    vm = pl.BlockSpec(memory_space=pltpu.VMEM)
    anywhere = pl.BlockSpec(memory_space=pl.ANY)
    size = sum(a.size * a.dtype.itemsize for a in args)
    return pl.pallas_call(
        kernel,
        in_specs=[vm] * (len(args) - after) + [anywhere] * after,
        out_specs=jax.tree.map(lambda _: vm, out_shape),
        out_shape=out_shape,
        scratch_shapes=list(scratch),
        compiler_params=pltpu.CompilerParams(vmem_limit_bytes=32 << 20),
        cost_estimate=pl.CostEstimate(flops=size, bytes_accessed=2 * size, transcendentals=0),
        name=name,
    )(*args)


def ring_z_kernel(*refs):
    ins, outs = refs[:NX], refs[NX + 1 :]
    mz = lax.axis_index("z")
    for i in range(NZ):
        for y in range(NY):
            at = pl.ds((y * NZ + lax.rem(mz + i, NZ)) * POS, POS)
            outs[i][y] = sum(r[at].astype(F32) for r in ins).astype(BF)


def ring_y_kernel(*refs):
    ins, outs = refs[:NZ], refs[NZ:]
    my = lax.axis_index("y")
    for i in range(NY):
        at = lax.rem(my + i, NY)
        outs[i][...] = sum(r[at].astype(F32) for r in ins)


def finish_kernel(x_ref, *rest):
    y_refs, out_ref, inv = rest[:-2], rest[-2], rest[-1]
    rows = out_ref.shape[1]
    width = x_ref.shape[2]
    my = lax.axis_index("y")
    notes = sum(x_ref[s, POS * rows :].astype(F32) for s in range(TILES))
    den = 1.0 / jnp.maximum(notes[:, :LANE] + notes[:, LANE:], 1.0)
    for p in range(POS):
        turned = jnp.transpose(jnp.broadcast_to(den[p : p + 1], (LANE, LANE)))[:rows]
        inv[p] = turned
        total = x_ref[0, p * rows : (p + 1) * rows].astype(F32)
        for s in range(1, TILES):
            total += x_ref[s, p * rows : (p + 1) * rows].astype(F32)
        for j in range(width // LANE):
            out_ref[p, :, j * LANE : (j + 1) * LANE] = total[:, j * LANE : (j + 1) * LANE] * turned
    for i in range(NY):
        at = pl.ds(pl.multiple_of(lax.rem(my - i + NY, NY) * SUB, SUB), SUB)
        for p in range(POS):
            scale = inv[p, at, :]
            for j in range(width // LANE):
                lanes = slice(width + j * LANE, width + (j + 1) * LANE)
                out_ref[p, at, lanes] = y_refs[i][p, :, j * LANE : (j + 1) * LANE] * scale


def ring(pieces, axis, size):
    out = [pieces[0]]
    for i in range(1, size):
        out.append(lax.ppermute(pieces[i], axis, [(s, (s + i) % size) for s in range(size)]))
    return out


def per_device(image, inv_var, kernel_index, dest, position, row_taps, col_taps):
    _, side, _ = image.shape
    rows, width = side // VISITS, side // 2
    shape = jax.ShapeDtypeStruct
    x_part, y_parts = match(kernel_index, dest[:, 0], position, row_taps, col_taps, image, inv_var)

    arrived = [y_parts[0]]
    for i in range(1, len(Y_OFFSETS)):
        dc, dy = Y_OFFSETS[i]
        perm = [
            (c * NY + y, ((c + dc) % NC) * NY + (y + dy) % NY) for c in range(NC) for y in range(NY)
        ]
        arrived.append(lax.ppermute(y_parts[i], ("core", "y"), perm))
    x_in = lax.all_to_all(x_part, ("x", "core"), 0, 0, tiled=True)

    scratch = [
        pltpu.VMEM((COUNT, rows, width), F32),
        pltpu.VMEM((1, LANE), jnp.int32),
        pltpu.SMEM((1, LANE), jnp.int32),
        pltpu.SemaphoreType.DMA,
    ]
    mine = vmem_call(gather_y_kernel, "gather_y", [shape((COUNT, SUB, width), BF)] * NX, arrived, scratch)
    along_x = ring(mine, "x", NX)
    x_sum = vmem_call(
        gather_x_kernel, "gather_x", shape((TILES, POS * rows + SUB, width), BF), (x_in, mine[0]), scratch, 1
    )
    x_out = lax.all_to_all(x_sum, ("y", "z"), 0, 0, tiled=True)
    along_z = vmem_call(
        ring_z_kernel, "ring_z", [shape((NY, POS, SUB, width), BF)] * NZ, (*along_x, x_sum), after=1
    )
    along_z = ring(along_z, "z", NZ)
    along_y = vmem_call(ring_y_kernel, "ring_y", [shape((POS, SUB, width), F32)] * NY, along_z)
    along_y = ring(along_y, "y", NY)
    out = vmem_call(
        finish_kernel,
        "finish",
        shape((POS, rows, side), F32),
        (x_out, *along_y),
        [pltpu.VMEM((POS, rows, LANE), F32)],
    )
    return out[None]


def solution(mesh):
    mesh = Mesh(mesh.devices.reshape(NX, NC, NY, NZ), ("x", "core", "y", "z"))
    every = ("x", "core", "y", "z")
    in_specs = (P(every, None, None), P(every, None), P(every), P(every, None), P(every), P(), P())
    out_specs = P(("y", "z"), None, ("x", "core"), None)
    return jax.shard_map(
        per_device, mesh=mesh, in_specs=in_specs, out_specs=out_specs, check_vma=False
    )
```

time: 596 us -> 138 us (0.23); the launches traced: 587 us -> 136 us
  local copies, waits for them, and re-layouts: 188 us -> 5.21 us
  matrix products: 138 us -> 0 us
  waiting for transfers between devices: 188 us -> 60 us
  Pallas kernels: 0 us -> 34.3 us
  other arithmetic: 21.6 us -> 0 us
  between operations: 14.4 us -> 0.08 us
    dot_general x10 -> x0, matrix products: 138 us -> none  [the longest x1 39.3 us: weigh_sum(): jnp.einsum('snp,snrc->nprc', table_f, weighted, precision=lax.Precision.H...]
    all_to_all x4 -> x2, waiting for transfers between devices: 112 us -> 0.01 us  [the longest x1 0.01 us: per_device(): x_in = lax.all_to_all(x_part, ('x', 'core'), 0, 0, tiled=True)]
    unnamed x23 -> x16, local copies, waits for them, and re-layouts: 87 us -> 5.21 us
    unnamed x4 -> x0, waiting for transfers between devices: 75.6 us -> none
    ppermute x0 -> x16, waiting for transfers between devices: none -> 60 us  [the longest x7 31.9 us: per_device(): arrived.append(lax.ppermute(y_parts[i], ('core', 'y'), perm))]
    another operation x4 -> x0, local copies, waits for them, and re-layouts: 39.8 us -> none  [band_tables(): repeated = jnp.tile(flipped, (1, side_len))]
    pallas_call x0 -> x7, Pallas kernels: none -> 34.3 us  [the longest x1 15.6 us: match(): pl.pallas_call(first_kernel, grid_spec=pltpu.PrefetchScalarGridSpec(num_s...]
    reshape x3 -> x0, local copies, waits for them, and re-layouts: 33.7 us -> none  [the longest x2 33 us: band_tables(): return window.reshape(kernel_count, side_len, span - 1)[:, :, :side_len]]
  transfers between devices with their start and end apart: 6 -> 18, of which waited for: 3 -> 11; matrix products, arithmetic and copies ran while one was open for 58% -> 0% of each run, Pallas kernels for 0% -> 2%
where the time goes in v2:
time: 138 us; the launch traced here: 136 us
  waiting for transfers between devices  60 us (43%)
  starting transfers between devices  36.9 us (27%)
  Pallas kernels  34.3 us (25%)
  local copies, waits for them, and re-layouts  5.21 us (4%)
    ppermute x7, waiting for transfers between devices, per_device(): arrived.append(lax.ppermute(y_parts[i], ('core', 'y'), perm))  31.9 us
    ppermute x9, waiting for transfers between devices, ring(): lax.ppermute(pieces[i], axis, [(s, (s + i) % size) for s in range(size)])  28.1 us
    ppermute x9, starting transfers between devices, ring(): lax.ppermute(pieces[i], axis, [(s, (s + i) % size) for s in range(size)])  16.7 us
    pallas_call x1, Pallas kernels, match(): pl.pallas_call(first_kernel, grid_spec=pltpu.PrefetchScalarGridSpec(num_s...  15.6 us
    pallas_call x1, Pallas kernels, match(): pl.pallas_call(second_kernel, grid_spec=pltpu.PrefetchScalarGridSpec(num_...  12.1 us
    all_to_all x1, starting transfers between devices, per_device(): x_out = lax.all_to_all(x_sum, ('y', 'z'), 0, 0, tiled=True)  7.95 us
    ppermute x7, starting transfers between devices, per_device(): arrived.append(lax.ppermute(y_parts[i], ('core', 'y'), perm))  7.9 us
    pallas_call x5, Pallas kernels, vmem_call(): pl.pallas_call(kernel, in_specs=[vm] * (len(args) - after) + [anywhere] *...  6.57 us
  transfers between devices with their start and end apart: 18, of which 11 were waited for; matrix products, arithmetic and copies ran while one was open for 0% of the time, Pallas kernels for 2%

profile of v2, /device:TPU:0, one launch (start us, length us, event | category | flops | bytes accessed | tf_op | source)
XLA Modules:
  0.0 136.5 jit_solution(11368236860752652071)
XLA Ops:
  0.0 15.6 %match_first.1 = (bf16[12,512,512]{2,1,0:T(8,128)(2,1)}, bf16[784,256]{1,0:T(8,128)(2,1)}, bf16[784,256]{1,0:T(8,128)(2,1)}, bf16[784,256]{1,0:T(8,128)(2,1)}, b...) custom-call(s32[12]{0:T(128)} %kidx_ref.3, ...), custom_call_target="tpu_custom_call" | custom-call | flops 4831838208 | bytes 15728640 | tf_op jit(solution)/shard_map/match_first/pallas_call | solution.py:136
  15.6 12.1 %match_second.1 = bf16[8,784,256]{2,1,0:T(8,128)(2,1)} custom-call(s32[12]{0:T(128)} %kidx_ref.3, s32[12]{0:T(128)} %bitcast.3, s32[12]{0:T(128)} %pos_ref.3, f32[8,41]{1,0:T(8,128)} %ctap_ref.3, bf16[12,512,512]{2,1,0:T(8,128)(2,1)} %get-tuple-element.26.mid_ref, bf16[12,512]{1,0:T(8,128)(2,1)} %iv_ref.3), custom_call_target="tpu_custom_call" | custom-call | flops 1610612736 | bytes 9437184 | tf_op jit(solution)/shard_map/match_second/pallas_call | solution.py:152
  27.7 4.4 %all-to-all-start = ((bf16[8,784,256]{2,1,0:T(8,128)(2,1)}), bf16[8,784,256]{2,1,0:T(8,128)(2,1)S(1)}, u32[]{:S(2)}, u32[]{:S(2)}) async-start(bf16[8,784,256]{2,1,0:T(8,128)(2,1)} %match_second.1), calls=%async_computation | async-start | bytes 6422528 | tf_op jit(solution)/shard_map/all_to_all | solution.py:299
  32.1 1.6 %collective-permute-start = (bf16[784,256]{1,0:T(8,128)(2,1)}, bf16[784,256]{1,0:T(8,128)(2,1)S(1)}, u32[]{:S(2)}, u32[]{:S(2)}) collective-permute-start(bf16[784,256]{1,0:T(8,128)(2,1)} %get-tuple-element.28), channel_id=1, source_target_pairs={{0,4},{4,8},{8,12},{12,0},{16,20},{20,24},{24,28},{28,16},{1,5},{5... | collective-permute-start | bytes 1204232 | tf_op jit(solution)/shard_map/ppermute | solution.py:298
  33.7 2.9 %collective-permute-start.1 = (bf16[784,256]{1,0:T(8,128)(2,1)}, bf16[784,256]{1,0:T(8,128)(2,1)S(1)}, u32[]{:S(2)}, u32[]{:S(2)}) collective-permute-start(bf16[784,256]{1,0:T(8,128)(2,1)} %get-tuple-element.29), channel_id=1, source_target_pairs={{0,8},{4,12},{8,0},{12,4},{16,24},{20,28},{24,16},{28,20},{1,9},{5... | collective-permute-start | bytes 1204232 | tf_op jit(solution)/shard_map/ppermute | solution.py:298
  36.6 1.3 collective-permute-start.2
  37.9 0.0 collective-permute-start.3
  37.9 0.8 collective-permute-start.4
  38.7 6.9 %collective-permute-done.rest_1_ = bf16[784,256]{1,0:T(8,128)(2,1)S(1)} collective-permute-done((bf16[784,256]{1,0:T(8,128)(2,1)}, bf16[784,256]{1,0:T(8,128)(2,1)S(1)}, u32[]{:S(2)}, u32[]{:S(2)}) %collective-permute-start) | collective-permute-done | bytes 401440 | tf_op jit(solution)/shard_map/ppermute | solution.py:298
  45.6 1.0 collective-permute-start.5
  46.6 8.9 %collective-permute-done.1.rest_2_ = bf16[784,256]{1,0:T(8,128)(2,1)S(1)} collective-permute-done((bf16[784,256]{1,0:T(8,128)(2,1)}, bf16[784,256]{1,0:T(8,128)(2,1)S(1)}, u32[]{:S(2)}, u32[]{:S(2)}) %collective-permute-start.1) | collective-permute-done | bytes 401440 | tf_op jit(solution)/shard_map/ppermute | solution.py:298
  55.5 0.2 collective-permute-start.6
  55.7 0.0 collective-permute-done.2.rest_3_
  55.7 0.0 collective-permute-done.3.rest_4_
  55.8 6.4 %collective-permute-done.4.rest_5_ = bf16[784,256]{1,0:T(8,128)(2,1)S(1)} collective-permute-done((bf16[784,256]{1,0:T(8,128)(2,1)}, bf16[784,256]{1,0:T(8,128)(2,1)S(1)}, u32[]{:S(2)}, u32[]{:S(2)}) %collective-permute-start.4) | collective-permute-done | bytes 401440 | tf_op jit(solution)/shard_map/ppermute | solution.py:298
  62.2 9.8 %collective-permute-done.5.rest_6_ = bf16[784,256]{1,0:T(8,128)(2,1)S(1)} collective-permute-done((bf16[784,256]{1,0:T(8,128)(2,1)}, bf16[784,256]{1,0:T(8,128)(2,1)S(1)}, u32[]{:S(2)}, u32[]{:S(2)}) %collective-permute-start.5) | collective-permute-done | bytes 401440 | tf_op jit(solution)/shard_map/ppermute | solution.py:298
  71.9 0.0 collective-permute-done.6.rest_7_
  71.9 0.0 copy-start.3
  71.9 1.0 copy-done.3
  72.9 1.8 %gather_y.1 = (bf16[64,16,256]{2,1,0:T(8,128)(2,1)S(1)}, bf16[64,16,256]{2,1,0:T(8,128)(2,1)S(1)}, bf16[64,16,256]{2,1,0:T(8,128)(2,1)S(1)}, bf16[64,16,256]{2,1,0:T(8,128)(2,1)S(1)}) custom-call(bf16[784,256]{1,0:T(8,128)(2,1)S(1)} %copy-done.3, bf16[784,256]{1,0:T(8,128)(2,1)S(1)} %collective-permute-done.rest_1_, ...), custom_call_target="tpu_custom_call" | custom-call | flops 3211264 | bytes 6422528 | tf_op jit(solution)/shard_map/gather_y/pallas_call | solution.py:226
  74.8 0.0 copy-start
  74.8 0.8 copy-done
  75.5 0.0 copy-start.4
  75.5 0.8 copy-done.4
  76.3 0.0 copy-start.6
  76.3 0.8 copy-done.6
  77.1 0.0 copy-start.7
  77.1 0.8 copy-done.7
  77.9 0.0 all-to-all-done.in_ref
  77.9 0.0 copy-start.1
  77.9 1.0 copy-done.1
  79.0 3.3 %gather_x.1.refs_4_ = bf16[16,272,256]{2,1,0:T(8,128)(2,1)} custom-call(bf16[8,784,256]{2,1,0:T(8,128)(2,1)S(1)} %all-to-all-done.in_ref, bf16[64,16,256]{2,1,0:T(8,128)(2,1)S(1)} %copy-done.1), custom_call_target="tpu_custom_call" | custom-call | flops 3735552 | bytes 7471104 | tf_op jit(solution)/shard_map/gather_x/pallas_call | solution.py:226
  82.3 0.0 copy-start.5
  82.3 0.0 copy-start.2
  82.3 8.0 %all-to-all-start.1 = ((bf16[16,272,256]{2,1,0:T(8,128)(2,1)}), bf16[16,272,256]{2,1,0:T(8,128)(2,1)S(1)}, u32[]{:S(2)}, u32[]{:S(2)}) async-start(bf16[16,272,256]{2,1,0:T(8,128)(2,1)} %gather_x.1.refs_4_), calls=%async_computation.1 | async-start | bytes 4456448 | tf_op jit(solution)/shard_map/all_to_all | solution.py:312
  90.3 1.7 %collective-permute-start.7 = (bf16[64,16,256]{2,1,0:T(8,128)(2,1)}, bf16[64,16,256]{2,1,0:T(8,128)(2,1)S(1)}, u32[]{:S(2)}, u32[]{:S(2)}) collective-permute-start(bf16[64,16,256]{2,1,0:T(8,128)(2,1)} %copy-done.7), channel_id=1, source_target_pairs={{0,32},{32,64},{64,96},{96,0},{1,33},{33,65},{65,97},{97,1},{2,34}... | collective-permute-start | bytes 1572872 | tf_op jit(solution)/shard_map/ppermute | solution.py:282
  92.0 2.7 %collective-permute-start.8 = (bf16[64,16,256]{2,1,0:T(8,128)(2,1)}, bf16[64,16,256]{2,1,0:T(8,128)(2,1)S(1)}, u32[]{:S(2)}, u32[]{:S(2)}) collective-permute-start(bf16[64,16,256]{2,1,0:T(8,128)(2,1)} %copy-done.6), channel_id=1, source_target_pairs={{0,64},{32,96},{64,0},{96,32},{1,65},{33,97},{65,1},{97,33},{2,66}... | collective-permute-start | bytes 1572872 | tf_op jit(solution)/shard_map/ppermute | solution.py:282
  94.7 0.0 copy-done.5
  94.7 1.5 %collective-permute-start.9 = (bf16[64,16,256]{2,1,0:T(8,128)(2,1)S(1)}, bf16[64,16,256]{2,1,0:T(8,128)(2,1)S(1)}, u32[]{:S(2)}, u32[]{:S(2)}) collective-permute-start(bf16[64,16,256]{2,1,0:T(8,128)(2,1)S(1)} %copy-done.5), channel_id=1, source_target_pairs={{0,96},{32,0},{64,32},{96,64},{1,97},{33,1},{65,33},{97,65},{2,98}... | collective-permute-start | bytes 1572872 | tf_op jit(solution)/shard_map/ppermute | solution.py:282
  96.2 9.4 %collective-permute-done.7.refs_1_ = bf16[64,16,256]{2,1,0:T(8,128)(2,1)S(1)} collective-permute-done((bf16[64,16,256]{2,1,0:T(8,128)(2,1)}, bf16[64,16,256]{2,1,0:T(8,128)(2,1)S(1)}, u32[]{:S(2)}, u32[]{:S(2)}) %collective-permute-start.7) | collective-permute-done | bytes 524320 | tf_op jit(solution)/shard_map/ppermute | solution.py:282
  105.5 11.7 %collective-permute-done.8.refs_2_ = bf16[64,16,256]{2,1,0:T(8,128)(2,1)S(1)} collective-permute-done((bf16[64,16,256]{2,1,0:T(8,128)(2,1)}, bf16[64,16,256]{2,1,0:T(8,128)(2,1)S(1)}, u32[]{:S(2)}, u32[]{:S(2)}) %collective-permute-start.8) | collective-permute-done | bytes 524320 | tf_op jit(solution)/shard_map/ppermute | solution.py:282
  117.3 0.0 collective-permute-done.9.refs_3_
  117.3 0.0 copy-done.2
  117.3 0.3 ring_z.1
  117.5 1.6 %collective-permute-start.10 = (bf16[4,4,16,256]{3,2,1,0:T(8,128)(2,1)S(1)}, bf16[4,4,16,256]{3,2,1,0:T(8,128)(2,1)S(1)}, u32[]{:S(2)}, u32[]{:S(2)}) collective-permute-start(bf16[4,4,16,256]{3,2,1,0:T(8,128)(2,1)S(1)} %get-tuple-element.40), channel_id=1, source_target_pairs={{0,1},{1,2},{2,3},{3,0},{4,5},{5,6},{6,7},{7,4},{8,9},{9,10},{10,1... | collective-permute-start | bytes 393224 | tf_op jit(solution)/shard_map/ppermute | solution.py:282
  119.2 2.7 %collective-permute-start.11 = (bf16[4,4,16,256]{3,2,1,0:T(8,128)(2,1)S(1)}, bf16[4,4,16,256]{3,2,1,0:T(8,128)(2,1)S(1)}, u32[]{:S(2)}, u32[]{:S(2)}) collective-permute-start(bf16[4,4,16,256]{3,2,1,0:T(8,128)(2,1)S(1)} %get-tuple-element.41), channel_id=1, source_target_pairs={{0,2},{1,3},{2,0},{3,1},{4,6},{5,7},{6,4},{7,5},{8,10},{9,11},{10,... | collective-permute-start | bytes 393224 | tf_op jit(solution)/shard_map/ppermute | solution.py:282
  121.9 1.5 %collective-permute-start.12 = (bf16[4,4,16,256]{3,2,1,0:T(8,128)(2,1)S(1)}, bf16[4,4,16,256]{3,2,1,0:T(8,128)(2,1)S(1)}, u32[]{:S(2)}, u32[]{:S(2)}) collective-permute-start(bf16[4,4,16,256]{3,2,1,0:T(8,128)(2,1)S(1)} %get-tuple-element.42), channel_id=1, source_target_pairs={{0,3},{1,0},{2,1},{3,2},{4,7},{5,4},{6,5},{7,6},{8,11},{9,8},{10,9... | collective-permute-start | bytes 393224 | tf_op jit(solution)/shard_map/ppermute | solution.py:282
  123.3 1.5 %collective-permute-done.10.refs_1_ = bf16[4,4,16,256]{3,2,1,0:T(8,128)(2,1)S(1)} collective-permute-done((bf16[4,4,16,256]{3,2,1,0:T(8,128)(2,1)S(1)}, bf16[4,4,16,256]{3,2,1,0:T(8,128)(2,1)S(1)}, u32[]{:S(2)}, u32[]{:S(2)}) %collective-permute-start.10) | collective-permute-done | bytes 131104 | tf_op jit(solution)/shard_map/ppermute | solution.py:282
  124.8 2.7 %collective-permute-done.11.refs_2_ = bf16[4,4,16,256]{3,2,1,0:T(8,128)(2,1)S(1)} collective-permute-done((bf16[4,4,16,256]{3,2,1,0:T(8,128)(2,1)S(1)}, bf16[4,4,16,256]{3,2,1,0:T(8,128)(2,1)S(1)}, u32[]{:S(2)}, u32[]{:S(2)}) %collective-permute-start.11) | collective-permute-done | bytes 131104 | tf_op jit(solution)/shard_map/ppermute | solution.py:282
  127.5 0.0 collective-permute-done.12.refs_3_
  127.5 0.1 ring_y.1
  127.5 0.9 collective-permute-start.13
  128.4 2.7 %collective-permute-start.14 = (f32[4,16,256]{2,1,0:T(8,128)S(1)}, f32[4,16,256]{2,1,0:T(8,128)S(1)}, u32[]{:S(2)}, u32[]{:S(2)}) collective-permute-start(f32[4,16,256]{2,1,0:T(8,128)S(1)} %get-tuple-element.45), channel_id=1, source_target_pairs={{0,8},{4,12},{8,0},{12,4},{1,9},{5,13},{9,1},{13,5},{2,10},{6,14},... | collective-permute-start | bytes 196616 | tf_op jit(solution)/shard_map/ppermute | solution.py:282
  131.1 1.5 %collective-permute-start.15 = (f32[4,16,256]{2,1,0:T(8,128)S(1)}, f32[4,16,256]{2,1,0:T(8,128)S(1)}, u32[]{:S(2)}, u32[]{:S(2)}) collective-permute-start(f32[4,16,256]{2,1,0:T(8,128)S(1)} %get-tuple-element.46), channel_id=1, source_target_pairs={{0,12},{4,0},{8,4},{12,8},{1,13},{5,1},{9,5},{13,9},{2,14},{6,2},{... | collective-permute-start | bytes 196616 | tf_op jit(solution)/shard_map/ppermute | solution.py:282
  132.6 0.5 collective-permute-done.13.rest_1_
  133.1 1.1 collective-permute-done.14.rest_2_
  134.2 1.2 collective-permute-done.15.rest_3_
  135.4 0.0 all-to-all-done.1.x_ref
  135.4 1.1 finish.1
Async XLA Ops:
  27.7 50.2 %all-to-all-start = ((bf16[8,784,256]{2,1,0:T(8,128)(2,1)}), bf16[8,784,256]{2,1,0:T(8,128)(2,1)S(1)}, u32[]{:S(2)}, u32[]{:S(2)}) async-start(bf16[8,784,256]{2,1,0:T(8,128)(2,1)} %match_second.1), calls=%async_computation | async-start | bytes 6422528 | tf_op jit(solution)/shard_map/all_to_all | solution.py:299
  32.1 13.5 %collective-permute-start = (bf16[784,256]{1,0:T(8,128)(2,1)}, bf16[784,256]{1,0:T(8,128)(2,1)S(1)}, u32[]{:S(2)}, u32[]{:S(2)}) collective-permute-start(bf16[784,256]{1,0:T(8,128)(2,1)} %get-tuple-element.28), channel_id=1, source_target_pairs={{0,4},{4,8},{8,12},{12,0},{16,20},{20,24},{24,28},{28,16},{1,5},{5... | collective-permute-start | bytes 1204232 | tf_op jit(solution)/shard_map/ppermute | solution.py:298
  33.7 21.8 %collective-permute-start.1 = (bf16[784,256]{1,0:T(8,128)(2,1)}, bf16[784,256]{1,0:T(8,128)(2,1)S(1)}, u32[]{:S(2)}, u32[]{:S(2)}) collective-permute-start(bf16[784,256]{1,0:T(8,128)(2,1)} %get-tuple-element.29), channel_id=1, source_target_pairs={{0,8},{4,12},{8,0},{12,4},{16,24},{20,28},{24,16},{28,20},{1,9},{5... | collective-permute-start | bytes 1204232 | tf_op jit(solution)/shard_map/ppermute | solution.py:298
  36.6 19.2 %collective-permute-start.2 = (bf16[784,256]{1,0:T(8,128)(2,1)}, bf16[784,256]{1,0:T(8,128)(2,1)S(1)}, u32[]{:S(2)}, u32[]{:S(2)}) collective-permute-start(bf16[784,256]{1,0:T(8,128)(2,1)} %get-tuple-element.30), channel_id=1, source_target_pairs={{0,12},{4,0},{8,4},{12,8},{16,28},{20,16},{24,20},{28,24},{1,13},{... | collective-permute-start | bytes 1204232 | tf_op jit(solution)/shard_map/ppermute | solution.py:298
  37.9 17.8 %collective-permute-start.3 = (bf16[784,256]{1,0:T(8,128)(2,1)}, bf16[784,256]{1,0:T(8,128)(2,1)S(1)}, u32[]{:S(2)}, u32[]{:S(2)}) collective-permute-start(bf16[784,256]{1,0:T(8,128)(2,1)} %get-tuple-element.31), channel_id=1, source_target_pairs={{0,16},{4,20},{8,24},{12,28},{16,0},{20,4},{24,8},{28,12},{1,17},{... | collective-permute-start | bytes 1204232 | tf_op jit(solution)/shard_map/ppermute | solution.py:298
  37.9 24.2 %collective-permute-start.4 = (bf16[784,256]{1,0:T(8,128)(2,1)}, bf16[784,256]{1,0:T(8,128)(2,1)S(1)}, u32[]{:S(2)}, u32[]{:S(2)}) collective-permute-start(bf16[784,256]{1,0:T(8,128)(2,1)} %get-tuple-element.32), channel_id=1, source_target_pairs={{0,20},{4,24},{8,28},{12,16},{16,4},{20,8},{24,12},{28,0},{1,21},{... | collective-permute-start | bytes 1204232 | tf_op jit(solution)/shard_map/ppermute | solution.py:298
  45.6 26.3 %collective-permute-start.5 = (bf16[784,256]{1,0:T(8,128)(2,1)}, bf16[784,256]{1,0:T(8,128)(2,1)S(1)}, u32[]{:S(2)}, u32[]{:S(2)}) collective-permute-start(bf16[784,256]{1,0:T(8,128)(2,1)} %get-tuple-element.33), channel_id=1, source_target_pairs={{0,24},{4,28},{8,16},{12,20},{16,8},{20,12},{24,0},{28,4},{1,25},{... | collective-permute-start | bytes 1204232 | tf_op jit(solution)/shard_map/ppermute | solution.py:298
  55.5 16.4 %collective-permute-start.6 = (bf16[784,256]{1,0:T(8,128)(2,1)}, bf16[784,256]{1,0:T(8,128)(2,1)S(1)}, u32[]{:S(2)}, u32[]{:S(2)}) collective-permute-start(bf16[784,256]{1,0:T(8,128)(2,1)} %get-tuple-element.34), channel_id=1, source_target_pairs={{0,28},{4,16},{8,20},{12,24},{16,12},{20,0},{24,4},{28,8},{1,29},{... | collective-permute-start | bytes 1204232 | tf_op jit(solution)/shard_map/ppermute | solution.py:298
  71.9 1.0 copy-start.3
  74.8 0.8 copy-start
  75.5 0.8 copy-start.4
  76.3 0.8 copy-start.6
  77.1 0.8 copy-start.7
  77.9 1.0 copy-start.1
  82.3 12.4 %copy-start.5 = (bf16[64,16,256]{2,1,0:T(8,128)(2,1)S(1)}, bf16[64,16,256]{2,1,0:T(8,128)(2,1)}, u32[]{:S(2)}) copy-start(bf16[64,16,256]{2,1,0:T(8,128)(2,1)} %copy-done.4) | copy-start | bytes 1572868
  82.3 35.0 %copy-start.2 = (bf16[64,16,256]{2,1,0:T(8,128)(2,1)S(1)}, bf16[64,16,256]{2,1,0:T(8,128)(2,1)}, u32[]{:S(2)}) copy-start(bf16[64,16,256]{2,1,0:T(8,128)(2,1)} %copy-done) | copy-start | bytes 1572868
  82.3 53.0 %all-to-all-start.1 = ((bf16[16,272,256]{2,1,0:T(8,128)(2,1)}), bf16[16,272,256]{2,1,0:T(8,128)(2,1)S(1)}, u32[]{:S(2)}, u32[]{:S(2)}) async-start(bf16[16,272,256]{2,1,0:T(8,128)(2,1)} %gather_x.1.refs_4_), calls=%async_computation.1 | async-start | bytes 4456448 | tf_op jit(solution)/shard_map/all_to_all | solution.py:312
  90.3 15.3 %collective-permute-start.7 = (bf16[64,16,256]{2,1,0:T(8,128)(2,1)}, bf16[64,16,256]{2,1,0:T(8,128)(2,1)S(1)}, u32[]{:S(2)}, u32[]{:S(2)}) collective-permute-start(bf16[64,16,256]{2,1,0:T(8,128)(2,1)} %copy-done.7), channel_id=1, source_target_pairs={{0,32},{32,64},{64,96},{96,0},{1,33},{33,65},{65,97},{97,1},{2,34}... | collective-permute-start | bytes 1572872 | tf_op jit(solution)/shard_map/ppermute | solution.py:282
  92.0 25.2 %collective-permute-start.8 = (bf16[64,16,256]{2,1,0:T(8,128)(2,1)}, bf16[64,16,256]{2,1,0:T(8,128)(2,1)S(1)}, u32[]{:S(2)}, u32[]{:S(2)}) collective-permute-start(bf16[64,16,256]{2,1,0:T(8,128)(2,1)} %copy-done.6), channel_id=1, source_target_pairs={{0,64},{32,96},{64,0},{96,32},{1,65},{33,97},{65,1},{97,33},{2,66}... | collective-permute-start | bytes 1572872 | tf_op jit(solution)/shard_map/ppermute | solution.py:282
  94.7 22.6 %collective-permute-start.9 = (bf16[64,16,256]{2,1,0:T(8,128)(2,1)S(1)}, bf16[64,16,256]{2,1,0:T(8,128)(2,1)S(1)}, u32[]{:S(2)}, u32[]{:S(2)}) collective-permute-start(bf16[64,16,256]{2,1,0:T(8,128)(2,1)S(1)} %copy-done.5), channel_id=1, source_target_pairs={{0,96},{32,0},{64,32},{96,64},{1,97},{33,1},{65,33},{97,65},{2,98}... | collective-permute-start | bytes 1572872 | tf_op jit(solution)/shard_map/ppermute | solution.py:282
  117.5 7.3 %collective-permute-start.10 = (bf16[4,4,16,256]{3,2,1,0:T(8,128)(2,1)S(1)}, bf16[4,4,16,256]{3,2,1,0:T(8,128)(2,1)S(1)}, u32[]{:S(2)}, u32[]{:S(2)}) collective-permute-start(bf16[4,4,16,256]{3,2,1,0:T(8,128)(2,1)S(1)} %get-tuple-element.40), channel_id=1, source_target_pairs={{0,1},{1,2},{2,3},{3,0},{4,5},{5,6},{6,7},{7,4},{8,9},{9,10},{10,1... | collective-permute-start | bytes 393224 | tf_op jit(solution)/shard_map/ppermute | solution.py:282
  119.2 8.3 %collective-permute-start.11 = (bf16[4,4,16,256]{3,2,1,0:T(8,128)(2,1)S(1)}, bf16[4,4,16,256]{3,2,1,0:T(8,128)(2,1)S(1)}, u32[]{:S(2)}, u32[]{:S(2)}) collective-permute-start(bf16[4,4,16,256]{3,2,1,0:T(8,128)(2,1)S(1)} %get-tuple-element.41), channel_id=1, source_target_pairs={{0,2},{1,3},{2,0},{3,1},{4,6},{5,7},{6,4},{7,5},{8,10},{9,11},{10,... | collective-permute-start | bytes 393224 | tf_op jit(solution)/shard_map/ppermute | solution.py:282
  121.9 5.6 %collective-permute-start.12 = (bf16[4,4,16,256]{3,2,1,0:T(8,128)(2,1)S(1)}, bf16[4,4,16,256]{3,2,1,0:T(8,128)(2,1)S(1)}, u32[]{:S(2)}, u32[]{:S(2)}) collective-permute-start(bf16[4,4,16,256]{3,2,1,0:T(8,128)(2,1)S(1)} %get-tuple-element.42), channel_id=1, source_target_pairs={{0,3},{1,0},{2,1},{3,2},{4,7},{5,4},{6,5},{7,6},{8,11},{9,8},{10,9... | collective-permute-start | bytes 393224 | tf_op jit(solution)/shard_map/ppermute | solution.py:282
  127.5 5.5 %collective-permute-start.13 = (f32[4,16,256]{2,1,0:T(8,128)S(1)}, f32[4,16,256]{2,1,0:T(8,128)S(1)}, u32[]{:S(2)}, u32[]{:S(2)}) collective-permute-start(f32[4,16,256]{2,1,0:T(8,128)S(1)} %get-tuple-element.44), channel_id=1, source_target_pairs={{0,4},{4,8},{8,12},{12,0},{1,5},{5,9},{9,13},{13,1},{2,6},{6,10},{... | collective-permute-start | bytes 196616 | tf_op jit(solution)/shard_map/ppermute | solution.py:282
  128.4 5.8 %collective-permute-start.14 = (f32[4,16,256]{2,1,0:T(8,128)S(1)}, f32[4,16,256]{2,1,0:T(8,128)S(1)}, u32[]{:S(2)}, u32[]{:S(2)}) collective-permute-start(f32[4,16,256]{2,1,0:T(8,128)S(1)} %get-tuple-element.45), channel_id=1, source_target_pairs={{0,8},{4,12},{8,0},{12,4},{1,9},{5,13},{9,1},{13,5},{2,10},{6,14},... | collective-permute-start | bytes 196616 | tf_op jit(solution)/shard_map/ppermute | solution.py:282
  131.1 4.3 %collective-permute-start.15 = (f32[4,16,256]{2,1,0:T(8,128)S(1)}, f32[4,16,256]{2,1,0:T(8,128)S(1)}, u32[]{:S(2)}, u32[]{:S(2)}) collective-permute-start(f32[4,16,256]{2,1,0:T(8,128)S(1)} %get-tuple-element.46), channel_id=1, source_target_pairs={{0,12},{4,0},{8,4},{12,8},{1,13},{5,1},{9,5},{13,9},{2,14},{6,2},{... | collective-permute-start | bytes 196616 | tf_op jit(solution)/shard_map/ppermute | solution.py:282

commit v3 on v2

v3 whole, which is shorter than its diff:
```python
import functools

import jax
import jax.numpy as jnp
import numpy as np
from jax import lax
from jax.experimental import pallas as pl
from jax.experimental.pallas import tpu as pltpu
from jax.sharding import Mesh, PartitionSpec as P

NB = 8
POS = 4
LANE = 128
BF = jnp.bfloat16
F32 = jnp.float32
NX, NC, NY, NZ = 4, 2, 4, 4
VISITS, TILES = NX * NC, NY * NZ
COUNT = TILES * POS
SUB = 16
VMEM_BIG = 60 << 20
WORK = 40_000_000_000
GX, GY, RZ = 40000000000, 40000000000, 1000000000
Y_OFFSETS = ((0, 0), (1, 0), (0, 1), (0, 2), (1, 2), (0, 3), (1, 1), (1, 3))


GROUP = 4


def toeplitz(row, length):
    wide = jnp.broadcast_to(row, (LANE, length))
    return pltpu.roll(wide, 0, 1, stride=1, stride_axis=0)


def band_blocks(table, taps_ref, turned):
    count = taps_ref.shape[1]
    half = (count - 1) // 2
    length = 3 * LANE
    q = lax.broadcasted_iota(jnp.int32, (count, length), 0)
    n = lax.broadcasted_iota(jnp.int32, (count, length), 1)
    hit = n - q == LANE - half if turned else n + q == LANE + half
    base = jnp.dot(taps_ref[...].astype(BF), hit.astype(F32).astype(BF), preferred_element_type=F32)
    for k in range(NB):
        table[k] = toeplitz(base[k : k + 1], length).astype(BF)


def put_band(band, block, row0, col0):
    for a in range(band.shape[0] // LANE):
        at = row0 + a
        lo, hi = max(at - 1, col0), min(at + 2, col0 + band.shape[1] // LANE)
        if lo < hi:
            off = (lo - (at - 1)) * LANE
            band[a * LANE : (a + 1) * LANE, (lo - col0) * LANE : (hi - col0) * LANE] = block[
                :, off : off + (hi - lo) * LANE
            ]


def combo_rows(dest_ref, pos_ref, blocks):
    row = lax.broadcasted_iota(jnp.int32, (SUB, LANE), 0)
    places = jnp.full((SUB, LANE), COUNT, jnp.int32)
    for b in range(blocks):
        places = jnp.where(row == b, dest_ref[b] * POS + pos_ref[b], places)
    return places.astype(F32).astype(BF)


def lane_weights(ivt, b, width):
    onehot = (lax.broadcasted_iota(jnp.int32, (LANE, LANE), 0) == b).astype(F32).astype(BF)
    weight = jnp.dot(ivt[...], onehot, preferred_element_type=F32)
    return jnp.concatenate([weight] * (width // LANE), axis=1)


def padded_weights(iv_ref):
    blocks, side = iv_ref.shape
    return jnp.concatenate([iv_ref[...].astype(F32), jnp.zeros((LANE - blocks, side), F32)], axis=0)


def match_x_kernel(kidx_ref, dest_ref, pos_ref, rtap_ref, ctap_ref, iv_ref, img_ref, x_ref, mid_ref, *scratch):
    rtab, ctab, rband, cband, ivt, image, mids, x_buf, in_sem, mid_sem, x_sem = scratch
    blocks, side = iv_ref.shape
    rows, width = side // VISITS, side // 2
    top = blocks * rows
    loads = [pltpu.make_async_copy(img_ref.at[b], image.at[b], in_sem.at[b]) for b in range(blocks)]
    for load in loads:
        load.start()

    places = combo_rows(dest_ref, pos_ref, blocks)
    weights = padded_weights(iv_ref)
    ivt[...] = jnp.transpose(weights).astype(BF)
    for v in range(VISITS):
        part = weights[:SUB, (v // 2) * LANE : (v // 2 + 1) * LANE]
        if v % 2:
            part = pltpu.roll(part, rows, 1)
        x_buf[v, top:, :LANE] = part.astype(BF)
        x_buf[v, top:, LANE:] = places
    band_blocks(rtab, rtap_ref, False)
    band_blocks(ctab, ctap_ref, True)
    rband[...] = jnp.zeros_like(rband)
    cband[...] = jnp.zeros_like(cband)

    stores = []
    for b in range(blocks):
        k = kidx_ref[b]
        put_band(rband, rtab.at[k], 0, 0)
        put_band(cband, ctab.at[k], 0, 0)
        weight = lane_weights(ivt, b, width)
        loads[b].wait()
        mid = jnp.dot(rband[...], image[b], preferred_element_type=F32).astype(BF)
        mids[b] = mid[:, LANE:]
        stores.append(pltpu.make_async_copy(mids.at[b], mid_ref.at[b], mid_sem.at[b]))
        stores[-1].start()
        matched = jnp.dot(mid[:, : 3 * LANE], cband[...], preferred_element_type=F32)
        weighted = (matched * weight).astype(BF)
        for v in range(VISITS):
            x_buf[v, b * rows : (b + 1) * rows] = weighted[v * rows : (v + 1) * rows]
        if (b + 1) % GROUP == 0 or b + 1 == blocks:
            g = b // GROUP
            first = g * GROUP * rows
            last = (b + 1) * rows + (SUB if b + 1 == blocks else 0)
            part = pl.ds(first, last - first)
            stores.append(pltpu.make_async_copy(x_buf.at[:, part], x_ref.at[:, part], x_sem.at[g]))
            stores[-1].start()
    for store in stores:
        store.wait()


def match_y_kernel(kidx_ref, dest_ref, pos_ref, ctap_ref, iv_ref, mid_ref, *rest):
    n = len(Y_OFFSETS)
    y_refs = rest[:n]
    ctab, cband, ivt, mids, y_buf, whole, in_sem, y_sem = rest[n:]
    blocks, side = iv_ref.shape
    tiles, rows, width = side // LANE, side // VISITS, side // 2
    top = blocks * rows
    loads = [pltpu.make_async_copy(mid_ref.at[b], mids.at[b], in_sem.at[b]) for b in range(blocks)]
    for load in loads:
        load.start()

    places = combo_rows(dest_ref, pos_ref, blocks)
    ivt[...] = jnp.transpose(padded_weights(iv_ref)).astype(BF)
    for i in range(n):
        y_buf[i, top:, :LANE] = places
        y_buf[i, top:, LANE:] = places
    band_blocks(ctab, ctap_ref, True)
    cband[...] = jnp.zeros_like(cband)

    mc, my = lax.axis_index("core"), lax.axis_index("y")
    stores = []
    for b in range(blocks):
        put_band(cband, ctab.at[kidx_ref[b]], tiles - 3, tiles // 2)
        weight = lane_weights(ivt, b, width)
        loads[b].wait()
        matched = jnp.dot(mids[b], cband[...], preferred_element_type=F32)
        whole[b % 2] = (matched * weight).astype(BF)
        for i, (dc, dy) in enumerate(Y_OFFSETS):
            core, sub = lax.rem(mc + dc, NC), lax.rem(my + dy, NY)
            for x in range(NX):
                start = pl.multiple_of((x * NC + core) * rows + sub * SUB, SUB)
                y_buf[i, b * rows + x * SUB : b * rows + (x + 1) * SUB] = whole[b % 2, pl.ds(start, SUB), :]
        if (b + 1) % GROUP == 0 or b + 1 == blocks:
            g = b // GROUP
            first = g * GROUP * rows
            last = (b + 1) * rows + (SUB if b + 1 == blocks else 0)
            part = pl.ds(first, last - first)
            for i in range(n):
                stores.append(pltpu.make_async_copy(y_buf.at[i, part], y_refs[i].at[part], y_sem.at[g, i]))
                stores[-1].start()
    for store in stores:
        store.wait()


def match(kidx, dest, position, row_taps, col_taps, image, inv_var):
    blocks, side, _ = image.shape
    rows, width = side // VISITS, side // 2
    tall = blocks * rows + SUB
    groups = -(-blocks // GROUP)
    n = len(Y_OFFSETS)
    smem = pl.BlockSpec(memory_space=pltpu.SMEM)
    vmem = pl.BlockSpec(memory_space=pltpu.VMEM)
    hbm = pl.BlockSpec(memory_space=pltpu.HBM)
    table = pltpu.VMEM((NB, LANE, 3 * LANE), BF)
    band = pltpu.VMEM((3 * LANE, width), BF)
    turned = pltpu.VMEM((side, LANE), BF)
    sems = pltpu.SemaphoreType.DMA
    shape = jax.ShapeDtypeStruct
    rest = (blocks, side, side - LANE)
    params = pltpu.CompilerParams(vmem_limit_bytes=VMEM_BIG)
    cost = pl.CostEstimate(flops=WORK, bytes_accessed=image.size * 4, transcendentals=0)
    x_part, mid = pl.pallas_call(
        match_x_kernel,
        in_specs=[smem] * 3 + [vmem] * 3 + [hbm],
        out_specs=[hbm] * 2,
        out_shape=[shape((VISITS, tall, width), BF), shape(rest, BF)],
        scratch_shapes=[
            table,
            table,
            pltpu.VMEM((side, side), BF),
            band,
            turned,
            pltpu.VMEM(image.shape, BF),
            pltpu.VMEM(rest, BF),
            pltpu.VMEM((VISITS, tall, width), BF),
            sems((blocks,)),
            sems((blocks,)),
            sems((groups,)),
        ],
        compiler_params=params,
        cost_estimate=cost,
        name="match_x",
    )(kidx, dest, position, row_taps, col_taps, inv_var, image)
    y_parts = pl.pallas_call(
        match_y_kernel,
        in_specs=[smem] * 3 + [vmem] * 2 + [hbm],
        out_specs=[hbm] * n,
        out_shape=[shape((tall, width), BF)] * n,
        scratch_shapes=[
            table,
            band,
            turned,
            pltpu.VMEM(rest, BF),
            pltpu.VMEM((n, tall, width), BF),
            pltpu.VMEM((2, side, width), BF),
            sems((blocks,)),
            sems((groups, n)),
        ],
        compiler_params=params,
        cost_estimate=cost,
        name="match_y",
    )(kidx, dest, position, col_taps, inv_var, mid)
    return x_part, y_parts


def read_places(notes, flat, smem, sem):
    places = jnp.concatenate([n.astype(F32) for n in notes], axis=0)
    size = VISITS * SUB
    row = lax.broadcasted_iota(jnp.int32, (size, LANE), 0)
    lane = lax.broadcasted_iota(jnp.int32, (size, LANE), 1)
    line = jnp.sum(jnp.where(row == lane, places, 0.0), axis=0, keepdims=True)
    flat[...] = line.astype(jnp.int32)
    copy = pltpu.make_async_copy(flat, smem, sem)
    copy.start()
    copy.wait()
    return line


def gather_x_kernel(in_ref, out_hbm, acc, flat, smem, sem, out_ref, out_sem):
    rows, width = acc.shape[1:]
    blocks = (in_ref.shape[1] - SUB) // rows
    top = blocks * rows
    line = read_places([in_ref[v, top:, LANE:] for v in range(VISITS)], flat, smem, sem)
    acc[...] = jnp.zeros_like(acc)
    for v in range(VISITS):
        for b in range(blocks):
            acc[smem[0, v * SUB + b]] += in_ref[v, b * rows : (b + 1) * rows].astype(F32)
    place = lax.broadcasted_iota(jnp.int32, (COUNT, LANE), 0)
    hit = (place == line.astype(jnp.int32)).astype(F32).astype(BF)
    weights = jnp.concatenate([in_ref[v, top:, :LANE].astype(F32) for v in range(VISITS)], axis=0).astype(BF)
    den = jnp.dot(hit, weights, preferred_element_type=F32)
    high = den.astype(BF).astype(F32)
    both = jnp.concatenate([high, den - high], axis=1)
    stores = []
    for t in range(TILES):
        for p in range(POS):
            out_ref[t, p * rows : (p + 1) * rows] = acc[t * POS + p].astype(BF)
        pad = jnp.zeros((SUB - POS, width), F32)
        out_ref[t, POS * rows :] = jnp.concatenate([both[t * POS : (t + 1) * POS], pad], axis=0).astype(BF)
        if (t + 1) % GROUP == 0:
            part = pl.ds(t + 1 - GROUP, GROUP)
            stores.append(pltpu.make_async_copy(out_ref.at[part], out_hbm.at[part], out_sem.at[t // GROUP]))
            stores[-1].start()
    for store in stores:
        store.wait()


def gather_y_kernel(*rest):
    n = len(Y_OFFSETS)
    pieces, outs, (acc, flat, smem, sem, out_buf, out_sem) = rest[:n], rest[n + 1 : -6], rest[-6:]
    rows = acc.shape[1]
    blocks = (pieces[0].shape[0] - SUB) // rows
    mx = lax.axis_index("x")
    read_places([r[blocks * rows :, LANE:] for r in pieces], flat, smem, sem)
    acc[...] = jnp.zeros_like(acc)
    for i in range(n):
        for b in range(blocks):
            acc[smem[0, i * SUB + b]] += pieces[i][b * rows : (b + 1) * rows].astype(F32)
    stores = [pltpu.make_async_copy(out_buf.at[i], outs[i], out_sem.at[i]) for i in range(NX)]
    for i in range(NX):
        to = pl.multiple_of(lax.rem(mx + i, NX) * SUB, SUB)
        out_buf[i] = acc[:, pl.ds(to, SUB), :].astype(BF)
        stores[i].start()
    for store in stores:
        store.wait()


def vmem_call(kernel, name, out_shape, args, scratch=(), after=0, flops=0, hbm_out=False):
    vm = pl.BlockSpec(memory_space=pltpu.VMEM)
    anywhere = pl.BlockSpec(memory_space=pl.ANY)
    size = sum(a.size * a.dtype.itemsize for a in args)
    flops = flops or size
    return pl.pallas_call(
        kernel,
        in_specs=[vm] * (len(args) - after) + [anywhere] * after,
        out_specs=jax.tree.map(lambda _: pl.BlockSpec(memory_space=pltpu.HBM) if hbm_out else vm, out_shape),
        out_shape=out_shape,
        scratch_shapes=list(scratch),
        compiler_params=pltpu.CompilerParams(vmem_limit_bytes=32 << 20),
        cost_estimate=pl.CostEstimate(flops=flops, bytes_accessed=2 * size, transcendentals=0),
        name=name,
    )(*args)


def ring_z_kernel(*refs):
    ins, outs = refs[:NX], refs[NX:]
    mz = lax.axis_index("z")
    for i in range(NZ):
        for y in range(NY):
            at = pl.ds((y * NZ + lax.rem(mz + i, NZ)) * POS, POS)
            outs[i][y] = sum(r[at].astype(F32) for r in ins).astype(BF)


def ring_y_kernel(*refs):
    ins, outs = refs[:NZ], refs[NZ:]
    my = lax.axis_index("y")
    for i in range(NY):
        at = lax.rem(my + i, NY)
        outs[i][...] = sum(r[at].astype(F32) for r in ins)


def finish_kernel(x_ref, *rest):
    y_refs, out_ref, inv = rest[:-2], rest[-2], rest[-1]
    rows = out_ref.shape[1]
    width = x_ref.shape[2]
    my = lax.axis_index("y")
    notes = sum(x_ref[s, POS * rows :].astype(F32) for s in range(TILES))
    den = 1.0 / jnp.maximum(notes[:, :LANE] + notes[:, LANE:], 1.0)
    for p in range(POS):
        turned = jnp.transpose(jnp.broadcast_to(den[p : p + 1], (LANE, LANE)))[:rows]
        inv[p] = turned
        total = x_ref[0, p * rows : (p + 1) * rows].astype(F32)
        for s in range(1, TILES):
            total += x_ref[s, p * rows : (p + 1) * rows].astype(F32)
        for j in range(width // LANE):
            out_ref[p, :, j * LANE : (j + 1) * LANE] = total[:, j * LANE : (j + 1) * LANE] * turned
    for i in range(NY):
        at = pl.ds(pl.multiple_of(lax.rem(my - i + NY, NY) * SUB, SUB), SUB)
        for p in range(POS):
            scale = inv[p, at, :]
            for j in range(width // LANE):
                lanes = slice(width + j * LANE, width + (j + 1) * LANE)
                out_ref[p, at, lanes] = y_refs[i][p, :, j * LANE : (j + 1) * LANE] * scale


def ring(pieces, axis, size):
    out = [pieces[0]]
    for i in range(1, size):
        out.append(lax.ppermute(pieces[i], axis, [(s, (s + i) % size) for s in range(size)]))
    return out


def per_device(image, inv_var, kernel_index, dest, position, row_taps, col_taps):
    _, side, _ = image.shape
    rows, width = side // VISITS, side // 2
    shape = jax.ShapeDtypeStruct
    x_part, y_parts = match(kernel_index, dest[:, 0], position, row_taps, col_taps, image, inv_var)

    arrived = [y_parts[0]]
    for i in range(1, len(Y_OFFSETS)):
        dc, dy = Y_OFFSETS[i]
        perm = [
            (c * NY + y, ((c + dc) % NC) * NY + (y + dy) % NY) for c in range(NC) for y in range(NY)
        ]
        arrived.append(lax.ppermute(y_parts[i], ("core", "y"), perm))
    x_in = lax.all_to_all(x_part, ("x", "core"), 0, 0, tiled=True)

    scratch = [
        pltpu.VMEM((COUNT, rows, width), F32),
        pltpu.VMEM((1, LANE), jnp.int32),
        pltpu.SMEM((1, LANE), jnp.int32),
        pltpu.SemaphoreType.DMA,
    ]
    y_scratch = scratch + [pltpu.VMEM((NX, COUNT, SUB, width), BF), pltpu.SemaphoreType.DMA((NX,))]
    x_scratch = scratch + [
        pltpu.VMEM((TILES, POS * rows + SUB, width), BF),
        pltpu.SemaphoreType.DMA((TILES // GROUP,)),
    ]
    x_sum = vmem_call(
        gather_x_kernel, "gather_x", shape((TILES, POS * rows + SUB, width), BF), (x_in,), x_scratch, 0, GX, True
    )
    mine = vmem_call(gather_y_kernel, "gather_y", [shape((COUNT, SUB, width), BF)] * NX, (*arrived, x_sum), y_scratch, 1, GY, True)
    along_x = ring(mine, "x", NX)
    x_out = lax.all_to_all(x_sum, ("y", "z"), 0, 0, tiled=True)
    along_z = vmem_call(
        ring_z_kernel, "ring_z", [shape((NY, POS, SUB, width), BF)] * NZ, along_x, flops=RZ
    )
    along_z = ring(along_z, "z", NZ)
    along_y = vmem_call(ring_y_kernel, "ring_y", [shape((POS, SUB, width), F32)] * NY, along_z)
    along_y = ring(along_y, "y", NY)
    out = vmem_call(
        finish_kernel,
        "finish",
        shape((POS, rows, side), F32),
        (x_out, *along_y),
        [pltpu.VMEM((POS, rows, LANE), F32)],
    )
    return out[None]


def solution(mesh):
    mesh = Mesh(mesh.devices.reshape(NX, NC, NY, NZ), ("x", "core", "y", "z"))
    every = ("x", "core", "y", "z")
    in_specs = (P(every, None, None), P(every, None), P(every), P(every, None), P(every), P(), P())
    out_specs = P(("y", "z"), None, ("x", "core"), None)
    return jax.shard_map(
        per_device, mesh=mesh, in_specs=in_specs, out_specs=out_specs, check_vma=False
    )
```

time: 138 us -> 121 us (0.88)
  waiting for transfers between devices: 60 us -> 50.9 us
  Pallas kernels: 34.3 us -> 27.4 us
    ppermute x7, waiting for transfers between devices: 31.9 us -> 6.64 us  [per_device(): arrived.append(lax.ppermute(y_parts[i], ('core', 'y'), perm))]
    all_to_all x1, waiting for transfers between devices: 0.01 us -> 15.4 us  [per_device(): x_in = lax.all_to_all(x_part, ('x', 'core'), 0, 0, tiled=True)]
    pallas_call x2, Pallas kernels: 27.7 us -> 20.1 us  [the longest x1 11.8 us: match(): pl.pallas_call(match_x_kernel, in_specs=[smem] * 3 + [vmem] * 3 + [hbm],...]
    unnamed x16 -> x14, local copies, waits for them, and re-layouts: 5.21 us -> 4.57 us
  transfers between devices with their start and end apart: 18 -> 18, of which waited for: 11 -> 8; matrix products, arithmetic and copies ran while one was open for 0% -> 0% of each run, Pallas kernels for 2% -> 12%
where the time goes in v3:
time: 121 us; the launch traced here: 120 us
  waiting for transfers between devices  50.9 us (42%)
  starting transfers between devices  37.3 us (31%)
  Pallas kernels  27.4 us (23%)
  local copies, waits for them, and re-layouts  4.57 us (4%)
    ppermute x9, waiting for transfers between devices, ring(): lax.ppermute(pieces[i], axis, [(s, (s + i) % size) for s in range(size)])  28.9 us
    ppermute x9, starting transfers between devices, ring(): lax.ppermute(pieces[i], axis, [(s, (s + i) % size) for s in range(size)])  17.4 us
    all_to_all x1, waiting for transfers between devices, per_device(): x_in = lax.all_to_all(x_part, ('x', 'core'), 0, 0, tiled=True)  15.4 us
    pallas_call x1, Pallas kernels, match(): pl.pallas_call(match_x_kernel, in_specs=[smem] * 3 + [vmem] * 3 + [hbm],...  11.8 us
    pallas_call x1, Pallas kernels, match(): pl.pallas_call(match_y_kernel, in_specs=[smem] * 3 + [vmem] * 2 + [hbm],...  8.36 us
    all_to_all x1, starting transfers between devices, per_device(): x_out = lax.all_to_all(x_sum, ('y', 'z'), 0, 0, tiled=True)  8.34 us
    pallas_call x5, Pallas kernels, vmem_call(): pl.pallas_call(kernel, in_specs=[vm] * (len(args) - after) + [anywhere] *...  7.21 us
    ppermute x7, starting transfers between devices, per_device(): arrived.append(lax.ppermute(y_parts[i], ('core', 'y'), perm))  7.18 us
  transfers between devices with their start and end apart: 18, of which 8 were waited for; matrix products, arithmetic and copies ran while one was open for 0% of the time, Pallas kernels for 12%

profile of v3, /device:TPU:0, one launch (start us, length us, event | category | flops | bytes accessed | tf_op | source)
XLA Modules:
  0.0 120.3 jit_solution(12606194965706178213)
XLA Ops:
  0.0 11.8 %match_x.1 = (bf16[8,784,256]{2,1,0:T(8,128)(2,1)}, bf16[12,512,384]{2,1,0:T(8,128)(2,1)}) custom-call(s32[12]{0:T(128)} %kidx_ref.3, s32[12]{0:T(128)} %bitcast.2, s32[12]{0:T(128)} %pos_ref.3, f32[8,41]{1,0:T(8,128)} %rtap_ref.1, f32[8,41]{1,0:T(8,128)} %ctap_ref.3, bf16[12,512]{1,0:T(8,128)(2,1)} %iv_ref.3, bf16[12,512,512]{2,1,0:T(8,128)(2,1)} %img_ref.1), custom_call_target="tpu_custom_call" | custom-call | flops 40000000000 | bytes 12582912 | tf_op jit(solution)/shard_map/match_x/pallas_call | solution.py:186
  11.8 4.4 %all-to-all-start = ((bf16[8,784,256]{2,1,0:T(8,128)(2,1)}), bf16[8,784,256]{2,1,0:T(8,128)(2,1)S(1)}, u32[]{:S(2)}, u32[]{:S(2)}) async-start(bf16[8,784,256]{2,1,0:T(8,128)(2,1)} %get-tuple-element.27), calls=%async_computation | async-start | bytes 6422528 | tf_op jit(solution)/shard_map/all_to_all | solution.py:370
  16.2 8.4 %match_y.1 = (bf16[784,256]{1,0:T(8,128)(2,1)}, bf16[784,256]{1,0:T(8,128)(2,1)}, bf16[784,256]{1,0:T(8,128)(2,1)}, bf16[784,256]{1,0:T(8,128)(2,1)}, bf16[784,2...) custom-call(s32[12]{0:T(128)} %kidx_ref.3, s32[12]{0:T(128)} %bitcast.3, ...), custom_call_target="tpu_custom_call" | custom-call | flops 40000000000 | bytes 12582912 | tf_op jit(solution)/shard_map/match_y/pallas_call | solution.py:208
  24.6 0.6 collective-permute-start
  25.1 1.6 %collective-permute-start.1 = (bf16[784,256]{1,0:T(8,128)(2,1)}, bf16[784,256]{1,0:T(8,128)(2,1)S(1)}, u32[]{:S(2)}, u32[]{:S(2)}) collective-permute-start(bf16[784,256]{1,0:T(8,128)(2,1)} %get-tuple-element.31), channel_id=1, source_target_pairs={{0,4},{4,8},{8,12},{12,0},{16,20},{20,24},{24,28},{28,16},{1,5},{5... | collective-permute-start | bytes 1204232 | tf_op jit(solution)/shard_map/ppermute | solution.py:369
  26.7 2.9 %collective-permute-start.2 = (bf16[784,256]{1,0:T(8,128)(2,1)}, bf16[784,256]{1,0:T(8,128)(2,1)}, u32[]{:S(2)}, u32[]{:S(2)}) collective-permute-start(bf16[784,256]{1,0:T(8,128)(2,1)} %get-tuple-element.32), channel_id=1, source_target_pairs={{0,8},{4,12},{8,0},{12,4},{16,24},{20,28},{24,16},{28,20},{1,9},{5... | collective-permute-start | bytes 1204232 | tf_op jit(solution)/shard_map/ppermute | solution.py:369
  29.7 0.0 collective-permute-start.3
  29.7 1.7 %collective-permute-start.4 = (bf16[784,256]{1,0:T(8,128)(2,1)}, bf16[784,256]{1,0:T(8,128)(2,1)}, u32[]{:S(2)}, u32[]{:S(2)}) collective-permute-start(bf16[784,256]{1,0:T(8,128)(2,1)} %get-tuple-element.34), channel_id=1, source_target_pairs={{0,12},{4,0},{8,4},{12,8},{16,28},{20,16},{24,20},{28,24},{1,13},{... | collective-permute-start | bytes 1204232 | tf_op jit(solution)/shard_map/ppermute | solution.py:369
  31.4 0.0 collective-permute-done.rest_1_
  31.4 0.0 copy-start.2
  31.4 0.8 copy-done.2
  32.2 0.3 collective-permute-start.5
  32.5 6.6 %collective-permute-done.1.rest_2_ = bf16[784,256]{1,0:T(8,128)(2,1)S(1)} collective-permute-done((bf16[784,256]{1,0:T(8,128)(2,1)}, bf16[784,256]{1,0:T(8,128)(2,1)S(1)}, u32[]{:S(2)}, u32[]{:S(2)}) %collective-permute-start.1) | collective-permute-done | bytes 401440 | tf_op jit(solution)/shard_map/ppermute | solution.py:369
  39.1 0.0 copy-start.4
  39.1 0.8 copy-done.4
  39.9 0.0 collective-permute-start.6
  39.9 15.4 %all-to-all-done.in_ref = bf16[8,784,256]{2,1,0:T(8,128)(2,1)S(1)} async-done(((bf16[8,784,256]{2,1,0:T(8,128)(2,1)}), bf16[8,784,256]{2,1,0:T(8,128)(2,1)S(1)}, u32[]{:S(2)}, u32[]{:S(2)}) %all-to-all-start) | async-done | bytes 3211296 | tf_op jit(solution)/shard_map/all_to_all | solution.py:370
  55.3 2.3 %gather_x.1.rest_8_ = bf16[16,272,256]{2,1,0:T(8,128)(2,1)S(1)} custom-call(bf16[8,784,256]{2,1,0:T(8,128)(2,1)S(1)} %all-to-all-done.in_ref), custom_call_target="tpu_custom_call" | custom-call | flops 40000000000 | bytes 6422528 | tf_op jit(solution)/shard_map/gather_x/pallas_call | solution.py:297
  57.7 0.0 copy-start
  57.7 1.4 %copy-done = bf16[16,272,256]{2,1,0:T(8,128)(2,1)} copy-done((bf16[16,272,256]{2,1,0:T(8,128)(2,1)}, bf16[16,272,256]{2,1,0:T(8,128)(2,1)S(1)}, u32[]{:S(2)}) %copy-start) | copy-done | bytes 2228248
  59.1 0.0 copy-start.3
  59.1 0.0 copy-start.5
  59.1 0.0 copy-start.6
  59.1 8.3 %all-to-all-start.1 = ((bf16[16,272,256]{2,1,0:T(8,128)(2,1)}), bf16[16,272,256]{2,1,0:T(8,128)(2,1)S(1)}, u32[]{:S(2)}, u32[]{:S(2)}) async-start(bf16[16,272,256]{2,1,0:T(8,128)(2,1)} %copy-done), calls=%async_computation.1 | async-start | bytes 4456448 | tf_op jit(solution)/shard_map/all_to_all | solution.py:388
  67.4 0.0 collective-permute-done.2.rest_3_
  67.4 0.0 collective-permute-done.3.rest_4_
  67.4 0.0 collective-permute-done.4.rest_5_
  67.4 0.0 collective-permute-done.5.rest_6_
  67.5 0.0 collective-permute-done.6.rest_7_
  67.5 0.0 copy-done.3
  67.5 0.0 copy-done.5
  67.5 0.0 copy-done.6
  67.5 0.0 copy-start.1
  67.5 1.6 %copy-done.1 = bf16[16,272,256]{2,1,0:T(8,128)(2,1)S(1)} copy-done((bf16[16,272,256]{2,1,0:T(8,128)(2,1)S(1)}, bf16[16,272,256]{2,1,0:T(8,128)(2,1)}, u32[]{:S(2)}) %copy-start.1) | copy-done | bytes 2228248
  69.1 3.5 %gather_y.1 = (bf16[64,16,256]{2,1,0:T(8,128)(2,1)S(1)}, bf16[64,16,256]{2,1,0:T(8,128)(2,1)S(1)}, bf16[64,16,256]{2,1,0:T(8,128)(2,1)S(1)}, bf16[64,16,256]{2,1,0:T(8,128)(2,1)S(1)}) custom-call(bf16[784,256]{1,0:T(8,128)(2,1)S(1)} %copy-done.6, bf16[784,256]{1,0:T(8,128)(2,1)S(1)} %copy-done.3, bf16[784,256]{1,0:T(8,128)(2,1)S(1)} %copy-done.5, ...), custom_call_target="tpu_custom_call" | custom-call | flops 40000000000 | bytes 10878976 | tf_op jit(solution)/shard_map/gather_y/pallas_call | solution.py:297
  72.6 1.7 %collective-permute-start.7 = (bf16[64,16,256]{2,1,0:T(8,128)(2,1)S(1)}, bf16[64,16,256]{2,1,0:T(8,128)(2,1)S(1)}, u32[]{:S(2)}, u32[]{:S(2)}) collective-permute-start(bf16[64,16,256]{2,1,0:T(8,128)(2,1)S(1)} %get-tuple-element.38), channel_id=1, source_target_pairs={{0,32},{32,64},{64,96},{96,0},{1,33},{33,65},{65,97},{97,1},{2,34}... | collective-permute-start | bytes 1572872 | tf_op jit(solution)/shard_map/ppermute | solution.py:353
  74.3 2.7 %collective-permute-start.8 = (bf16[64,16,256]{2,1,0:T(8,128)(2,1)S(1)}, bf16[64,16,256]{2,1,0:T(8,128)(2,1)S(1)}, u32[]{:S(2)}, u32[]{:S(2)}) collective-permute-start(bf16[64,16,256]{2,1,0:T(8,128)(2,1)S(1)} %get-tuple-element.39), channel_id=1, source_target_pairs={{0,64},{32,96},{64,0},{96,32},{1,65},{33,97},{65,1},{97,33},{2,66}... | collective-permute-start | bytes 1572872 | tf_op jit(solution)/shard_map/ppermute | solution.py:353
  77.0 1.5 %collective-permute-start.9 = (bf16[64,16,256]{2,1,0:T(8,128)(2,1)S(1)}, bf16[64,16,256]{2,1,0:T(8,128)(2,1)S(1)}, u32[]{:S(2)}, u32[]{:S(2)}) collective-permute-start(bf16[64,16,256]{2,1,0:T(8,128)(2,1)S(1)} %get-tuple-element.40), channel_id=1, source_target_pairs={{0,96},{32,0},{64,32},{96,64},{1,97},{33,1},{65,33},{97,65},{2,98}... | collective-permute-start | bytes 1572872 | tf_op jit(solution)/shard_map/ppermute | solution.py:353
  78.4 9.7 %collective-permute-done.7.refs_1_ = bf16[64,16,256]{2,1,0:T(8,128)(2,1)S(1)} collective-permute-done((bf16[64,16,256]{2,1,0:T(8,128)(2,1)S(1)}, bf16[64,16,256]{2,1,0:T(8,128)(2,1)S(1)}, u32[]{:S(2)}, u32[]{:S(2)}) %collective-permute-start.7) | collective-permute-done | bytes 524320 | tf_op jit(solution)/shard_map/ppermute | solution.py:353
  88.1 12.3 %collective-permute-done.8.refs_2_ = bf16[64,16,256]{2,1,0:T(8,128)(2,1)S(1)} collective-permute-done((bf16[64,16,256]{2,1,0:T(8,128)(2,1)S(1)}, bf16[64,16,256]{2,1,0:T(8,128)(2,1)S(1)}, u32[]{:S(2)}, u32[]{:S(2)}) %collective-permute-start.8) | collective-permute-done | bytes 524320 | tf_op jit(solution)/shard_map/ppermute | solution.py:353
  100.4 0.0 collective-permute-done.9.refs_3_
  100.4 0.3 ring_z.1
  100.7 1.7 %collective-permute-start.10 = (bf16[4,4,16,256]{3,2,1,0:T(8,128)(2,1)S(1)}, bf16[4,4,16,256]{3,2,1,0:T(8,128)(2,1)S(1)}, u32[]{:S(2)}, u32[]{:S(2)}) collective-permute-start(bf16[4,4,16,256]{3,2,1,0:T(8,128)(2,1)S(1)} %get-tuple-element.42), channel_id=1, source_target_pairs={{0,1},{1,2},{2,3},{3,0},{4,5},{5,6},{6,7},{7,4},{8,9},{9,10},{10,1... | collective-permute-start | bytes 393224 | tf_op jit(solution)/shard_map/ppermute | solution.py:353
  102.4 2.7 %collective-permute-start.11 = (bf16[4,4,16,256]{3,2,1,0:T(8,128)(2,1)S(1)}, bf16[4,4,16,256]{3,2,1,0:T(8,128)(2,1)S(1)}, u32[]{:S(2)}, u32[]{:S(2)}) collective-permute-start(bf16[4,4,16,256]{3,2,1,0:T(8,128)(2,1)S(1)} %get-tuple-element.43), channel_id=1, source_target_pairs={{0,2},{1,3},{2,0},{3,1},{4,6},{5,7},{6,4},{7,5},{8,10},{9,11},{10,... | collective-permute-start | bytes 393224 | tf_op jit(solution)/shard_map/ppermute | solution.py:353
  105.1 1.5 %collective-permute-start.12 = (bf16[4,4,16,256]{3,2,1,0:T(8,128)(2,1)S(1)}, bf16[4,4,16,256]{3,2,1,0:T(8,128)(2,1)S(1)}, u32[]{:S(2)}, u32[]{:S(2)}) collective-permute-start(bf16[4,4,16,256]{3,2,1,0:T(8,128)(2,1)S(1)} %get-tuple-element.44), channel_id=1, source_target_pairs={{0,3},{1,0},{2,1},{3,2},{4,7},{5,4},{6,5},{7,6},{8,11},{9,8},{10,9... | collective-permute-start | bytes 393224 | tf_op jit(solution)/shard_map/ppermute | solution.py:353
  106.6 1.4 %collective-permute-done.10.refs_1_ = bf16[4,4,16,256]{3,2,1,0:T(8,128)(2,1)S(1)} collective-permute-done((bf16[4,4,16,256]{3,2,1,0:T(8,128)(2,1)S(1)}, bf16[4,4,16,256]{3,2,1,0:T(8,128)(2,1)S(1)}, u32[]{:S(2)}, u32[]{:S(2)}) %collective-permute-start.10) | collective-permute-done | bytes 131104 | tf_op jit(solution)/shard_map/ppermute | solution.py:353
  108.0 2.6 %collective-permute-done.11.refs_2_ = bf16[4,4,16,256]{3,2,1,0:T(8,128)(2,1)S(1)} collective-permute-done((bf16[4,4,16,256]{3,2,1,0:T(8,128)(2,1)S(1)}, bf16[4,4,16,256]{3,2,1,0:T(8,128)(2,1)S(1)}, u32[]{:S(2)}, u32[]{:S(2)}) %collective-permute-start.11) | collective-permute-done | bytes 131104 | tf_op jit(solution)/shard_map/ppermute | solution.py:353
  110.6 0.0 collective-permute-done.12.refs_3_
  110.6 0.1 ring_y.1
  110.7 1.6 %collective-permute-start.13 = (f32[4,16,256]{2,1,0:T(8,128)S(1)}, f32[4,16,256]{2,1,0:T(8,128)S(1)}, u32[]{:S(2)}, u32[]{:S(2)}) collective-permute-start(f32[4,16,256]{2,1,0:T(8,128)S(1)} %get-tuple-element.46), channel_id=1, source_target_pairs={{0,4},{4,8},{8,12},{12,0},{1,5},{5,9},{9,13},{13,1},{2,6},{6,10},{... | collective-permute-start | bytes 196616 | tf_op jit(solution)/shard_map/ppermute | solution.py:353
  112.3 2.7 %collective-permute-start.14 = (f32[4,16,256]{2,1,0:T(8,128)S(1)}, f32[4,16,256]{2,1,0:T(8,128)S(1)}, u32[]{:S(2)}, u32[]{:S(2)}) collective-permute-start(f32[4,16,256]{2,1,0:T(8,128)S(1)} %get-tuple-element.47), channel_id=1, source_target_pairs={{0,8},{4,12},{8,0},{12,4},{1,9},{5,13},{9,1},{13,5},{2,10},{6,14},... | collective-permute-start | bytes 196616 | tf_op jit(solution)/shard_map/ppermute | solution.py:353
  114.9 1.5 %collective-permute-start.15 = (f32[4,16,256]{2,1,0:T(8,128)S(1)}, f32[4,16,256]{2,1,0:T(8,128)S(1)}, u32[]{:S(2)}, u32[]{:S(2)}) collective-permute-start(f32[4,16,256]{2,1,0:T(8,128)S(1)} %get-tuple-element.48), channel_id=1, source_target_pairs={{0,12},{4,0},{8,4},{12,8},{1,13},{5,1},{9,5},{13,9},{2,14},{6,2},{... | collective-permute-start | bytes 196616 | tf_op jit(solution)/shard_map/ppermute | solution.py:353
  116.4 0.0 collective-permute-done.13.rest_1_
  116.4 1.6 %collective-permute-done.14.rest_2_ = f32[4,16,256]{2,1,0:T(8,128)S(1)} collective-permute-done((f32[4,16,256]{2,1,0:T(8,128)S(1)}, f32[4,16,256]{2,1,0:T(8,128)S(1)}, u32[]{:S(2)}, u32[]{:S(2)}) %collective-permute-start.14) | collective-permute-done | bytes 65568 | tf_op jit(solution)/shard_map/ppermute | solution.py:353
  118.0 1.2 collective-permute-done.15.rest_3_
  119.2 0.0 all-to-all-done.1.x_ref
  119.2 1.1 finish.1
Async XLA Ops:
  11.8 43.5 %all-to-all-start = ((bf16[8,784,256]{2,1,0:T(8,128)(2,1)}), bf16[8,784,256]{2,1,0:T(8,128)(2,1)S(1)}, u32[]{:S(2)}, u32[]{:S(2)}) async-start(bf16[8,784,256]{2,1,0:T(8,128)(2,1)} %get-tuple-element.27), calls=%async_computation | async-start | bytes 6422528 | tf_op jit(solution)/shard_map/all_to_all | solution.py:370
  24.6 6.9 %collective-permute-start = (bf16[784,256]{1,0:T(8,128)(2,1)}, bf16[784,256]{1,0:T(8,128)(2,1)S(1)}, u32[]{:S(2)}, u32[]{:S(2)}) collective-permute-start(bf16[784,256]{1,0:T(8,128)(2,1)} %get-tuple-element.30), channel_id=1, source_target_pairs={{0,16},{4,20},{8,24},{12,28},{16,0},{20,4},{24,8},{28,12},{1,17},{... | collective-permute-start | bytes 1204232 | tf_op jit(solution)/shard_map/ppermute | solution.py:369
  25.1 14.0 %collective-permute-start.1 = (bf16[784,256]{1,0:T(8,128)(2,1)}, bf16[784,256]{1,0:T(8,128)(2,1)S(1)}, u32[]{:S(2)}, u32[]{:S(2)}) collective-permute-start(bf16[784,256]{1,0:T(8,128)(2,1)} %get-tuple-element.31), channel_id=1, source_target_pairs={{0,4},{4,8},{8,12},{12,0},{16,20},{20,24},{24,28},{28,16},{1,5},{5... | collective-permute-start | bytes 1204232 | tf_op jit(solution)/shard_map/ppermute | solution.py:369
  26.7 40.7 %collective-permute-start.2 = (bf16[784,256]{1,0:T(8,128)(2,1)}, bf16[784,256]{1,0:T(8,128)(2,1)}, u32[]{:S(2)}, u32[]{:S(2)}) collective-permute-start(bf16[784,256]{1,0:T(8,128)(2,1)} %get-tuple-element.32), channel_id=1, source_target_pairs={{0,8},{4,12},{8,0},{12,4},{16,24},{20,28},{24,16},{28,20},{1,9},{5... | collective-permute-start | bytes 1204232 | tf_op jit(solution)/shard_map/ppermute | solution.py:369
  29.7 37.8 %collective-permute-start.3 = (bf16[784,256]{1,0:T(8,128)(2,1)}, bf16[784,256]{1,0:T(8,128)(2,1)}, u32[]{:S(2)}, u32[]{:S(2)}) collective-permute-start(bf16[784,256]{1,0:T(8,128)(2,1)} %get-tuple-element.33), channel_id=1, source_target_pairs={{0,24},{4,28},{8,16},{12,20},{16,8},{20,12},{24,0},{28,4},{1,25},{... | collective-permute-start | bytes 1204232 | tf_op jit(solution)/shard_map/ppermute | solution.py:369
  29.7 37.8 %collective-permute-start.4 = (bf16[784,256]{1,0:T(8,128)(2,1)}, bf16[784,256]{1,0:T(8,128)(2,1)}, u32[]{:S(2)}, u32[]{:S(2)}) collective-permute-start(bf16[784,256]{1,0:T(8,128)(2,1)} %get-tuple-element.34), channel_id=1, source_target_pairs={{0,12},{4,0},{8,4},{12,8},{16,28},{20,16},{24,20},{28,24},{1,13},{... | collective-permute-start | bytes 1204232 | tf_op jit(solution)/shard_map/ppermute | solution.py:369
  31.4 0.8 copy-start.2
  32.2 35.3 %collective-permute-start.5 = (bf16[784,256]{1,0:T(8,128)(2,1)}, bf16[784,256]{1,0:T(8,128)(2,1)}, u32[]{:S(2)}, u32[]{:S(2)}) collective-permute-start(bf16[784,256]{1,0:T(8,128)(2,1)} %get-tuple-element.35), channel_id=1, source_target_pairs={{0,20},{4,24},{8,28},{12,16},{16,4},{20,8},{24,12},{28,0},{1,21},{... | collective-permute-start | bytes 1204232 | tf_op jit(solution)/shard_map/ppermute | solution.py:369
  39.1 0.8 copy-start.4
  39.9 27.5 %collective-permute-start.6 = (bf16[784,256]{1,0:T(8,128)(2,1)}, bf16[784,256]{1,0:T(8,128)(2,1)}, u32[]{:S(2)}, u32[]{:S(2)}) collective-permute-start(bf16[784,256]{1,0:T(8,128)(2,1)} %get-tuple-element.36), channel_id=1, source_target_pairs={{0,28},{4,16},{8,20},{12,24},{16,12},{20,0},{24,4},{28,8},{1,29},{... | collective-permute-start | bytes 1204232 | tf_op jit(solution)/shard_map/ppermute | solution.py:369
  57.7 1.4 %copy-start = (bf16[16,272,256]{2,1,0:T(8,128)(2,1)}, bf16[16,272,256]{2,1,0:T(8,128)(2,1)S(1)}, u32[]{:S(2)}) copy-start(bf16[16,272,256]{2,1,0:T(8,128)(2,1)S(1)} %gather_x.1.rest_8_) | copy-start | bytes 6684676
  59.1 8.4 %copy-start.3 = (bf16[784,256]{1,0:T(8,128)(2,1)S(1)}, bf16[784,256]{1,0:T(8,128)(2,1)}, u32[]{:S(2)}) copy-start(bf16[784,256]{1,0:T(8,128)(2,1)} %copy-done.2) | copy-start | bytes 1204228
  59.1 8.4 %copy-start.5 = (bf16[784,256]{1,0:T(8,128)(2,1)S(1)}, bf16[784,256]{1,0:T(8,128)(2,1)}, u32[]{:S(2)}) copy-start(bf16[784,256]{1,0:T(8,128)(2,1)} %copy-done.4) | copy-start | bytes 1204228
  59.1 8.4 %copy-start.6 = (bf16[784,256]{1,0:T(8,128)(2,1)S(1)}, bf16[784,256]{1,0:T(8,128)(2,1)}, u32[]{:S(2)}) copy-start(bf16[784,256]{1,0:T(8,128)(2,1)} %get-tuple-element.29.rest_0_) | copy-start | bytes 1204228
  59.1 60.1 %all-to-all-start.1 = ((bf16[16,272,256]{2,1,0:T(8,128)(2,1)}), bf16[16,272,256]{2,1,0:T(8,128)(2,1)S(1)}, u32[]{:S(2)}, u32[]{:S(2)}) async-start(bf16[16,272,256]{2,1,0:T(8,128)(2,1)} %copy-done), calls=%async_computation.1 | async-start | bytes 4456448 | tf_op jit(solution)/shard_map/all_to_all | solution.py:388
  67.5 1.6 %copy-start.1 = (bf16[16,272,256]{2,1,0:T(8,128)(2,1)S(1)}, bf16[16,272,256]{2,1,0:T(8,128)(2,1)}, u32[]{:S(2)}) copy-start(bf16[16,272,256]{2,1,0:T(8,128)(2,1)} %copy-done) | copy-start | bytes 6684676
  72.6 15.5 %collective-permute-start.7 = (bf16[64,16,256]{2,1,0:T(8,128)(2,1)S(1)}, bf16[64,16,256]{2,1,0:T(8,128)(2,1)S(1)}, u32[]{:S(2)}, u32[]{:S(2)}) collective-permute-start(bf16[64,16,256]{2,1,0:T(8,128)(2,1)S(1)} %get-tuple-element.38), channel_id=1, source_target_pairs={{0,32},{32,64},{64,96},{96,0},{1,33},{33,65},{65,97},{97,1},{2,34}... | collective-permute-start | bytes 1572872 | tf_op jit(solution)/shard_map/ppermute | solution.py:353
  74.3 26.1 %collective-permute-start.8 = (bf16[64,16,256]{2,1,0:T(8,128)(2,1)S(1)}, bf16[64,16,256]{2,1,0:T(8,128)(2,1)S(1)}, u32[]{:S(2)}, u32[]{:S(2)}) collective-permute-start(bf16[64,16,256]{2,1,0:T(8,128)(2,1)S(1)} %get-tuple-element.39), channel_id=1, source_target_pairs={{0,64},{32,96},{64,0},{96,32},{1,65},{33,97},{65,1},{97,33},{2,66}... | collective-permute-start | bytes 1572872 | tf_op jit(solution)/shard_map/ppermute | solution.py:353
  77.0 23.5 %collective-permute-start.9 = (bf16[64,16,256]{2,1,0:T(8,128)(2,1)S(1)}, bf16[64,16,256]{2,1,0:T(8,128)(2,1)S(1)}, u32[]{:S(2)}, u32[]{:S(2)}) collective-permute-start(bf16[64,16,256]{2,1,0:T(8,128)(2,1)S(1)} %get-tuple-element.40), channel_id=1, source_target_pairs={{0,96},{32,0},{64,32},{96,64},{1,97},{33,1},{65,33},{97,65},{2,98}... | collective-permute-start | bytes 1572872 | tf_op jit(solution)/shard_map/ppermute | solution.py:353
  100.7 7.3 %collective-permute-start.10 = (bf16[4,4,16,256]{3,2,1,0:T(8,128)(2,1)S(1)}, bf16[4,4,16,256]{3,2,1,0:T(8,128)(2,1)S(1)}, u32[]{:S(2)}, u32[]{:S(2)}) collective-permute-start(bf16[4,4,16,256]{3,2,1,0:T(8,128)(2,1)S(1)} %get-tuple-element.42), channel_id=1, source_target_pairs={{0,1},{1,2},{2,3},{3,0},{4,5},{5,6},{6,7},{7,4},{8,9},{9,10},{10,1... | collective-permute-start | bytes 393224 | tf_op jit(solution)/shard_map/ppermute | solution.py:353
  102.4 8.2 %collective-permute-start.11 = (bf16[4,4,16,256]{3,2,1,0:T(8,128)(2,1)S(1)}, bf16[4,4,16,256]{3,2,1,0:T(8,128)(2,1)S(1)}, u32[]{:S(2)}, u32[]{:S(2)}) collective-permute-start(bf16[4,4,16,256]{3,2,1,0:T(8,128)(2,1)S(1)} %get-tuple-element.43), channel_id=1, source_target_pairs={{0,2},{1,3},{2,0},{3,1},{4,6},{5,7},{6,4},{7,5},{8,10},{9,11},{10,... | collective-permute-start | bytes 393224 | tf_op jit(solution)/shard_map/ppermute | solution.py:353
  105.1 5.5 %collective-permute-start.12 = (bf16[4,4,16,256]{3,2,1,0:T(8,128)(2,1)S(1)}, bf16[4,4,16,256]{3,2,1,0:T(8,128)(2,1)S(1)}, u32[]{:S(2)}, u32[]{:S(2)}) collective-permute-start(bf16[4,4,16,256]{3,2,1,0:T(8,128)(2,1)S(1)} %get-tuple-element.44), channel_id=1, source_target_pairs={{0,3},{1,0},{2,1},{3,2},{4,7},{5,4},{6,5},{7,6},{8,11},{9,8},{10,9... | collective-permute-start | bytes 393224 | tf_op jit(solution)/shard_map/ppermute | solution.py:353
  110.7 5.7 %collective-permute-start.13 = (f32[4,16,256]{2,1,0:T(8,128)S(1)}, f32[4,16,256]{2,1,0:T(8,128)S(1)}, u32[]{:S(2)}, u32[]{:S(2)}) collective-permute-start(f32[4,16,256]{2,1,0:T(8,128)S(1)} %get-tuple-element.46), channel_id=1, source_target_pairs={{0,4},{4,8},{8,12},{12,0},{1,5},{5,9},{9,13},{13,1},{2,6},{6,10},{... | collective-permute-start | bytes 196616 | tf_op jit(solution)/shard_map/ppermute | solution.py:353
  112.3 5.8 %collective-permute-start.14 = (f32[4,16,256]{2,1,0:T(8,128)S(1)}, f32[4,16,256]{2,1,0:T(8,128)S(1)}, u32[]{:S(2)}, u32[]{:S(2)}) collective-permute-start(f32[4,16,256]{2,1,0:T(8,128)S(1)} %get-tuple-element.47), channel_id=1, source_target_pairs={{0,8},{4,12},{8,0},{12,4},{1,9},{5,13},{9,1},{13,5},{2,10},{6,14},... | collective-permute-start | bytes 196616 | tf_op jit(solution)/shard_map/ppermute | solution.py:353
  114.9 4.3 %collective-permute-start.15 = (f32[4,16,256]{2,1,0:T(8,128)S(1)}, f32[4,16,256]{2,1,0:T(8,128)S(1)}, u32[]{:S(2)}, u32[]{:S(2)}) collective-permute-start(f32[4,16,256]{2,1,0:T(8,128)S(1)} %get-tuple-element.48), channel_id=1, source_target_pairs={{0,12},{4,0},{8,4},{12,8},{1,13},{5,1},{9,5},{13,9},{2,14},{6,2},{... | collective-permute-start | bytes 196616 | tf_op jit(solution)/shard_map/ppermute | solution.py:353

commit v4 on v3

--- a/solution.py
+++ b/solution.py
@@ -24,6 +24,8 @@
 
 
 GROUP = 4
+RING_ORDER = (2, 1, 3)
+AHEAD = 3
 
 
 def toeplitz(row, length):
@@ -79,7 +81,7 @@
     rows, width = side // VISITS, side // 2
     top = blocks * rows
     loads = [pltpu.make_async_copy(img_ref.at[b], image.at[b], in_sem.at[b]) for b in range(blocks)]
-    for load in loads:
+    for load in loads[:AHEAD]:
         load.start()
 
     places = combo_rows(dest_ref, pos_ref, blocks)
@@ -103,6 +105,8 @@
         put_band(cband, ctab.at[k], 0, 0)
         weight = lane_weights(ivt, b, width)
         loads[b].wait()
+        if b + AHEAD < blocks:
+            loads[b + AHEAD].start()
         mid = jnp.dot(rband[...], image[b], preferred_element_type=F32).astype(BF)
         mids[b] = mid[:, LANE:]
         stores.append(pltpu.make_async_copy(mids.at[b], mid_ref.at[b], mid_sem.at[b]))
@@ -130,7 +134,7 @@
     tiles, rows, width = side // LANE, side // VISITS, side // 2
     top = blocks * rows
     loads = [pltpu.make_async_copy(mid_ref.at[b], mids.at[b], in_sem.at[b]) for b in range(blocks)]
-    for load in loads:
+    for load in loads[:AHEAD]:
         load.start()
 
     places = combo_rows(dest_ref, pos_ref, blocks)
@@ -147,6 +151,8 @@
         put_band(cband, ctab.at[kidx_ref[b]], tiles - 3, tiles // 2)
         weight = lane_weights(ivt, b, width)
         loads[b].wait()
+        if b + AHEAD < blocks:
+            loads[b + AHEAD].start()
         matched = jnp.dot(mids[b], cband[...], preferred_element_type=F32)
         whole[b % 2] = (matched * weight).astype(BF)
         for i, (dc, dy) in enumerate(Y_OFFSETS):
@@ -240,10 +246,11 @@
     return line
 
 
-def gather_x_kernel(in_ref, out_hbm, acc, flat, smem, sem, out_ref, out_sem):
+def gather_x_kernel(in_ref, out_hbm, done_ref, acc, flat, smem, sem, out_ref, out_sem):
     rows, width = acc.shape[1:]
     blocks = (in_ref.shape[1] - SUB) // rows
     top = blocks * rows
+    done_ref[...] = jnp.zeros_like(done_ref)
     line = read_places([in_ref[v, top:, LANE:] for v in range(VISITS)], flat, smem, sem)
     acc[...] = jnp.zeros_like(acc)
     for v in range(VISITS):
@@ -290,6 +297,7 @@
 
 
 def vmem_call(kernel, name, out_shape, args, scratch=(), after=0, flops=0, hbm_out=False):
+    hbm_out = hbm_out or jax.tree.map(lambda _: False, out_shape)
     vm = pl.BlockSpec(memory_space=pltpu.VMEM)
     anywhere = pl.BlockSpec(memory_space=pl.ANY)
     size = sum(a.size * a.dtype.itemsize for a in args)
@@ -297,7 +305,7 @@
     return pl.pallas_call(
         kernel,
         in_specs=[vm] * (len(args) - after) + [anywhere] * after,
-        out_specs=jax.tree.map(lambda _: pl.BlockSpec(memory_space=pltpu.HBM) if hbm_out else vm, out_shape),
+        out_specs=jax.tree.map(lambda far: pl.BlockSpec(memory_space=pltpu.HBM) if far else vm, hbm_out),
         out_shape=out_shape,
         scratch_shapes=list(scratch),
         compiler_params=pltpu.CompilerParams(vmem_limit_bytes=32 << 20),
@@ -338,8 +346,8 @@
             total += x_ref[s, p * rows : (p + 1) * rows].astype(F32)
         for j in range(width // LANE):
             out_ref[p, :, j * LANE : (j + 1) * LANE] = total[:, j * LANE : (j + 1) * LANE] * turned
-    for i in range(NY):
-        at = pl.ds(pl.multiple_of(lax.rem(my - i + NY, NY) * SUB, SUB), SUB)
+    for i, step in enumerate((0,) + RING_ORDER):
+        at = pl.ds(pl.multiple_of(lax.rem(my - step + NY, NY) * SUB, SUB), SUB)
         for p in range(POS):
             scale = inv[p, at, :]
             for j in range(width // LANE):
@@ -349,7 +357,7 @@
 
 def ring(pieces, axis, size):
     out = [pieces[0]]
-    for i in range(1, size):
+    for i in RING_ORDER:
         out.append(lax.ppermute(pieces[i], axis, [(s, (s + i) % size) for s in range(size)]))
     return out
 
@@ -380,10 +388,10 @@
         pltpu.VMEM((TILES, POS * rows + SUB, width), BF),
         pltpu.SemaphoreType.DMA((TILES // GROUP,)),
     ]
-    x_sum = vmem_call(
-        gather_x_kernel, "gather_x", shape((TILES, POS * rows + SUB, width), BF), (x_in,), x_scratch, 0, GX, True
+    x_sum, x_done = vmem_call(
+        gather_x_kernel, "gather_x", (shape((TILES, POS * rows + SUB, width), BF), shape((8, LANE), F32)), (x_in,), x_scratch, 0, GX, (True, False)
     )
-    mine = vmem_call(gather_y_kernel, "gather_y", [shape((COUNT, SUB, width), BF)] * NX, (*arrived, x_sum), y_scratch, 1, GY, True)
+    mine = vmem_call(gather_y_kernel, "gather_y", [shape((COUNT, SUB, width), BF)] * NX, (*arrived, x_done), y_scratch, 1, GY, [True] * NX)
     along_x = ring(mine, "x", NX)
     x_out = lax.all_to_all(x_sum, ("y", "z"), 0, 0, tiled=True)
     along_z = vmem_call(

time: 121 us -> 119 us (0.983)
  waiting for transfers between devices: 50.9 us -> 48.6 us
  starting transfers between devices: 37.3 us -> 39.3 us
  local copies, waits for them, and re-layouts: 4.57 us -> 2.95 us
    ppermute x9, waiting for transfers between devices: 28.9 us -> 26.6 us  [ring(): lax.ppermute(pieces[i], axis, [(s, (s + i) % size) for s in range(size)])]
    ppermute x9, starting transfers between devices: 17.4 us -> 19.4 us  [ring(): lax.ppermute(pieces[i], axis, [(s, (s + i) % size) for s in range(size)])]
    unnamed x14 -> x12, local copies, waits for them, and re-layouts: 4.57 us -> 2.95 us
where the time goes in v4:
time: 119 us; the launch traced here: 118 us
  waiting for transfers between devices  48.6 us (41%)
  starting transfers between devices  39.3 us (33%)
  Pallas kernels  27.4 us (23%)
  local copies, waits for them, and re-layouts  2.95 us (2%)
    ppermute x9, waiting for transfers between devices, ring(): lax.ppermute(pieces[i], axis, [(s, (s + i) % size) for s in range(size)])  26.6 us
    ppermute x9, starting transfers between devices, ring(): lax.ppermute(pieces[i], axis, [(s, (s + i) % size) for s in range(size)])  19.4 us
    all_to_all x1, waiting for transfers between devices, per_device(): x_in = lax.all_to_all(x_part, ('x', 'core'), 0, 0, tiled=True)  15.4 us
    pallas_call x1, Pallas kernels, match(): pl.pallas_call(match_x_kernel, in_specs=[smem] * 3 + [vmem] * 3 + [hbm],...  11.8 us
    pallas_call x1, Pallas kernels, match(): pl.pallas_call(match_y_kernel, in_specs=[smem] * 3 + [vmem] * 2 + [hbm],...  8.38 us
    all_to_all x1, starting transfers between devices, per_device(): x_out = lax.all_to_all(x_sum, ('y', 'z'), 0, 0, tiled=True)  8.36 us
    pallas_call x5, Pallas kernels, vmem_call(): pl.pallas_call(kernel, in_specs=[vm] * (len(args) - after) + [anywhere] *...  7.21 us
    ppermute x7, starting transfers between devices, per_device(): arrived.append(lax.ppermute(y_parts[i], ('core', 'y'), perm))  7.17 us
  transfers between devices with their start and end apart: 18, of which 8 were waited for; matrix products, arithmetic and copies ran while one was open for 0% of the time, Pallas kernels for 12%

profile of v4, /device:TPU:0, one launch (start us, length us, event | category | flops | bytes accessed | tf_op | source)
XLA Modules:
  0.0 118.4 jit_solution(2423561292424595665)
XLA Ops:
  0.0 11.8 %match_x.1 = (bf16[8,784,256]{2,1,0:T(8,128)(2,1)}, bf16[12,512,384]{2,1,0:T(8,128)(2,1)}) custom-call(s32[12]{0:T(128)} %kidx_ref.3, s32[12]{0:T(128)} %bitcast.2, s32[12]{0:T(128)} %pos_ref.3, f32[8,41]{1,0:T(8,128)} %rtap_ref.1, f32[8,41]{1,0:T(8,128)} %ctap_ref.3, bf16[12,512]{1,0:T(8,128)(2,1)} %iv_ref.3, bf16[12,512,512]{2,1,0:T(8,128)(2,1)} %img_ref.1), custom_call_target="tpu_custom_call" | custom-call | flops 40000000000 | bytes 12582912 | tf_op jit(solution)/shard_map/match_x/pallas_call | solution.py:192
  11.8 4.4 %all-to-all-start = ((bf16[8,784,256]{2,1,0:T(8,128)(2,1)}), bf16[8,784,256]{2,1,0:T(8,128)(2,1)S(1)}, u32[]{:S(2)}, u32[]{:S(2)}) async-start(bf16[8,784,256]{2,1,0:T(8,128)(2,1)} %get-tuple-element.29), calls=%async_computation | async-start | bytes 6422528 | tf_op jit(solution)/shard_map/all_to_all | solution.py:378
  16.2 8.4 %match_y.1 = (bf16[784,256]{1,0:T(8,128)(2,1)}, bf16[784,256]{1,0:T(8,128)(2,1)}, bf16[784,256]{1,0:T(8,128)(2,1)}, bf16[784,256]{1,0:T(8,128)(2,1)}, bf16[784,2...) custom-call(s32[12]{0:T(128)} %kidx_ref.3, s32[12]{0:T(128)} %bitcast.3, ...), custom_call_target="tpu_custom_call" | custom-call | flops 40000000000 | bytes 12582912 | tf_op jit(solution)/shard_map/match_y/pallas_call | solution.py:214
  24.6 0.6 collective-permute-start
  25.2 1.6 %collective-permute-start.1 = (bf16[784,256]{1,0:T(8,128)(2,1)}, bf16[784,256]{1,0:T(8,128)(2,1)S(1)}, u32[]{:S(2)}, u32[]{:S(2)}) collective-permute-start(bf16[784,256]{1,0:T(8,128)(2,1)} %get-tuple-element.34), channel_id=1, source_target_pairs={{0,4},{4,8},{8,12},{12,0},{16,20},{20,24},{24,28},{28,16},{1,5},{5... | collective-permute-start | bytes 1204232 | tf_op jit(solution)/shard_map/ppermute | solution.py:377
  26.8 2.9 %collective-permute-start.2 = (bf16[784,256]{1,0:T(8,128)(2,1)}, bf16[784,256]{1,0:T(8,128)(2,1)}, u32[]{:S(2)}, u32[]{:S(2)}) collective-permute-start(bf16[784,256]{1,0:T(8,128)(2,1)} %get-tuple-element.35), channel_id=1, source_target_pairs={{0,8},{4,12},{8,0},{12,4},{16,24},{20,28},{24,16},{28,20},{1,9},{5... | collective-permute-start | bytes 1204232 | tf_op jit(solution)/shard_map/ppermute | solution.py:377
  29.7 0.0 collective-permute-start.3
  29.7 1.6 %collective-permute-start.4 = (bf16[784,256]{1,0:T(8,128)(2,1)}, bf16[784,256]{1,0:T(8,128)(2,1)}, u32[]{:S(2)}, u32[]{:S(2)}) collective-permute-start(bf16[784,256]{1,0:T(8,128)(2,1)} %get-tuple-element.37), channel_id=1, source_target_pairs={{0,12},{4,0},{8,4},{12,8},{16,28},{20,16},{24,20},{28,24},{1,13},{... | collective-permute-start | bytes 1204232 | tf_op jit(solution)/shard_map/ppermute | solution.py:377
  31.3 0.0 collective-permute-done.rest_1_
  31.3 0.0 copy-start.1
  31.3 0.8 copy-done.1
  32.0 0.5 collective-permute-start.5
  32.6 6.6 %collective-permute-done.1.rest_2_ = bf16[784,256]{1,0:T(8,128)(2,1)S(1)} collective-permute-done((bf16[784,256]{1,0:T(8,128)(2,1)}, bf16[784,256]{1,0:T(8,128)(2,1)S(1)}, u32[]{:S(2)}, u32[]{:S(2)}) %collective-permute-start.1) | collective-permute-done | bytes 401440 | tf_op jit(solution)/shard_map/ppermute | solution.py:377
  39.2 0.0 copy-start.3
  39.2 0.8 copy-done.3
  39.9 0.0 collective-permute-start.6
  40.0 15.4 %all-to-all-done.in_ref = bf16[8,784,256]{2,1,0:T(8,128)(2,1)S(1)} async-done(((bf16[8,784,256]{2,1,0:T(8,128)(2,1)}), bf16[8,784,256]{2,1,0:T(8,128)(2,1)S(1)}, u32[]{:S(2)}, u32[]{:S(2)}) %all-to-all-start) | async-done | bytes 3211296 | tf_op jit(solution)/shard_map/all_to_all | solution.py:378
  55.3 2.3 %gather_x.1 = (bf16[16,272,256]{2,1,0:T(8,128)(2,1)S(1)}, f32[8,128]{1,0:T(8,128)S(1)}) custom-call(bf16[8,784,256]{2,1,0:T(8,128)(2,1)S(1)} %all-to-all-done.in_ref), custom_call_target="tpu_custom_call" | custom-call | flops 40000000000 | bytes 6422528 | tf_op jit(solution)/shard_map/gather_x/pallas_call | solution.py:305
  57.7 0.0 copy-start
  57.7 1.4 %copy-done = bf16[16,272,256]{2,1,0:T(8,128)(2,1)} copy-done((bf16[16,272,256]{2,1,0:T(8,128)(2,1)}, bf16[16,272,256]{2,1,0:T(8,128)(2,1)S(1)}, u32[]{:S(2)}) %copy-start) | copy-done | bytes 2228248
  59.1 0.0 copy-start.2
  59.1 0.0 copy-start.4
  59.1 0.0 copy-start.5
  59.1 8.4 %all-to-all-start.1 = ((bf16[16,272,256]{2,1,0:T(8,128)(2,1)}), bf16[16,272,256]{2,1,0:T(8,128)(2,1)S(1)}, u32[]{:S(2)}, u32[]{:S(2)}) async-start(bf16[16,272,256]{2,1,0:T(8,128)(2,1)} %copy-done), calls=%async_computation.1 | async-start | bytes 4456448 | tf_op jit(solution)/shard_map/all_to_all | solution.py:396
  67.4 0.0 collective-permute-done.2.rest_3_
  67.5 0.0 collective-permute-done.3.rest_4_
  67.5 0.0 collective-permute-done.4.rest_5_
  67.5 0.0 collective-permute-done.5.rest_6_
  67.5 0.0 collective-permute-done.6.rest_7_
  67.5 0.0 copy-done.2
  67.5 0.0 copy-done.4
  67.5 0.0 copy-done.5
  67.5 3.5 %gather_y.1 = (bf16[64,16,256]{2,1,0:T(8,128)(2,1)S(1)}, bf16[64,16,256]{2,1,0:T(8,128)(2,1)S(1)}, bf16[64,16,256]{2,1,0:T(8,128)(2,1)S(1)}, bf16[64,16,256]{2,1,0:T(8,128)(2,1)S(1)}) custom-call(bf16[784,256]{1,0:T(8,128)(2,1)S(1)} %copy-done.5, bf16[784,256]{1,0:T(8,128)(2,1)S(1)} %copy-done.2, bf16[784,256]{1,0:T(8,128)(2,1)S(1)} %copy-done.4, ...), custom_call_target="tpu_custom_call" | custom-call | flops 40000000000 | bytes 6430720 | tf_op jit(solution)/shard_map/gather_y/pallas_call | solution.py:305
  71.0 3.2 %collective-permute-start.7 = (bf16[64,16,256]{2,1,0:T(8,128)(2,1)S(1)}, bf16[64,16,256]{2,1,0:T(8,128)(2,1)S(1)}, u32[]{:S(2)}, u32[]{:S(2)}) collective-permute-start(bf16[64,16,256]{2,1,0:T(8,128)(2,1)S(1)} %get-tuple-element.42), channel_id=1, source_target_pairs={{0,64},{32,96},{64,0},{96,32},{1,65},{33,97},{65,1},{97,33},{2,66}... | collective-permute-start | bytes 1572872 | tf_op jit(solution)/shard_map/ppermute | solution.py:361
  74.2 0.6 collective-permute-start.8
  74.8 2.7 %collective-permute-start.9 = (bf16[64,16,256]{2,1,0:T(8,128)(2,1)S(1)}, bf16[64,16,256]{2,1,0:T(8,128)(2,1)S(1)}, u32[]{:S(2)}, u32[]{:S(2)}) collective-permute-start(bf16[64,16,256]{2,1,0:T(8,128)(2,1)S(1)} %get-tuple-element.44), channel_id=1, source_target_pairs={{0,96},{32,0},{64,32},{96,64},{1,97},{33,1},{65,33},{97,65},{2,98}... | collective-permute-start | bytes 1572872 | tf_op jit(solution)/shard_map/ppermute | solution.py:361
  77.5 9.9 %collective-permute-done.7.refs_1_ = bf16[64,16,256]{2,1,0:T(8,128)(2,1)S(1)} collective-permute-done((bf16[64,16,256]{2,1,0:T(8,128)(2,1)S(1)}, bf16[64,16,256]{2,1,0:T(8,128)(2,1)S(1)}, u32[]{:S(2)}, u32[]{:S(2)}) %collective-permute-start.7) | collective-permute-done | bytes 524320 | tf_op jit(solution)/shard_map/ppermute | solution.py:361
  87.4 10.7 %collective-permute-done.8.refs_2_ = bf16[64,16,256]{2,1,0:T(8,128)(2,1)S(1)} collective-permute-done((bf16[64,16,256]{2,1,0:T(8,128)(2,1)S(1)}, bf16[64,16,256]{2,1,0:T(8,128)(2,1)S(1)}, u32[]{:S(2)}, u32[]{:S(2)}) %collective-permute-start.8) | collective-permute-done | bytes 524320 | tf_op jit(solution)/shard_map/ppermute | solution.py:361
  98.1 0.2 collective-permute-done.9.refs_3_
  98.3 0.3 ring_z.1
  98.6 3.2 %collective-permute-start.10 = (bf16[4,4,16,256]{3,2,1,0:T(8,128)(2,1)S(1)}, bf16[4,4,16,256]{3,2,1,0:T(8,128)(2,1)S(1)}, u32[]{:S(2)}, u32[]{:S(2)}) collective-permute-start(bf16[4,4,16,256]{3,2,1,0:T(8,128)(2,1)S(1)} %get-tuple-element.46), channel_id=1, source_target_pairs={{0,2},{1,3},{2,0},{3,1},{4,6},{5,7},{6,4},{7,5},{8,10},{9,11},{10,... | collective-permute-start | bytes 393224 | tf_op jit(solution)/shard_map/ppermute | solution.py:361
  101.8 0.6 collective-permute-start.11
  102.4 2.7 %collective-permute-start.12 = (bf16[4,4,16,256]{3,2,1,0:T(8,128)(2,1)S(1)}, bf16[4,4,16,256]{3,2,1,0:T(8,128)(2,1)S(1)}, u32[]{:S(2)}, u32[]{:S(2)}) collective-permute-start(bf16[4,4,16,256]{3,2,1,0:T(8,128)(2,1)S(1)} %get-tuple-element.48), channel_id=1, source_target_pairs={{0,3},{1,0},{2,1},{3,2},{4,7},{5,4},{6,5},{7,6},{8,11},{9,8},{10,9... | collective-permute-start | bytes 393224 | tf_op jit(solution)/shard_map/ppermute | solution.py:361
  105.0 1.2 %collective-permute-done.10.refs_1_ = bf16[4,4,16,256]{3,2,1,0:T(8,128)(2,1)S(1)} collective-permute-done((bf16[4,4,16,256]{3,2,1,0:T(8,128)(2,1)S(1)}, bf16[4,4,16,256]{3,2,1,0:T(8,128)(2,1)S(1)}, u32[]{:S(2)}, u32[]{:S(2)}) %collective-permute-start.10) | collective-permute-done | bytes 131104 | tf_op jit(solution)/shard_map/ppermute | solution.py:361
  106.3 2.2 %collective-permute-done.11.refs_2_ = bf16[4,4,16,256]{3,2,1,0:T(8,128)(2,1)S(1)} collective-permute-done((bf16[4,4,16,256]{3,2,1,0:T(8,128)(2,1)S(1)}, bf16[4,4,16,256]{3,2,1,0:T(8,128)(2,1)S(1)}, u32[]{:S(2)}, u32[]{:S(2)}) %collective-permute-start.11) | collective-permute-done | bytes 131104 | tf_op jit(solution)/shard_map/ppermute | solution.py:361
  108.5 0.0 collective-permute-done.12.refs_3_
  108.5 0.1 ring_y.1
  108.6 3.2 %collective-permute-start.13 = (f32[4,16,256]{2,1,0:T(8,128)S(1)}, f32[4,16,256]{2,1,0:T(8,128)S(1)}, u32[]{:S(2)}, u32[]{:S(2)}) collective-permute-start(f32[4,16,256]{2,1,0:T(8,128)S(1)} %get-tuple-element.50), channel_id=1, source_target_pairs={{0,8},{4,12},{8,0},{12,4},{1,9},{5,13},{9,1},{13,5},{2,10},{6,14},... | collective-permute-start | bytes 196616 | tf_op jit(solution)/shard_map/ppermute | solution.py:361
  111.8 0.6 collective-permute-start.14
  112.4 2.7 %collective-permute-start.15 = (f32[4,16,256]{2,1,0:T(8,128)S(1)}, f32[4,16,256]{2,1,0:T(8,128)S(1)}, u32[]{:S(2)}, u32[]{:S(2)}) collective-permute-start(f32[4,16,256]{2,1,0:T(8,128)S(1)} %get-tuple-element.52), channel_id=1, source_target_pairs={{0,12},{4,0},{8,4},{12,8},{1,13},{5,1},{9,5},{13,9},{2,14},{6,2},{... | collective-permute-start | bytes 196616 | tf_op jit(solution)/shard_map/ppermute | solution.py:361
  115.0 0.0 collective-permute-done.13.rest_1_
  115.0 2.2 %collective-permute-done.14.rest_2_ = f32[4,16,256]{2,1,0:T(8,128)S(1)} collective-permute-done((f32[4,16,256]{2,1,0:T(8,128)S(1)}, f32[4,16,256]{2,1,0:T(8,128)S(1)}, u32[]{:S(2)}, u32[]{:S(2)}) %collective-permute-start.14) | collective-permute-done | bytes 65568 | tf_op jit(solution)/shard_map/ppermute | solution.py:361
  117.3 0.0 collective-permute-done.15.rest_3_
  117.3 0.0 all-to-all-done.1.x_ref
  117.3 1.1 finish.1
Async XLA Ops:
  11.8 43.5 %all-to-all-start = ((bf16[8,784,256]{2,1,0:T(8,128)(2,1)}), bf16[8,784,256]{2,1,0:T(8,128)(2,1)S(1)}, u32[]{:S(2)}, u32[]{:S(2)}) async-start(bf16[8,784,256]{2,1,0:T(8,128)(2,1)} %get-tuple-element.29), calls=%async_computation | async-start | bytes 6422528 | tf_op jit(solution)/shard_map/all_to_all | solution.py:378
  24.6 6.7 %collective-permute-start = (bf16[784,256]{1,0:T(8,128)(2,1)}, bf16[784,256]{1,0:T(8,128)(2,1)S(1)}, u32[]{:S(2)}, u32[]{:S(2)}) collective-permute-start(bf16[784,256]{1,0:T(8,128)(2,1)} %get-tuple-element.33), channel_id=1, source_target_pairs={{0,16},{4,20},{8,24},{12,28},{16,0},{20,4},{24,8},{28,12},{1,17},{... | collective-permute-start | bytes 1204232 | tf_op jit(solution)/shard_map/ppermute | solution.py:377
  25.2 14.0 %collective-permute-start.1 = (bf16[784,256]{1,0:T(8,128)(2,1)}, bf16[784,256]{1,0:T(8,128)(2,1)S(1)}, u32[]{:S(2)}, u32[]{:S(2)}) collective-permute-start(bf16[784,256]{1,0:T(8,128)(2,1)} %get-tuple-element.34), channel_id=1, source_target_pairs={{0,4},{4,8},{8,12},{12,0},{16,20},{20,24},{24,28},{28,16},{1,5},{5... | collective-permute-start | bytes 1204232 | tf_op jit(solution)/shard_map/ppermute | solution.py:377
  26.8 40.7 %collective-permute-start.2 = (bf16[784,256]{1,0:T(8,128)(2,1)}, bf16[784,256]{1,0:T(8,128)(2,1)}, u32[]{:S(2)}, u32[]{:S(2)}) collective-permute-start(bf16[784,256]{1,0:T(8,128)(2,1)} %get-tuple-element.35), channel_id=1, source_target_pairs={{0,8},{4,12},{8,0},{12,4},{16,24},{20,28},{24,16},{28,20},{1,9},{5... | collective-permute-start | bytes 1204232 | tf_op jit(solution)/shard_map/ppermute | solution.py:377
  29.7 37.8 %collective-permute-start.3 = (bf16[784,256]{1,0:T(8,128)(2,1)}, bf16[784,256]{1,0:T(8,128)(2,1)}, u32[]{:S(2)}, u32[]{:S(2)}) collective-permute-start(bf16[784,256]{1,0:T(8,128)(2,1)} %get-tuple-element.36), channel_id=1, source_target_pairs={{0,24},{4,28},{8,16},{12,20},{16,8},{20,12},{24,0},{28,4},{1,25},{... | collective-permute-start | bytes 1204232 | tf_op jit(solution)/shard_map/ppermute | solution.py:377
  29.7 37.8 %collective-permute-start.4 = (bf16[784,256]{1,0:T(8,128)(2,1)}, bf16[784,256]{1,0:T(8,128)(2,1)}, u32[]{:S(2)}, u32[]{:S(2)}) collective-permute-start(bf16[784,256]{1,0:T(8,128)(2,1)} %get-tuple-element.37), channel_id=1, source_target_pairs={{0,12},{4,0},{8,4},{12,8},{16,28},{20,16},{24,20},{28,24},{1,13},{... | collective-permute-start | bytes 1204232 | tf_op jit(solution)/shard_map/ppermute | solution.py:377
  31.3 0.8 copy-start.1
  32.0 35.4 %collective-permute-start.5 = (bf16[784,256]{1,0:T(8,128)(2,1)}, bf16[784,256]{1,0:T(8,128)(2,1)}, u32[]{:S(2)}, u32[]{:S(2)}) collective-permute-start(bf16[784,256]{1,0:T(8,128)(2,1)} %get-tuple-element.38), channel_id=1, source_target_pairs={{0,20},{4,24},{8,28},{12,16},{16,4},{20,8},{24,12},{28,0},{1,21},{... | collective-permute-start | bytes 1204232 | tf_op jit(solution)/shard_map/ppermute | solution.py:377
  39.2 0.8 copy-start.3
  39.9 27.5 %collective-permute-start.6 = (bf16[784,256]{1,0:T(8,128)(2,1)}, bf16[784,256]{1,0:T(8,128)(2,1)}, u32[]{:S(2)}, u32[]{:S(2)}) collective-permute-start(bf16[784,256]{1,0:T(8,128)(2,1)} %get-tuple-element.39), channel_id=1, source_target_pairs={{0,28},{4,16},{8,20},{12,24},{16,12},{20,0},{24,4},{28,8},{1,29},{... | collective-permute-start | bytes 1204232 | tf_op jit(solution)/shard_map/ppermute | solution.py:377
  57.7 1.4 %copy-start = (bf16[16,272,256]{2,1,0:T(8,128)(2,1)}, bf16[16,272,256]{2,1,0:T(8,128)(2,1)S(1)}, u32[]{:S(2)}) copy-start(bf16[16,272,256]{2,1,0:T(8,128)(2,1)S(1)} %get-tuple-element.30) | copy-start | bytes 6684676
  59.1 8.4 %copy-start.2 = (bf16[784,256]{1,0:T(8,128)(2,1)S(1)}, bf16[784,256]{1,0:T(8,128)(2,1)}, u32[]{:S(2)}) copy-start(bf16[784,256]{1,0:T(8,128)(2,1)} %copy-done.1) | copy-start | bytes 1204228
  59.1 8.4 %copy-start.4 = (bf16[784,256]{1,0:T(8,128)(2,1)S(1)}, bf16[784,256]{1,0:T(8,128)(2,1)}, u32[]{:S(2)}) copy-start(bf16[784,256]{1,0:T(8,128)(2,1)} %copy-done.3) | copy-start | bytes 1204228
  59.1 8.4 %copy-start.5 = (bf16[784,256]{1,0:T(8,128)(2,1)S(1)}, bf16[784,256]{1,0:T(8,128)(2,1)}, u32[]{:S(2)}) copy-start(bf16[784,256]{1,0:T(8,128)(2,1)} %get-tuple-element.32.rest_0_) | copy-start | bytes 1204228
  59.1 58.2 %all-to-all-start.1 = ((bf16[16,272,256]{2,1,0:T(8,128)(2,1)}), bf16[16,272,256]{2,1,0:T(8,128)(2,1)S(1)}, u32[]{:S(2)}, u32[]{:S(2)}) async-start(bf16[16,272,256]{2,1,0:T(8,128)(2,1)} %copy-done), calls=%async_computation.1 | async-start | bytes 4456448 | tf_op jit(solution)/shard_map/all_to_all | solution.py:396
  71.0 16.4 %collective-permute-start.7 = (bf16[64,16,256]{2,1,0:T(8,128)(2,1)S(1)}, bf16[64,16,256]{2,1,0:T(8,128)(2,1)S(1)}, u32[]{:S(2)}, u32[]{:S(2)}) collective-permute-start(bf16[64,16,256]{2,1,0:T(8,128)(2,1)S(1)} %get-tuple-element.42), channel_id=1, source_target_pairs={{0,64},{32,96},{64,0},{96,32},{1,65},{33,97},{65,1},{97,33},{2,66}... | collective-permute-start | bytes 1572872 | tf_op jit(solution)/shard_map/ppermute | solution.py:361
  74.2 23.9 %collective-permute-start.8 = (bf16[64,16,256]{2,1,0:T(8,128)(2,1)S(1)}, bf16[64,16,256]{2,1,0:T(8,128)(2,1)S(1)}, u32[]{:S(2)}, u32[]{:S(2)}) collective-permute-start(bf16[64,16,256]{2,1,0:T(8,128)(2,1)S(1)} %get-tuple-element.43), channel_id=1, source_target_pairs={{0,32},{32,64},{64,96},{96,0},{1,33},{33,65},{65,97},{97,1},{2,34}... | collective-permute-start | bytes 1572872 | tf_op jit(solution)/shard_map/ppermute | solution.py:361
  74.8 23.5 %collective-permute-start.9 = (bf16[64,16,256]{2,1,0:T(8,128)(2,1)S(1)}, bf16[64,16,256]{2,1,0:T(8,128)(2,1)S(1)}, u32[]{:S(2)}, u32[]{:S(2)}) collective-permute-start(bf16[64,16,256]{2,1,0:T(8,128)(2,1)S(1)} %get-tuple-element.44), channel_id=1, source_target_pairs={{0,96},{32,0},{64,32},{96,64},{1,97},{33,1},{65,33},{97,65},{2,98}... | collective-permute-start | bytes 1572872 | tf_op jit(solution)/shard_map/ppermute | solution.py:361
  98.6 7.7 %collective-permute-start.10 = (bf16[4,4,16,256]{3,2,1,0:T(8,128)(2,1)S(1)}, bf16[4,4,16,256]{3,2,1,0:T(8,128)(2,1)S(1)}, u32[]{:S(2)}, u32[]{:S(2)}) collective-permute-start(bf16[4,4,16,256]{3,2,1,0:T(8,128)(2,1)S(1)} %get-tuple-element.46), channel_id=1, source_target_pairs={{0,2},{1,3},{2,0},{3,1},{4,6},{5,7},{6,4},{7,5},{8,10},{9,11},{10,... | collective-permute-start | bytes 393224 | tf_op jit(solution)/shard_map/ppermute | solution.py:361
  101.8 6.7 %collective-permute-start.11 = (bf16[4,4,16,256]{3,2,1,0:T(8,128)(2,1)S(1)}, bf16[4,4,16,256]{3,2,1,0:T(8,128)(2,1)S(1)}, u32[]{:S(2)}, u32[]{:S(2)}) collective-permute-start(bf16[4,4,16,256]{3,2,1,0:T(8,128)(2,1)S(1)} %get-tuple-element.47), channel_id=1, source_target_pairs={{0,1},{1,2},{2,3},{3,0},{4,5},{5,6},{6,7},{7,4},{8,9},{9,10},{10,1... | collective-permute-start | bytes 393224 | tf_op jit(solution)/shard_map/ppermute | solution.py:361
  102.4 6.1 %collective-permute-start.12 = (bf16[4,4,16,256]{3,2,1,0:T(8,128)(2,1)S(1)}, bf16[4,4,16,256]{3,2,1,0:T(8,128)(2,1)S(1)}, u32[]{:S(2)}, u32[]{:S(2)}) collective-permute-start(bf16[4,4,16,256]{3,2,1,0:T(8,128)(2,1)S(1)} %get-tuple-element.48), channel_id=1, source_target_pairs={{0,3},{1,0},{2,1},{3,2},{4,7},{5,4},{6,5},{7,6},{8,11},{9,8},{10,9... | collective-permute-start | bytes 393224 | tf_op jit(solution)/shard_map/ppermute | solution.py:361
  108.6 6.5 %collective-permute-start.13 = (f32[4,16,256]{2,1,0:T(8,128)S(1)}, f32[4,16,256]{2,1,0:T(8,128)S(1)}, u32[]{:S(2)}, u32[]{:S(2)}) collective-permute-start(f32[4,16,256]{2,1,0:T(8,128)S(1)} %get-tuple-element.50), channel_id=1, source_target_pairs={{0,8},{4,12},{8,0},{12,4},{1,9},{5,13},{9,1},{13,5},{2,10},{6,14},... | collective-permute-start | bytes 196616 | tf_op jit(solution)/shard_map/ppermute | solution.py:361
  111.8 5.5 %collective-permute-start.14 = (f32[4,16,256]{2,1,0:T(8,128)S(1)}, f32[4,16,256]{2,1,0:T(8,128)S(1)}, u32[]{:S(2)}, u32[]{:S(2)}) collective-permute-start(f32[4,16,256]{2,1,0:T(8,128)S(1)} %get-tuple-element.51), channel_id=1, source_target_pairs={{0,4},{4,8},{8,12},{12,0},{1,5},{5,9},{9,13},{13,1},{2,6},{6,10},{... | collective-permute-start | bytes 196616 | tf_op jit(solution)/shard_map/ppermute | solution.py:361
  112.4 4.9 %collective-permute-start.15 = (f32[4,16,256]{2,1,0:T(8,128)S(1)}, f32[4,16,256]{2,1,0:T(8,128)S(1)}, u32[]{:S(2)}, u32[]{:S(2)}) collective-permute-start(f32[4,16,256]{2,1,0:T(8,128)S(1)} %get-tuple-element.52), channel_id=1, source_target_pairs={{0,12},{4,0},{8,4},{12,8},{1,13},{5,1},{9,5},{13,9},{2,14},{6,2},{... | collective-permute-start | bytes 196616 | tf_op jit(solution)/shard_map/ppermute | solution.py:361

commit v5 on v4

--- a/solution.py
+++ b/solution.py
@@ -23,7 +23,7 @@
 Y_OFFSETS = ((0, 0), (1, 0), (0, 1), (0, 2), (1, 2), (0, 3), (1, 1), (1, 3))
 
 
-GROUP = 4
+GROUP = 2
 RING_ORDER = (2, 1, 3)
 AHEAD = 3
 
@@ -246,7 +246,7 @@
     return line
 
 
-def gather_x_kernel(in_ref, out_hbm, done_ref, acc, flat, smem, sem, out_ref, out_sem):
+def gather_x_kernel(in_ref, out_ref, done_ref, acc, flat, smem, sem):
     rows, width = acc.shape[1:]
     blocks = (in_ref.shape[1] - SUB) // rows
     top = blocks * rows
@@ -262,18 +262,11 @@
     den = jnp.dot(hit, weights, preferred_element_type=F32)
     high = den.astype(BF).astype(F32)
     both = jnp.concatenate([high, den - high], axis=1)
-    stores = []
     for t in range(TILES):
         for p in range(POS):
             out_ref[t, p * rows : (p + 1) * rows] = acc[t * POS + p].astype(BF)
         pad = jnp.zeros((SUB - POS, width), F32)
         out_ref[t, POS * rows :] = jnp.concatenate([both[t * POS : (t + 1) * POS], pad], axis=0).astype(BF)
-        if (t + 1) % GROUP == 0:
-            part = pl.ds(t + 1 - GROUP, GROUP)
-            stores.append(pltpu.make_async_copy(out_ref.at[part], out_hbm.at[part], out_sem.at[t // GROUP]))
-            stores[-1].start()
-    for store in stores:
-        store.wait()
 
 
 def gather_y_kernel(*rest):
@@ -384,12 +377,8 @@
         pltpu.SemaphoreType.DMA,
     ]
     y_scratch = scratch + [pltpu.VMEM((NX, COUNT, SUB, width), BF), pltpu.SemaphoreType.DMA((NX,))]
-    x_scratch = scratch + [
-        pltpu.VMEM((TILES, POS * rows + SUB, width), BF),
-        pltpu.SemaphoreType.DMA((TILES // GROUP,)),
-    ]
     x_sum, x_done = vmem_call(
-        gather_x_kernel, "gather_x", (shape((TILES, POS * rows + SUB, width), BF), shape((8, LANE), F32)), (x_in,), x_scratch, 0, GX, (True, False)
+        gather_x_kernel, "gather_x", (shape((TILES, POS * rows + SUB, width), BF), shape((8, LANE), F32)), (x_in,), scratch, 0, GX
     )
     mine = vmem_call(gather_y_kernel, "gather_y", [shape((COUNT, SUB, width), BF)] * NX, (*arrived, x_done), y_scratch, 1, GY, [True] * NX)
     along_x = ring(mine, "x", NX)

time: 119 us -> 119 us (level)
  no operation moved by 1% of the time
where the time goes in v5:
time: 119 us; the launch traced here: 118 us
  waiting for transfers between devices  48.6 us (41%)
  starting transfers between devices  39.3 us (33%)
  Pallas kernels  26.9 us (23%)
  local copies, waits for them, and re-layouts  2.95 us (2%)
    ppermute x9, waiting for transfers between devices, ring(): lax.ppermute(pieces[i], axis, [(s, (s + i) % size) for s in range(size)])  26.6 us
    ppermute x9, starting transfers between devices, ring(): lax.ppermute(pieces[i], axis, [(s, (s + i) % size) for s in range(size)])  19.4 us
    all_to_all x1, waiting for transfers between devices, per_device(): x_in = lax.all_to_all(x_part, ('x', 'core'), 0, 0, tiled=True)  15.4 us
    pallas_call x1, Pallas kernels, match(): pl.pallas_call(match_x_kernel, in_specs=[smem] * 3 + [vmem] * 3 + [hbm],...  11.7 us
    pallas_call x1, Pallas kernels, match(): pl.pallas_call(match_y_kernel, in_specs=[smem] * 3 + [vmem] * 2 + [hbm],...  8.4 us
    all_to_all x1, starting transfers between devices, per_device(): x_out = lax.all_to_all(x_sum, ('y', 'z'), 0, 0, tiled=True)  8.39 us
    ppermute x7, starting transfers between devices, per_device(): arrived.append(lax.ppermute(y_parts[i], ('core', 'y'), perm))  7.18 us
    pallas_call x5, Pallas kernels, vmem_call(): pl.pallas_call(kernel, in_specs=[vm] * (len(args) - after) + [anywhere] *...  6.82 us
  transfers between devices with their start and end apart: 18, of which 8 were waited for; matrix products, arithmetic and copies ran while one was open for 0% of the time, Pallas kernels for 12%

profile of v5, /device:TPU:0, one launch (start us, length us, event | category | flops | bytes accessed | tf_op | source)
XLA Modules:
  0.0 117.9 jit_solution(14038175469893827920)
XLA Ops:
  0.0 11.7 %match_x.1 = (bf16[8,784,256]{2,1,0:T(8,128)(2,1)}, bf16[12,512,384]{2,1,0:T(8,128)(2,1)}) custom-call(s32[12]{0:T(128)} %kidx_ref.3, s32[12]{0:T(128)} %bitcast.2, s32[12]{0:T(128)} %pos_ref.3, f32[8,41]{1,0:T(8,128)} %rtap_ref.1, f32[8,41]{1,0:T(8,128)} %ctap_ref.3, bf16[12,512]{1,0:T(8,128)(2,1)} %iv_ref.3, bf16[12,512,512]{2,1,0:T(8,128)(2,1)} %img_ref.1), custom_call_target="tpu_custom_call" | custom-call | flops 40000000000 | bytes 12582912 | tf_op jit(solution)/shard_map/match_x/pallas_call | solution.py:192
  11.7 4.4 %all-to-all-start = ((bf16[8,784,256]{2,1,0:T(8,128)(2,1)}), bf16[8,784,256]{2,1,0:T(8,128)(2,1)S(1)}, u32[]{:S(2)}, u32[]{:S(2)}) async-start(bf16[8,784,256]{2,1,0:T(8,128)(2,1)} %get-tuple-element.29), calls=%async_computation | async-start | bytes 6422528 | tf_op jit(solution)/shard_map/all_to_all | solution.py:371
  16.1 8.4 %match_y.1 = (bf16[784,256]{1,0:T(8,128)(2,1)}, bf16[784,256]{1,0:T(8,128)(2,1)}, bf16[784,256]{1,0:T(8,128)(2,1)}, bf16[784,256]{1,0:T(8,128)(2,1)}, bf16[784,2...) custom-call(s32[12]{0:T(128)} %kidx_ref.3, s32[12]{0:T(128)} %bitcast.3, ...), custom_call_target="tpu_custom_call" | custom-call | flops 40000000000 | bytes 12582912 | tf_op jit(solution)/shard_map/match_y/pallas_call | solution.py:214
  24.5 0.6 collective-permute-start
  25.1 1.6 %collective-permute-start.1 = (bf16[784,256]{1,0:T(8,128)(2,1)}, bf16[784,256]{1,0:T(8,128)(2,1)S(1)}, u32[]{:S(2)}, u32[]{:S(2)}) collective-permute-start(bf16[784,256]{1,0:T(8,128)(2,1)} %get-tuple-element.34), channel_id=1, source_target_pairs={{0,4},{4,8},{8,12},{12,0},{16,20},{20,24},{24,28},{28,16},{1,5},{5... | collective-permute-start | bytes 1204232 | tf_op jit(solution)/shard_map/ppermute | solution.py:370
  26.6 2.9 %collective-permute-start.2 = (bf16[784,256]{1,0:T(8,128)(2,1)}, bf16[784,256]{1,0:T(8,128)(2,1)}, u32[]{:S(2)}, u32[]{:S(2)}) collective-permute-start(bf16[784,256]{1,0:T(8,128)(2,1)} %get-tuple-element.35), channel_id=1, source_target_pairs={{0,8},{4,12},{8,0},{12,4},{16,24},{20,28},{24,16},{28,20},{1,9},{5... | collective-permute-start | bytes 1204232 | tf_op jit(solution)/shard_map/ppermute | solution.py:370
  29.6 0.0 collective-permute-start.3
  29.6 1.6 %collective-permute-start.4 = (bf16[784,256]{1,0:T(8,128)(2,1)}, bf16[784,256]{1,0:T(8,128)(2,1)}, u32[]{:S(2)}, u32[]{:S(2)}) collective-permute-start(bf16[784,256]{1,0:T(8,128)(2,1)} %get-tuple-element.37), channel_id=1, source_target_pairs={{0,12},{4,0},{8,4},{12,8},{16,28},{20,16},{24,20},{28,24},{1,13},{... | collective-permute-start | bytes 1204232 | tf_op jit(solution)/shard_map/ppermute | solution.py:370
  31.1 0.0 collective-permute-done.rest_1_
  31.1 0.0 copy-start.1
  31.2 0.8 copy-done.1
  31.9 0.5 collective-permute-start.5
  32.4 6.6 %collective-permute-done.1.rest_2_ = bf16[784,256]{1,0:T(8,128)(2,1)S(1)} collective-permute-done((bf16[784,256]{1,0:T(8,128)(2,1)}, bf16[784,256]{1,0:T(8,128)(2,1)S(1)}, u32[]{:S(2)}, u32[]{:S(2)}) %collective-permute-start.1) | collective-permute-done | bytes 401440 | tf_op jit(solution)/shard_map/ppermute | solution.py:370
  39.1 0.0 copy-start.3
  39.1 0.8 copy-done.3
  39.8 0.0 collective-permute-start.6
  39.8 15.4 %all-to-all-done.in_ref = bf16[8,784,256]{2,1,0:T(8,128)(2,1)S(1)} async-done(((bf16[8,784,256]{2,1,0:T(8,128)(2,1)}), bf16[8,784,256]{2,1,0:T(8,128)(2,1)S(1)}, u32[]{:S(2)}, u32[]{:S(2)}) %all-to-all-start) | async-done | bytes 3211296 | tf_op jit(solution)/shard_map/all_to_all | solution.py:371
  55.2 1.9 %gather_x.1 = (bf16[16,272,256]{2,1,0:T(8,128)(2,1)S(1)}, f32[8,128]{1,0:T(8,128)S(1)}) custom-call(bf16[8,784,256]{2,1,0:T(8,128)(2,1)S(1)} %all-to-all-done.in_ref), custom_call_target="tpu_custom_call" | custom-call | flops 40000000000 | bytes 6422528 | tf_op jit(solution)/shard_map/gather_x/pallas_call | solution.py:298
  57.1 0.0 copy-start
  57.1 1.4 %copy-done = bf16[16,272,256]{2,1,0:T(8,128)(2,1)} copy-done((bf16[16,272,256]{2,1,0:T(8,128)(2,1)}, bf16[16,272,256]{2,1,0:T(8,128)(2,1)S(1)}, u32[]{:S(2)}) %copy-start) | copy-done | bytes 2228248
  58.5 0.0 copy-start.2
  58.5 0.0 copy-start.4
  58.5 0.0 copy-start.5
  58.5 8.4 %all-to-all-start.1 = ((bf16[16,272,256]{2,1,0:T(8,128)(2,1)}), bf16[16,272,256]{2,1,0:T(8,128)(2,1)S(1)}, u32[]{:S(2)}, u32[]{:S(2)}) async-start(bf16[16,272,256]{2,1,0:T(8,128)(2,1)} %copy-done), calls=%async_computation.1 | async-start | bytes 4456448 | tf_op jit(solution)/shard_map/all_to_all | solution.py:385
  66.9 0.0 collective-permute-done.2.rest_3_
  67.0 0.0 collective-permute-done.3.rest_4_
  67.0 0.0 collective-permute-done.4.rest_5_
  67.0 0.0 collective-permute-done.5.rest_6_
  67.0 0.0 collective-permute-done.6.rest_7_
  67.0 0.0 copy-done.2
  67.0 0.0 copy-done.4
  67.0 0.0 copy-done.5
  67.0 3.5 %gather_y.1 = (bf16[64,16,256]{2,1,0:T(8,128)(2,1)S(1)}, bf16[64,16,256]{2,1,0:T(8,128)(2,1)S(1)}, bf16[64,16,256]{2,1,0:T(8,128)(2,1)S(1)}, bf16[64,16,256]{2,1,0:T(8,128)(2,1)S(1)}) custom-call(bf16[784,256]{1,0:T(8,128)(2,1)S(1)} %copy-done.5, bf16[784,256]{1,0:T(8,128)(2,1)S(1)} %copy-done.2, bf16[784,256]{1,0:T(8,128)(2,1)S(1)} %copy-done.4, ...), custom_call_target="tpu_custom_call" | custom-call | flops 40000000000 | bytes 6430720 | tf_op jit(solution)/shard_map/gather_y/pallas_call | solution.py:298
  70.5 3.2 %collective-permute-start.7 = (bf16[64,16,256]{2,1,0:T(8,128)(2,1)S(1)}, bf16[64,16,256]{2,1,0:T(8,128)(2,1)S(1)}, u32[]{:S(2)}, u32[]{:S(2)}) collective-permute-start(bf16[64,16,256]{2,1,0:T(8,128)(2,1)S(1)} %get-tuple-element.42), channel_id=1, source_target_pairs={{0,64},{32,96},{64,0},{96,32},{1,65},{33,97},{65,1},{97,33},{2,66}... | collective-permute-start | bytes 1572872 | tf_op jit(solution)/shard_map/ppermute | solution.py:354
  73.7 0.6 collective-permute-start.8
  74.3 2.7 %collective-permute-start.9 = (bf16[64,16,256]{2,1,0:T(8,128)(2,1)S(1)}, bf16[64,16,256]{2,1,0:T(8,128)(2,1)S(1)}, u32[]{:S(2)}, u32[]{:S(2)}) collective-permute-start(bf16[64,16,256]{2,1,0:T(8,128)(2,1)S(1)} %get-tuple-element.44), channel_id=1, source_target_pairs={{0,96},{32,0},{64,32},{96,64},{1,97},{33,1},{65,33},{97,65},{2,98}... | collective-permute-start | bytes 1572872 | tf_op jit(solution)/shard_map/ppermute | solution.py:354
  76.9 9.9 %collective-permute-done.7.refs_1_ = bf16[64,16,256]{2,1,0:T(8,128)(2,1)S(1)} collective-permute-done((bf16[64,16,256]{2,1,0:T(8,128)(2,1)S(1)}, bf16[64,16,256]{2,1,0:T(8,128)(2,1)S(1)}, u32[]{:S(2)}, u32[]{:S(2)}) %collective-permute-start.7) | collective-permute-done | bytes 524320 | tf_op jit(solution)/shard_map/ppermute | solution.py:354
  86.9 10.7 %collective-permute-done.8.refs_2_ = bf16[64,16,256]{2,1,0:T(8,128)(2,1)S(1)} collective-permute-done((bf16[64,16,256]{2,1,0:T(8,128)(2,1)S(1)}, bf16[64,16,256]{2,1,0:T(8,128)(2,1)S(1)}, u32[]{:S(2)}, u32[]{:S(2)}) %collective-permute-start.8) | collective-permute-done | bytes 524320 | tf_op jit(solution)/shard_map/ppermute | solution.py:354
  97.6 0.2 collective-permute-done.9.refs_3_
  97.8 0.3 ring_z.1
  98.1 3.2 %collective-permute-start.10 = (bf16[4,4,16,256]{3,2,1,0:T(8,128)(2,1)S(1)}, bf16[4,4,16,256]{3,2,1,0:T(8,128)(2,1)S(1)}, u32[]{:S(2)}, u32[]{:S(2)}) collective-permute-start(bf16[4,4,16,256]{3,2,1,0:T(8,128)(2,1)S(1)} %get-tuple-element.46), channel_id=1, source_target_pairs={{0,2},{1,3},{2,0},{3,1},{4,6},{5,7},{6,4},{7,5},{8,10},{9,11},{10,... | collective-permute-start | bytes 393224 | tf_op jit(solution)/shard_map/ppermute | solution.py:354
  101.3 0.6 collective-permute-start.11
  101.9 2.7 %collective-permute-start.12 = (bf16[4,4,16,256]{3,2,1,0:T(8,128)(2,1)S(1)}, bf16[4,4,16,256]{3,2,1,0:T(8,128)(2,1)S(1)}, u32[]{:S(2)}, u32[]{:S(2)}) collective-permute-start(bf16[4,4,16,256]{3,2,1,0:T(8,128)(2,1)S(1)} %get-tuple-element.48), channel_id=1, source_target_pairs={{0,3},{1,0},{2,1},{3,2},{4,7},{5,4},{6,5},{7,6},{8,11},{9,8},{10,9... | collective-permute-start | bytes 393224 | tf_op jit(solution)/shard_map/ppermute | solution.py:354
  104.5 1.2 %collective-permute-done.10.refs_1_ = bf16[4,4,16,256]{3,2,1,0:T(8,128)(2,1)S(1)} collective-permute-done((bf16[4,4,16,256]{3,2,1,0:T(8,128)(2,1)S(1)}, bf16[4,4,16,256]{3,2,1,0:T(8,128)(2,1)S(1)}, u32[]{:S(2)}, u32[]{:S(2)}) %collective-permute-start.10) | collective-permute-done | bytes 131104 | tf_op jit(solution)/shard_map/ppermute | solution.py:354
  105.8 2.2 %collective-permute-done.11.refs_2_ = bf16[4,4,16,256]{3,2,1,0:T(8,128)(2,1)S(1)} collective-permute-done((bf16[4,4,16,256]{3,2,1,0:T(8,128)(2,1)S(1)}, bf16[4,4,16,256]{3,2,1,0:T(8,128)(2,1)S(1)}, u32[]{:S(2)}, u32[]{:S(2)}) %collective-permute-start.11) | collective-permute-done | bytes 131104 | tf_op jit(solution)/shard_map/ppermute | solution.py:354
  108.0 0.0 collective-permute-done.12.refs_3_
  108.0 0.1 ring_y.1
  108.1 3.2 %collective-permute-start.13 = (f32[4,16,256]{2,1,0:T(8,128)S(1)}, f32[4,16,256]{2,1,0:T(8,128)S(1)}, u32[]{:S(2)}, u32[]{:S(2)}) collective-permute-start(f32[4,16,256]{2,1,0:T(8,128)S(1)} %get-tuple-element.50), channel_id=1, source_target_pairs={{0,8},{4,12},{8,0},{12,4},{1,9},{5,13},{9,1},{13,5},{2,10},{6,14},... | collective-permute-start | bytes 196616 | tf_op jit(solution)/shard_map/ppermute | solution.py:354
  111.3 0.6 collective-permute-start.14
  111.9 2.7 %collective-permute-start.15 = (f32[4,16,256]{2,1,0:T(8,128)S(1)}, f32[4,16,256]{2,1,0:T(8,128)S(1)}, u32[]{:S(2)}, u32[]{:S(2)}) collective-permute-start(f32[4,16,256]{2,1,0:T(8,128)S(1)} %get-tuple-element.52), channel_id=1, source_target_pairs={{0,12},{4,0},{8,4},{12,8},{1,13},{5,1},{9,5},{13,9},{2,14},{6,2},{... | collective-permute-start | bytes 196616 | tf_op jit(solution)/shard_map/ppermute | solution.py:354
  114.5 0.0 collective-permute-done.13.rest_1_
  114.5 2.2 %collective-permute-done.14.rest_2_ = f32[4,16,256]{2,1,0:T(8,128)S(1)} collective-permute-done((f32[4,16,256]{2,1,0:T(8,128)S(1)}, f32[4,16,256]{2,1,0:T(8,128)S(1)}, u32[]{:S(2)}, u32[]{:S(2)}) %collective-permute-start.14) | collective-permute-done | bytes 65568 | tf_op jit(solution)/shard_map/ppermute | solution.py:354
  116.8 0.0 collective-permute-done.15.rest_3_
  116.8 0.0 all-to-all-done.1.x_ref
  116.8 1.1 finish.1
Async XLA Ops:
  11.7 43.5 %all-to-all-start = ((bf16[8,784,256]{2,1,0:T(8,128)(2,1)}), bf16[8,784,256]{2,1,0:T(8,128)(2,1)S(1)}, u32[]{:S(2)}, u32[]{:S(2)}) async-start(bf16[8,784,256]{2,1,0:T(8,128)(2,1)} %get-tuple-element.29), calls=%async_computation | async-start | bytes 6422528 | tf_op jit(solution)/shard_map/all_to_all | solution.py:371
  24.5 6.7 %collective-permute-start = (bf16[784,256]{1,0:T(8,128)(2,1)}, bf16[784,256]{1,0:T(8,128)(2,1)S(1)}, u32[]{:S(2)}, u32[]{:S(2)}) collective-permute-start(bf16[784,256]{1,0:T(8,128)(2,1)} %get-tuple-element.33), channel_id=1, source_target_pairs={{0,16},{4,20},{8,24},{12,28},{16,0},{20,4},{24,8},{28,12},{1,17},{... | collective-permute-start | bytes 1204232 | tf_op jit(solution)/shard_map/ppermute | solution.py:370
  25.1 14.0 %collective-permute-start.1 = (bf16[784,256]{1,0:T(8,128)(2,1)}, bf16[784,256]{1,0:T(8,128)(2,1)S(1)}, u32[]{:S(2)}, u32[]{:S(2)}) collective-permute-start(bf16[784,256]{1,0:T(8,128)(2,1)} %get-tuple-element.34), channel_id=1, source_target_pairs={{0,4},{4,8},{8,12},{12,0},{16,20},{20,24},{24,28},{28,16},{1,5},{5... | collective-permute-start | bytes 1204232 | tf_op jit(solution)/shard_map/ppermute | solution.py:370
  26.6 40.3 %collective-permute-start.2 = (bf16[784,256]{1,0:T(8,128)(2,1)}, bf16[784,256]{1,0:T(8,128)(2,1)}, u32[]{:S(2)}, u32[]{:S(2)}) collective-permute-start(bf16[784,256]{1,0:T(8,128)(2,1)} %get-tuple-element.35), channel_id=1, source_target_pairs={{0,8},{4,12},{8,0},{12,4},{16,24},{20,28},{24,16},{28,20},{1,9},{5... | collective-permute-start | bytes 1204232 | tf_op jit(solution)/shard_map/ppermute | solution.py:370
  29.6 37.4 %collective-permute-start.3 = (bf16[784,256]{1,0:T(8,128)(2,1)}, bf16[784,256]{1,0:T(8,128)(2,1)}, u32[]{:S(2)}, u32[]{:S(2)}) collective-permute-start(bf16[784,256]{1,0:T(8,128)(2,1)} %get-tuple-element.36), channel_id=1, source_target_pairs={{0,24},{4,28},{8,16},{12,20},{16,8},{20,12},{24,0},{28,4},{1,25},{... | collective-permute-start | bytes 1204232 | tf_op jit(solution)/shard_map/ppermute | solution.py:370
  29.6 37.4 %collective-permute-start.4 = (bf16[784,256]{1,0:T(8,128)(2,1)}, bf16[784,256]{1,0:T(8,128)(2,1)}, u32[]{:S(2)}, u32[]{:S(2)}) collective-permute-start(bf16[784,256]{1,0:T(8,128)(2,1)} %get-tuple-element.37), channel_id=1, source_target_pairs={{0,12},{4,0},{8,4},{12,8},{16,28},{20,16},{24,20},{28,24},{1,13},{... | collective-permute-start | bytes 1204232 | tf_op jit(solution)/shard_map/ppermute | solution.py:370
  31.1 0.8 copy-start.1
  31.9 35.1 %collective-permute-start.5 = (bf16[784,256]{1,0:T(8,128)(2,1)}, bf16[784,256]{1,0:T(8,128)(2,1)}, u32[]{:S(2)}, u32[]{:S(2)}) collective-permute-start(bf16[784,256]{1,0:T(8,128)(2,1)} %get-tuple-element.38), channel_id=1, source_target_pairs={{0,20},{4,24},{8,28},{12,16},{16,4},{20,8},{24,12},{28,0},{1,21},{... | collective-permute-start | bytes 1204232 | tf_op jit(solution)/shard_map/ppermute | solution.py:370
  39.1 0.8 copy-start.3
  39.8 27.2 %collective-permute-start.6 = (bf16[784,256]{1,0:T(8,128)(2,1)}, bf16[784,256]{1,0:T(8,128)(2,1)}, u32[]{:S(2)}, u32[]{:S(2)}) collective-permute-start(bf16[784,256]{1,0:T(8,128)(2,1)} %get-tuple-element.39), channel_id=1, source_target_pairs={{0,28},{4,16},{8,20},{12,24},{16,12},{20,0},{24,4},{28,8},{1,29},{... | collective-permute-start | bytes 1204232 | tf_op jit(solution)/shard_map/ppermute | solution.py:370
  57.1 1.4 %copy-start = (bf16[16,272,256]{2,1,0:T(8,128)(2,1)}, bf16[16,272,256]{2,1,0:T(8,128)(2,1)S(1)}, u32[]{:S(2)}) copy-start(bf16[16,272,256]{2,1,0:T(8,128)(2,1)S(1)} %get-tuple-element.30) | copy-start | bytes 6684676
  58.5 8.5 %copy-start.2 = (bf16[784,256]{1,0:T(8,128)(2,1)S(1)}, bf16[784,256]{1,0:T(8,128)(2,1)}, u32[]{:S(2)}) copy-start(bf16[784,256]{1,0:T(8,128)(2,1)} %copy-done.1) | copy-start | bytes 1204228
  58.5 8.5 %copy-start.4 = (bf16[784,256]{1,0:T(8,128)(2,1)S(1)}, bf16[784,256]{1,0:T(8,128)(2,1)}, u32[]{:S(2)}) copy-start(bf16[784,256]{1,0:T(8,128)(2,1)} %copy-done.3) | copy-start | bytes 1204228
  58.5 8.5 %copy-start.5 = (bf16[784,256]{1,0:T(8,128)(2,1)S(1)}, bf16[784,256]{1,0:T(8,128)(2,1)}, u32[]{:S(2)}) copy-start(bf16[784,256]{1,0:T(8,128)(2,1)} %get-tuple-element.32.rest_0_) | copy-start | bytes 1204228
  58.5 58.2 %all-to-all-start.1 = ((bf16[16,272,256]{2,1,0:T(8,128)(2,1)}), bf16[16,272,256]{2,1,0:T(8,128)(2,1)S(1)}, u32[]{:S(2)}, u32[]{:S(2)}) async-start(bf16[16,272,256]{2,1,0:T(8,128)(2,1)} %copy-done), calls=%async_computation.1 | async-start | bytes 4456448 | tf_op jit(solution)/shard_map/all_to_all | solution.py:385
  70.5 16.4 %collective-permute-start.7 = (bf16[64,16,256]{2,1,0:T(8,128)(2,1)S(1)}, bf16[64,16,256]{2,1,0:T(8,128)(2,1)S(1)}, u32[]{:S(2)}, u32[]{:S(2)}) collective-permute-start(bf16[64,16,256]{2,1,0:T(8,128)(2,1)S(1)} %get-tuple-element.42), channel_id=1, source_target_pairs={{0,64},{32,96},{64,0},{96,32},{1,65},{33,97},{65,1},{97,33},{2,66}... | collective-permute-start | bytes 1572872 | tf_op jit(solution)/shard_map/ppermute | solution.py:354
  73.7 23.9 %collective-permute-start.8 = (bf16[64,16,256]{2,1,0:T(8,128)(2,1)S(1)}, bf16[64,16,256]{2,1,0:T(8,128)(2,1)S(1)}, u32[]{:S(2)}, u32[]{:S(2)}) collective-permute-start(bf16[64,16,256]{2,1,0:T(8,128)(2,1)S(1)} %get-tuple-element.43), channel_id=1, source_target_pairs={{0,32},{32,64},{64,96},{96,0},{1,33},{33,65},{65,97},{97,1},{2,34}... | collective-permute-start | bytes 1572872 | tf_op jit(solution)/shard_map/ppermute | solution.py:354
  74.3 23.5 %collective-permute-start.9 = (bf16[64,16,256]{2,1,0:T(8,128)(2,1)S(1)}, bf16[64,16,256]{2,1,0:T(8,128)(2,1)S(1)}, u32[]{:S(2)}, u32[]{:S(2)}) collective-permute-start(bf16[64,16,256]{2,1,0:T(8,128)(2,1)S(1)} %get-tuple-element.44), channel_id=1, source_target_pairs={{0,96},{32,0},{64,32},{96,64},{1,97},{33,1},{65,33},{97,65},{2,98}... | collective-permute-start | bytes 1572872 | tf_op jit(solution)/shard_map/ppermute | solution.py:354
  98.1 7.7 %collective-permute-start.10 = (bf16[4,4,16,256]{3,2,1,0:T(8,128)(2,1)S(1)}, bf16[4,4,16,256]{3,2,1,0:T(8,128)(2,1)S(1)}, u32[]{:S(2)}, u32[]{:S(2)}) collective-permute-start(bf16[4,4,16,256]{3,2,1,0:T(8,128)(2,1)S(1)} %get-tuple-element.46), channel_id=1, source_target_pairs={{0,2},{1,3},{2,0},{3,1},{4,6},{5,7},{6,4},{7,5},{8,10},{9,11},{10,... | collective-permute-start | bytes 393224 | tf_op jit(solution)/shard_map/ppermute | solution.py:354
  101.3 6.7 %collective-permute-start.11 = (bf16[4,4,16,256]{3,2,1,0:T(8,128)(2,1)S(1)}, bf16[4,4,16,256]{3,2,1,0:T(8,128)(2,1)S(1)}, u32[]{:S(2)}, u32[]{:S(2)}) collective-permute-start(bf16[4,4,16,256]{3,2,1,0:T(8,128)(2,1)S(1)} %get-tuple-element.47), channel_id=1, source_target_pairs={{0,1},{1,2},{2,3},{3,0},{4,5},{5,6},{6,7},{7,4},{8,9},{9,10},{10,1... | collective-permute-start | bytes 393224 | tf_op jit(solution)/shard_map/ppermute | solution.py:354
  101.9 6.1 %collective-permute-start.12 = (bf16[4,4,16,256]{3,2,1,0:T(8,128)(2,1)S(1)}, bf16[4,4,16,256]{3,2,1,0:T(8,128)(2,1)S(1)}, u32[]{:S(2)}, u32[]{:S(2)}) collective-permute-start(bf16[4,4,16,256]{3,2,1,0:T(8,128)(2,1)S(1)} %get-tuple-element.48), channel_id=1, source_target_pairs={{0,3},{1,0},{2,1},{3,2},{4,7},{5,4},{6,5},{7,6},{8,11},{9,8},{10,9... | collective-permute-start | bytes 393224 | tf_op jit(solution)/shard_map/ppermute | solution.py:354
  108.1 6.5 %collective-permute-start.13 = (f32[4,16,256]{2,1,0:T(8,128)S(1)}, f32[4,16,256]{2,1,0:T(8,128)S(1)}, u32[]{:S(2)}, u32[]{:S(2)}) collective-permute-start(f32[4,16,256]{2,1,0:T(8,128)S(1)} %get-tuple-element.50), channel_id=1, source_target_pairs={{0,8},{4,12},{8,0},{12,4},{1,9},{5,13},{9,1},{13,5},{2,10},{6,14},... | collective-permute-start | bytes 196616 | tf_op jit(solution)/shard_map/ppermute | solution.py:354
  111.3 5.5 %collective-permute-start.14 = (f32[4,16,256]{2,1,0:T(8,128)S(1)}, f32[4,16,256]{2,1,0:T(8,128)S(1)}, u32[]{:S(2)}, u32[]{:S(2)}) collective-permute-start(f32[4,16,256]{2,1,0:T(8,128)S(1)} %get-tuple-element.51), channel_id=1, source_target_pairs={{0,4},{4,8},{8,12},{12,0},{1,5},{5,9},{9,13},{13,1},{2,6},{6,10},{... | collective-permute-start | bytes 196616 | tf_op jit(solution)/shard_map/ppermute | solution.py:354
  111.9 4.9 %collective-permute-start.15 = (f32[4,16,256]{2,1,0:T(8,128)S(1)}, f32[4,16,256]{2,1,0:T(8,128)S(1)}, u32[]{:S(2)}, u32[]{:S(2)}) collective-permute-start(f32[4,16,256]{2,1,0:T(8,128)S(1)} %get-tuple-element.52), channel_id=1, source_target_pairs={{0,12},{4,0},{8,4},{12,8},{1,13},{5,1},{9,5},{13,9},{2,14},{6,2},{... | collective-permute-start | bytes 196616 | tf_op jit(solution)/shard_map/ppermute | solution.py:354
